TPU v7x, 32 devices: a whole 2x2x4 slice. The times are simulated.
32 devices in a mesh: tx: 8 (over y, x, core), ty: 4 (over z).
Axes of the slice: x: 2, y: 2, z: 4, core: 2. Of those that a mesh axis runs over, the one named last changes fastest.
Arguments:
- object_slab: float32 [2, 2, 2048, 4096], P(None, None, 'tx', 'ty'), may hold values from -5 to 5
- probe: float32 [2, 256, 256], replicated, may hold values from -6 to 6
- patterns: float32 [256, 256, 256], P(('tx', 'ty')), may hold values from 0 to 4
- centers: int32 [256, 2], P(('tx', 'ty')), may hold values from 128 to 3968, as said below
- counts: int32 [32], replicated, may hold values from 0 to 8, as said below
Outputs:
- object_gradient: float32 [2, 2, 2048, 4096], P(None, None, 'tx', 'ty')
- probe_gradient: float32 [2, 256, 256], replicated
Inputs may be any that keep to these rules, and one draw needn't show every extreme that they name: Slot block d = i * (devices along ty) + j belongs to the device at tx-index i and ty-index j; each of its centers lies in that device's tile, rows i * 256 to (i + 1) * 256 - 1 and columns j * 1024 to (j + 1) * 1024 - 1, and the window of side 256 around it lies inside the object. Entry i * (devices along ty) + j is the number of used slots, always the first ones, of the device at tx-index i and ty-index j. The counts of two devices with the same ty-index whose tx-indices differ by half the tx axis add up to at most 8; some device has 8.
All inputs are finite; a program needn't handle non-finite values.
Results may differ from a plain program's by a relative error of at most 0.0003.
Values sent between devices are 32-bit elements; how exact they have to be, the bound alone decides.
No kernel may reach another device: no remote copies, remote signals or barrier semaphores. Data moves between devices by JAX's collectives and lax.ppermute only.
A program may use at most 128 MiB of HBM per device.

v0:
```python
import math

import jax
import jax.numpy as jnp
import ml_dtypes
import numpy as np
from jax import lax
from jax.experimental import pallas as pl
from jax.experimental.pallas import tpu as pltpu
from jax.sharding import PartitionSpec as P

KAPPA = 40.0
F32 = jnp.float32
FWD, INV, PROP, ADJ = 0, 1, 2, 3
LEFT = {FWD: (0, 2), INV: (1, 3), PROP: (4, 6), ADJ: (5, 7)}
RIGHT = {FWD: (1, 3), INV: (0, 2), PROP: (5, 7), ADJ: (4, 6)}


def tables(width):
    half = width // 2
    n = np.arange(half)
    freq = ((np.arange(width) + half) % width - half) / width
    factor = np.exp(-1j * math.pi * KAPPA * freq * freq)
    turn = 2j * np.pi / width
    scale = 1.0 / math.sqrt(width)
    even = np.exp(-turn * ((2 * n[:, None] * n[None, :]) % width)) * scale
    odd = np.exp(-turn * (((2 * n[:, None] + 1) * n[None, :]) % width)) * scale

    def combined(freqs):
        apart = n[:, None] - n[None, :]
        total = np.zeros((half, half), complex)
        for k in freqs:
            total += factor[k] * np.exp(turn * ((k * apart) % width))
        return total / width

    lefts, rights = [], []
    for c in (even, odd, combined(range(0, width, 2)), combined(range(1, width, 2))):
        real = np.block([[c.real, -c.imag], [c.imag, c.real]])
        for m in (real, real.T):
            hi = m.astype(ml_dtypes.bfloat16)
            lo = (m - hi.astype(np.float64)).astype(ml_dtypes.bfloat16)
            lefts.append(np.concatenate([hi, hi, lo], axis=1))
            rights.append(np.concatenate([hi, hi, lo], axis=0))
    return jnp.asarray(np.stack(lefts)), jnp.asarray(np.stack(rights))


def split(x):
    hi = x.astype(jnp.bfloat16)
    return hi, (x - hi.astype(F32)).astype(jnp.bfloat16)


def pair(x, y, axis):
    return jnp.concatenate([x, y], axis=axis)


def one_side(re, im, kind, axis, table):
    half = re.shape[axis] // 2

    def halves(x):
        return (x[:half], x[half:]) if axis == 0 else (x[:, :half], x[:, half:])

    a, b = halves(re)
    c, d = halves(im)
    if kind != INV:
        a, b, c, d = a + b, a - b, c + d, c - d

    def product(x, index):
        hi, lo = split(x)
        stacked = jnp.concatenate([hi, lo, hi], axis=axis)
        if axis == 0:
            return jnp.dot(table[index], stacked, preferred_element_type=F32)
        return jnp.dot(stacked, table[index], preferred_element_type=F32)

    even, odd = (LEFT if axis == 0 else RIGHT)[kind]
    a, c = halves(product(pair(a, c, axis), even))
    b, d = halves(product(pair(b, d, axis), odd))
    if kind == FWD:
        return pair(a, b, axis), pair(c, d, axis)
    return pair(a + b, a - b, axis), pair(c + d, c - d, axis)


def transform(re, im, kind, lefts, rights):
    re, im = one_side(re, im, kind, 1, rights)
    return one_side(re, im, kind, 0, lefts)


def times(a, b, c, d):
    return a * c - b * d, a * d + b * c


def conj_times(a, b, c, d):
    return a * c + b * d, a * d - b * c


def blocks_of(cols, width, rim):
    pieces = []
    at = 0
    while at < cols:
        block, inside = divmod(at + rim, width)
        count = min(width - inside, cols - at)
        pieces.append((at, count, block, inside))
        at += count
    return pieces


def kernel_body(
    rows, cols, bounds, mid, top, bottom, left, left_ends, right, right_ends, patterns, probe, lefts, rights,
    g_mid, g_top, g_bottom, g_left, g_right, g_probe, obj, acc, sem,
):
    width = probe.shape[-1]
    rim = width // 2
    tile_rows, tile_cols = mid.shape[2], mid.shape[3]
    last = obj.shape[0] - 1
    bands = ((rim, tile_rows), (0, rim), (rim + tile_rows, rim))

    copies = []
    for source, (row, count) in zip((mid, top, bottom), bands):
        for at, span, block, inside in blocks_of(tile_cols, width, rim):
            copies.append((source.at[:, :, :, at : at + span], obj.at[block, :, :, row : row + count, inside : inside + span]))
    for own, ends, block, inside in ((left, left_ends, 0, 0), (right, right_ends, last, rim)):
        lanes = slice(inside, inside + rim)
        copies.append((own, obj.at[block, :, :, rim : rim + tile_rows, lanes]))
        copies.append((ends.at[:, :, :rim], obj.at[block, :, :, :rim, lanes]))
        copies.append((ends.at[:, :, rim:], obj.at[block, :, :, rim + tile_rows :, lanes]))
    copies = [pltpu.make_async_copy(a, b, sem.at[i]) for i, (a, b) in enumerate(copies)]
    for copy in copies:
        copy.start()
    acc[...] = jnp.zeros_like(acc)
    g_probe[...] = jnp.zeros_like(g_probe)
    for copy in copies:
        copy.wait()

    row_index = lax.broadcasted_iota(jnp.int32, (width, width), 0)
    col_index = lax.broadcasted_iota(jnp.int32, (width, width), 1)

    def visit(slot, _):
        row, col = rows[slot], cols[slot]
        block = col // width
        shift = col % width
        below = row_index < row
        beside = col_index < shift

        def cut(level, part):
            upper = jnp.where(beside, obj[block + 1, level, part, :width], obj[block, level, part, :width])
            lower = jnp.where(beside, obj[block + 1, level, part, width:], obj[block, level, part, width:])
            return jnp.where(below, lower, upper)

        def deposit(level, part, term):
            zero = jnp.zeros_like(term)
            upper = jnp.where(below, zero, term)
            lower = jnp.where(below, term, zero)
            acc[block, level, part, :width] += jnp.where(beside, zero, upper)
            acc[block, level, part, width:] += jnp.where(beside, zero, lower)
            acc[block + 1, level, part, :width] += jnp.where(beside, upper, zero)
            acc[block + 1, level, part, width:] += jnp.where(beside, lower, zero)

        def rolled(x, down, along):
            return pltpu.roll(pltpu.roll(x, down, 0), along, 1)

        u0 = rolled(probe[0], row, shift), rolled(probe[1], row, shift)
        o0 = cut(0, 0), cut(0, 1)
        u1 = transform(*times(*u0, *o0), PROP, lefts, rights)
        o1 = cut(1, 0), cut(1, 1)
        far_re, far_im = transform(*times(*u1, *o1), FWD, lefts, rights)
        factor = 1.0 - patterns[slot] * lax.rsqrt(far_re * far_re + far_im * far_im + 1.0)
        chi = transform(far_re * factor, far_im * factor, INV, lefts, rights)
        for part, term in enumerate(conj_times(*u1, *chi)):
            deposit(1, part, term)
        chi = transform(*conj_times(*o1, *chi), ADJ, lefts, rights)
        for part, term in enumerate(conj_times(*u0, *chi)):
            deposit(0, part, term)
        up, back = (width - row) % width, (width - shift) % width
        for part, term in enumerate(conj_times(*o0, *chi)):
            g_probe[part] += rolled(term, up, back)
        return 0

    lax.fori_loop(bounds[0], bounds[1], visit, 0)

    copies = []
    for target, (row, count) in zip((g_mid, g_top, g_bottom), bands):
        for at, span, block, inside in blocks_of(tile_cols, width, rim):
            copies.append((acc.at[block, :, :, row : row + count, inside : inside + span], target.at[:, :, :, at : at + span]))
    copies.append((acc.at[0, :, :, :, :rim], g_left))
    copies.append((acc.at[last, :, :, :, rim:], g_right))
    copies = [pltpu.make_async_copy(a, b, sem.at[i]) for i, (a, b) in enumerate(copies)]
    for copy in copies:
        copy.start()
    for copy in copies:
        copy.wait()


def slot_gradients(rows, cols, bounds, mid, top, bottom, left, left_ends, right, right_ends, patterns, probe):
    width = probe.shape[-1]
    rim = width // 2
    slices, _, tile_rows, tile_cols = mid.shape
    blocks = (tile_cols + 2 * rim) // width
    smem = pl.BlockSpec(memory_space=pltpu.SMEM)
    vmem = pl.BlockSpec(memory_space=pltpu.VMEM)
    hbm = pl.BlockSpec(memory_space=pl.ANY)
    lefts, rights = tables(width)
    padded = (blocks, slices, 2, tile_rows + 2 * rim, width)
    row_part = jax.ShapeDtypeStruct(top.shape, F32)
    col_part = jax.ShapeDtypeStruct((slices, 2, tile_rows + 2 * rim, rim), F32)
    return pl.pallas_call(
        kernel_body,
        out_shape=(
            jax.ShapeDtypeStruct(mid.shape, F32), row_part, row_part, col_part, col_part,
            jax.ShapeDtypeStruct(probe.shape, F32),
        ),
        in_specs=[smem] * 3 + [hbm] * 7 + [vmem] * 4,
        out_specs=(hbm,) * 5 + (vmem,),
        scratch_shapes=[
            pltpu.VMEM(padded, F32),
            pltpu.VMEM(padded, F32),
            pltpu.SemaphoreType.DMA((3 * blocks + 6,)),
        ],
        compiler_params=pltpu.CompilerParams(vmem_limit_bytes=48 * 2**20),
        cost_estimate=pl.CostEstimate(flops=10**10, bytes_accessed=2 * 10**7, transcendentals=0),
    )(rows, cols, bounds, mid, top, bottom, left, left_ends, right, right_ends, patterns, probe, lefts, rights)


def send(x, axis, step):
    count = lax.axis_size(axis)
    return lax.ppermute(x, axis, [(i, i + step) for i in range(count) if 0 <= i + step < count])


def sum_everywhere(x, axes):
    flat = x.reshape(-1, x.shape[-1])
    done = []
    for axis in axes:
        count = lax.axis_size(axis)
        apart = 1
        while apart < count:
            bit = (lax.axis_index(axis) // apart) % 2
            half = flat.shape[0] // 2
            pairs = [(i, i ^ apart) for i in range(count)]
            mine = lax.dynamic_slice_in_dim(flat, bit * half, half, 0)
            other = lax.dynamic_slice_in_dim(flat, (1 - bit) * half, half, 0)
            flat = mine + lax.ppermute(other, axis, pairs)
            done.append((axis, pairs, bit))
            apart *= 2
    for axis, pairs, bit in reversed(done):
        other = lax.ppermute(flat, axis, pairs)
        low = jnp.where(bit == 0, flat, other)
        high = jnp.where(bit == 0, other, flat)
        flat = jnp.concatenate([low, high], axis=0)
    return flat.reshape(x.shape)


def per_device(object_slab, probe, patterns, centers, counts):
    tile_rows, tile_cols = object_slab.shape[2:]
    width = probe.shape[-1]
    rim = width // 2
    row_index = lax.axis_index("tx")
    col_index = lax.axis_index("ty")
    my_count = counts[row_index * lax.axis_size("ty") + col_index]
    bounds = jnp.stack([jnp.zeros((), jnp.int32), my_count])
    rows = centers[:, 0] - row_index * tile_rows
    cols = centers[:, 1] - col_index * tile_cols
    slots = patterns.shape[0]
    amplitudes = jnp.sqrt(patterns).reshape(slots, rim, 2, rim, 2).transpose(0, 2, 1, 4, 3).reshape(patterns.shape)

    top = send(object_slab[:, :, tile_rows - rim :], "tx", 1)
    bottom = send(object_slab[:, :, :rim], "tx", -1)
    left = send(object_slab[:, :, :, tile_cols - rim :], "ty", 1)
    right = send(object_slab[:, :, :, :rim], "ty", -1)
    ends = jnp.concatenate([top, bottom], axis=2)
    left_ends = send(ends[:, :, :, tile_cols - rim :], "ty", 1)
    right_ends = send(ends[:, :, :, :rim], "ty", -1)

    g_mid, g_top, g_bottom, g_left, g_right, g_probe = slot_gradients(
        rows, cols, bounds, object_slab, top, bottom, left, left_ends, right, right_ends, amplitudes, probe
    )

    from_left = send(g_right, "ty", 1)
    from_right = send(g_left, "ty", -1)

    def edges(x, first, last):
        x = x.at[:, :, :, :rim].add(from_left[:, :, first:last])
        return x.at[:, :, :, tile_cols - rim :].add(from_right[:, :, first:last])

    from_below = send(edges(g_top, 0, rim), "tx", -1)
    from_above = send(edges(g_bottom, tile_rows + rim, tile_rows + 2 * rim), "tx", 1)
    inner = edges(g_mid, rim, tile_rows + rim)
    inner = inner.at[:, :, :rim].add(from_above)
    inner = inner.at[:, :, tile_rows - rim :].add(from_below)
    probe_sum = sum_everywhere(g_probe, ("tx", "ty"))
    positions = jnp.maximum(jnp.sum(counts), 1).astype(F32)
    return (inner, probe_sum / jnp.sqrt(positions))


def solution(mesh):
    placed = (
        P(None, None, "tx", "ty"),
        P(),
        P(("tx", "ty"), None, None),
        P(("tx", "ty"), None),
        P(),
    )
    return jax.shard_map(
        per_device,
        mesh=mesh,
        in_specs=placed,
        out_specs=(P(None, None, "tx", "ty"), P()),
        check_vma=False,
    )
```

profile of v0, /device:TPU:1, one launch (start us, length us, event | category | flops | bytes accessed | tf_op | source)
XLA Modules:
  0.0 301.8 jit_solution(14922996482875595588)
XLA Ops:
  0.6 2.5 fusion.10
  3.2 4.5 %collective-permute-start = (f32[2,2,128,1024]{3,2,1,0:T(8,128)S(1)}, f32[2,2,128,1024]{3,2,1,0:T(8,128)S(1)}, u32[]{:S(2)}, u32[]{:S(2)}) collective-permute-start(f32[2,2,128,1024]{3,2,1,0:T(8,128)S(1)} %get-tuple-element.115), channel_id=1, source_target_pairs={{0,4},{4,8},{8,12},{12,16},{16,20},{20,24},{24,28},{1,5},{5,9},{9,... | collective-permute-start | bytes 6291464 | tf_op jit(solution)/shard_map/ppermute | solution.py:224
  7.7 1.9 collective-permute-start.1
  9.6 2.1 fusion.9
  11.7 3.2 %collective-permute-start.2 = (f32[2,2,256,128]{3,2,1,0:T(8,128)}, f32[2,2,256,128]{3,2,1,0:T(8,128)S(1)}, u32[]{:S(2)}, u32[]{:S(2)}) collective-permute-start(f32[2,2,256,128]{3,2,1,0:T(8,128)} %get-tuple-element.113), channel_id=1, source_target_pairs={{0,1},{1,2},{2,3},{4,5},{5,6},{6,7},{8,9},{9,10},{10,11},{12,13},{... | collective-permute-start | bytes 1572872 | tf_op jit(solution)/shard_map/ppermute | solution.py:224
  14.9 1.3 collective-permute-start.4
  16.2 14.4 %collective-permute-done.top = f32[2,2,128,1024]{3,2,1,0:T(8,128)S(1)} collective-permute-done((f32[2,2,128,1024]{3,2,1,0:T(8,128)S(1)}, f32[2,2,128,1024]{3,2,1,0:T(8,128)S(1)}, u32[]{:S(2)}, u32[]{:S(2)}) %collective-permute-start) | collective-permute-done | bytes 2097184 | tf_op jit(solution)/shard_map/ppermute | solution.py:224
  30.9 23.9 %collective-permute-done.1.bottom = f32[2,2,128,1024]{3,2,1,0:T(8,128)S(1)} collective-permute-done((f32[2,2,128,1024]{3,2,1,0:T(8,128)S(1)}, f32[2,2,128,1024]{3,2,1,0:T(8,128)S(1)}, u32[]{:S(2)}, u32[]{:S(2)}) %collective-permute-start.1) | collective-permute-done | bytes 2097184 | tf_op jit(solution)/shard_map/ppermute | solution.py:224
  55.0 1.3 fusion.8
  56.4 3.2 %collective-permute-start.3 = (f32[2,2,256,128]{3,2,1,0:T(8,128)}, f32[2,2,256,128]{3,2,1,0:T(8,128)S(1)}, u32[]{:S(2)}, u32[]{:S(2)}) collective-permute-start(f32[2,2,256,128]{3,2,1,0:T(8,128)} %get-tuple-element.111), channel_id=1, source_target_pairs={{0,1},{1,2},{2,3},{4,5},{5,6},{6,7},{8,9},{9,10},{10,11},{12,13},{... | collective-permute-start | bytes 1572872 | tf_op jit(solution)/shard_map/ppermute | solution.py:224
  59.6 1.3 collective-permute-start.5
  60.9 3.4 %sqrt.6 = f32[8,256,256]{2,1,0:T(8,128)} sqrt(f32[8,256,256]{2,1,0:T(8,128)} %param.25) | non-fusion elementwise | bytes 4194304 | tf_op jit(solution)/shard_map/sqrt | solution.py:261
  64.3 17.7 %copy.10 = f32[8,256,256]{0,2,1:T(8,128)} copy(f32[8,256,256]{2,1,0:T(8,128)} %sqrt.6) | data formatting | bytes 4194304 | tf_op jit(solution)/shard_map/sqrt | solution.py:261
  82.0 36.3 %copy.11 = f32[8,2,128,2,128]{4,3,2,1,0:T(2,128)} copy(f32[8,2,128,2,128]{0,3,4,1,2:T(2,128)} %bitcast.11) | data formatting | bytes 4194304 | tf_op jit(solution)/shard_map/transpose | solution.py:261
  118.2 4.0 %reshape.290.patterns = f32[8,256,256]{2,1,0:T(8,128)} reshape(f32[8,2,128,2,128]{4,3,2,1,0:T(2,128)} %copy.11) | data formatting | bytes 4194304 | tf_op jit(solution)/shard_map/reshape | solution.py:261
  126.7 1.0 copy-done.2
  127.8 1.0 copy-done.4
  128.8 1.0 copy-done.6
  129.8 1.0 copy-done.8
  130.9 10.4 %shard_map.86 = (f32[2,2,256,1024]{3,2,1,0:T(8,128)}, f32[2,2,128,1024]{3,2,1,0:T(8,128)}, f32[2,2,128,1024]{3,2,1,0:T(8,128)}, f32[2,2,512,128]{3,2,1,0:T(8,128...) custom-call(s32[8]{0:T(128)S(1)} %get-tuple-element.131.rows, s32[8]{0:T(128)S(1)} %get-tuple-element.130.cols, ...), custom_call_target="tpu_custom_call" | custom-call | flops 10000000000 | bytes 20000000 | tf_op jit(solution)/shard_map/pallas_call | solution.py:204
  141.5 1.5 collective-permute-done.10
  143.0 5.6 %collective-permute-start.11 = (f32[128,256]{1,0:T(8,128)S(1)}, f32[128,256]{1,0:T(8,128)S(1)}, u32[]{:S(2)}, u32[]{:S(2)}) collective-permute-start(f32[128,256]{1,0:T(8,128)S(1)} %constant_dynamic-slice_fusion.3), channel_id=1, source_target_pairs={{0,8},{4,12},{8,0},{12,4},{16,24},{20,28},{24,16},{28,20},{1,9},{5... | collective-permute-start | bytes 393224 | tf_op jit(solution)/shard_map/ppermute | solution.py:239
  148.6 3.7 %collective-permute-done.11 = f32[128,256]{1,0:T(8,128)S(1)} collective-permute-done((f32[128,256]{1,0:T(8,128)S(1)}, f32[128,256]{1,0:T(8,128)S(1)}, u32[]{:S(2)}, u32[]{:S(2)}) %collective-permute-start.11) | collective-permute-done | bytes 131104 | tf_op jit(solution)/shard_map/ppermute | solution.py:239
  152.4 10.7 %collective-permute-start.12 = (f32[64,256]{1,0:T(8,128)S(1)}, f32[64,256]{1,0:T(8,128)S(1)}, u32[]{:S(2)}, u32[]{:S(2)}) collective-permute-start(f32[64,256]{1,0:T(8,128)S(1)} %constant_dynamic-slice_fusion.2), channel_id=1, source_target_pairs={{0,16},{4,20},{8,24},{12,28},{16,0},{20,4},{24,8},{28,12},{1,17},{... | collective-permute-start | bytes 196616 | tf_op jit(solution)/shard_map/ppermute | solution.py:239
  163.1 1.7 collective-permute-done.12
  164.8 21.8 %collective-permute-start.13 = (f32[32,256]{1,0:T(8,128)S(1)}, f32[32,256]{1,0:T(8,128)S(1)}, u32[]{:S(2)}, u32[]{:S(2)}) collective-permute-start(f32[32,256]{1,0:T(8,128)S(1)} %constant_dynamic-slice_fusion.1), channel_id=1, source_target_pairs={{0,1},{1,0},{2,3},{3,2},{4,5},{5,4},{6,7},{7,6},{8,9},{9,8},{10,11... | collective-permute-start | bytes 98312 | tf_op jit(solution)/shard_map/ppermute | solution.py:239
  186.6 2.0 collective-permute-start.6
  188.7 2.3 collective-permute-start.14
  191.0 1.3 collective-permute-start.7
  192.3 17.7 %collective-permute-done.14 = f32[16,256]{1,0:T(8,128)S(1)} collective-permute-done((f32[16,256]{1,0:T(8,128)S(1)}, f32[16,256]{1,0:T(8,128)S(1)}, u32[]{:S(2)}, u32[]{:S(2)}) %collective-permute-start.14) | collective-permute-done | bytes 16416 | tf_op jit(solution)/shard_map/ppermute | solution.py:239
  210.0 2.8 collective-permute-start.15
  212.9 1.8 collective-permute-done.15
  214.7 1.3 collective-permute-start.16
  216.0 2.3 collective-permute-done.16
  218.4 1.9 fusion.5
  220.3 2.1 fusion.4
  222.4 8.2 %collective-permute-start.8 = (f32[2,2,128,1024]{3,2,1,0:T(8,128)}, f32[2,2,128,1024]{3,2,1,0:T(8,128)S(1)}, u32[]{:S(2)}, u32[]{:S(2)}) collective-permute-start(f32[2,2,128,1024]{3,2,1,0:T(8,128)} %get-tuple-element.117), channel_id=1, source_target_pairs={{0,4},{4,8},{8,12},{12,16},{16,20},{20,24},{24,28},{1,5},{5,9},{9,... | collective-permute-start | bytes 6291464 | tf_op jit(solution)/shard_map/ppermute | solution.py:224
  230.7 24.1 %collective-permute-done.17 = f32[64,256]{1,0:T(8,128)S(1)} collective-permute-done((f32[64,256]{1,0:T(8,128)S(1)}, f32[64,256]{1,0:T(8,128)S(1)}, u32[]{:S(2)}, u32[]{:S(2)}) %collective-permute-start.17) | collective-permute-done | bytes 65568 | tf_op jit(solution)/shard_map/ppermute | solution.py:243
  254.8 1.9 collective-permute-start.9
  256.9 4.7 %collective-permute-done.18 = f32[128,256]{1,0:T(8,128)} collective-permute-done((f32[128,256]{1,0:T(8,128)S(1)}, f32[128,256]{1,0:T(8,128)}, u32[]{:S(2)}, u32[]{:S(2)}) %collective-permute-start.18) | collective-permute-done | bytes 131104 | tf_op jit(solution)/shard_map/ppermute | solution.py:243
  261.5 0.9 broadcast_select_fusion.3
  263.2 23.8 %collective-permute-start.19 = (f32[256,256]{1,0:T(8,128)}, f32[256,256]{1,0:T(8,128)}, u32[]{:S(2)}, u32[]{:S(2)}) collective-permute-start(f32[256,256]{1,0:T(8,128)} %pad_maximum_fusion), channel_id=1, source_target_pairs={{0,4},{4,0},{8,12},{12,8},{16,20},{20,16},{24,28},{28,24},{1,5},{5... | collective-permute-start | bytes 786440 | tf_op jit(solution)/shard_map/ppermute | solution.py:243
  288.5 1.0 broadcast_select_fusion.1
  289.5 0.8 maximum_divide_fusion
  290.3 1.9 fusion.3
  292.2 2.1 fusion.2
  294.3 3.5 %fusion.1 = f32[2,2,256,1024]{3,2,1,0:T(8,128)} fusion(f32[2,2,256,1024]{3,2,1,0:T(8,128)} %fusion.2, f32[2,2,128,1024]{3,2,1,0:T(8,128)S(1)} %collective-permute-done.8), kind=kLoop, calls=%fused_computation.3 | loop fusion | flops 524288 | bytes 6291456 | tf_op jit(solution)/shard_map/scatter-add | solution.py:285
  297.7 4.1 %fusion = f32[2,2,256,1024]{3,2,1,0:T(8,128)} fusion(f32[2,2,256,1024]{3,2,1,0:T(8,128)} %fusion.1, f32[2,2,128,1024]{3,2,1,0:T(8,128)} %collective-permute-done.9), kind=kLoop, calls=%fused_computation.1 | loop fusion | flops 524288 | bytes 6291456 | tf_op jit(solution)/shard_map/scatter-add | solution.py:286
  (58 shorter events, 7.0 us)
Async XLA Ops:
  3.2 27.5 %collective-permute-start = (f32[2,2,128,1024]{3,2,1,0:T(8,128)S(1)}, f32[2,2,128,1024]{3,2,1,0:T(8,128)S(1)}, u32[]{:S(2)}, u32[]{:S(2)}) collective-permute-start(f32[2,2,128,1024]{3,2,1,0:T(8,128)S(1)} %get-tuple-element.115), channel_id=1, source_target_pairs={{0,4},{4,8},{8,12},{12,16},{16,20},{20,24},{24,28},{1,5},{5,9},{9,... | collective-permute-start | bytes 6291464 | tf_op jit(solution)/shard_map/ppermute | solution.py:224
  7.7 47.1 %collective-permute-start.1 = (f32[2,2,128,1024]{3,2,1,0:T(8,128)S(1)}, f32[2,2,128,1024]{3,2,1,0:T(8,128)S(1)}, u32[]{:S(2)}, u32[]{:S(2)}) collective-permute-start(f32[2,2,128,1024]{3,2,1,0:T(8,128)S(1)} %get-tuple-element.114), channel_id=1, source_target_pairs={{4,0},{8,4},{12,8},{16,12},{20,16},{24,20},{28,24},{5,1},{9,5},{13... | collective-permute-start | bytes 6291464 | tf_op jit(solution)/shard_map/ppermute | solution.py:224
  11.7 111.8 %collective-permute-start.2 = (f32[2,2,256,128]{3,2,1,0:T(8,128)}, f32[2,2,256,128]{3,2,1,0:T(8,128)S(1)}, u32[]{:S(2)}, u32[]{:S(2)}) collective-permute-start(f32[2,2,256,128]{3,2,1,0:T(8,128)} %get-tuple-element.113), channel_id=1, source_target_pairs={{0,1},{1,2},{2,3},{4,5},{5,6},{6,7},{8,9},{9,10},{10,11},{12,13},{... | collective-permute-start | bytes 1572872 | tf_op jit(solution)/shard_map/ppermute | solution.py:224
  14.9 109.4 %collective-permute-start.4 = (f32[2,2,256,128]{3,2,1,0:T(8,128)S(1)}, f32[2,2,256,128]{3,2,1,0:T(8,128)S(1)}, u32[]{:S(2)}, u32[]{:S(2)}) collective-permute-start(f32[2,2,256,128]{3,2,1,0:T(8,128)S(1)} %get-tuple-element.112), channel_id=1, source_target_pairs={{1,0},{2,1},{3,2},{5,4},{6,5},{7,6},{9,8},{10,9},{11,10},{13,12},{... | collective-permute-start | bytes 1572872 | tf_op jit(solution)/shard_map/ppermute | solution.py:224
  30.6 24.4 %copy-start.9 = (f32[2,2,128,1024]{3,2,1,0:T(8,128)}, f32[2,2,128,1024]{3,2,1,0:T(8,128)S(1)}, u32[]{:S(2)}) copy-start(f32[2,2,128,1024]{3,2,1,0:T(8,128)S(1)} %collective-permute-done.top) | copy-start | bytes 6291460
  54.8 1.6 copy-start.10
  56.4 68.7 %collective-permute-start.3 = (f32[2,2,256,128]{3,2,1,0:T(8,128)}, f32[2,2,256,128]{3,2,1,0:T(8,128)S(1)}, u32[]{:S(2)}, u32[]{:S(2)}) collective-permute-start(f32[2,2,256,128]{3,2,1,0:T(8,128)} %get-tuple-element.111), channel_id=1, source_target_pairs={{0,1},{1,2},{2,3},{4,5},{5,6},{6,7},{8,9},{9,10},{10,11},{12,13},{... | collective-permute-start | bytes 1572872 | tf_op jit(solution)/shard_map/ppermute | solution.py:224
  59.6 66.3 %collective-permute-start.5 = (f32[2,2,256,128]{3,2,1,0:T(8,128)}, f32[2,2,256,128]{3,2,1,0:T(8,128)S(1)}, u32[]{:S(2)}, u32[]{:S(2)}) collective-permute-start(f32[2,2,256,128]{3,2,1,0:T(8,128)} %get-tuple-element.110), channel_id=1, source_target_pairs={{1,0},{2,1},{3,2},{5,4},{6,5},{7,6},{9,8},{10,9},{11,10},{13,12},{... | collective-permute-start | bytes 1572872 | tf_op jit(solution)/shard_map/ppermute | solution.py:224
  118.2 4.0 %copy-start.12 = (s32[32]{0:T(128)S(1)}, s32[32]{0:T(128)}, u32[]{:S(2)}) copy-start(s32[32]{0:T(128)} %param.27) | copy-start | bytes 388
  118.2 5.3 %copy-start.11 = (s32[8,2]{0,1:T(2,128)S(1)}, s32[8,2]{0,1:T(2,128)}, u32[]{:S(2)}) copy-start(s32[8,2]{0,1:T(2,128)} %param.26) | copy-start | bytes 196
  118.2 8.5 %copy-start = (f32[2,256,256]{2,1,0:T(8,128)S(1)}, f32[2,256,256]{2,1,0:T(8,128)}, u32[]{:S(2)}) copy-start(f32[2,256,256]{2,1,0:T(8,128)} %probe.1) | copy-start | bytes 1572868
  123.5 0.8 copy-start.1
  124.3 0.8 copy-start.3
  125.1 0.8 copy-start.5
  125.9 0.8 copy-start.7
  126.7 1.0 copy-start.2
  127.8 1.0 copy-start.4
  128.8 1.0 copy-start.6
  129.8 1.0 copy-start.8
  141.3 1.6 collective-permute-start.10
  143.0 9.3 %collective-permute-start.11 = (f32[128,256]{1,0:T(8,128)S(1)}, f32[128,256]{1,0:T(8,128)S(1)}, u32[]{:S(2)}, u32[]{:S(2)}) collective-permute-start(f32[128,256]{1,0:T(8,128)S(1)} %constant_dynamic-slice_fusion.3), channel_id=1, source_target_pairs={{0,8},{4,12},{8,0},{12,4},{16,24},{20,28},{24,16},{28,20},{1,9},{5... | collective-permute-start | bytes 393224 | tf_op jit(solution)/shard_map/ppermute | solution.py:239
  152.4 12.4 %collective-permute-start.12 = (f32[64,256]{1,0:T(8,128)S(1)}, f32[64,256]{1,0:T(8,128)S(1)}, u32[]{:S(2)}, u32[]{:S(2)}) collective-permute-start(f32[64,256]{1,0:T(8,128)S(1)} %constant_dynamic-slice_fusion.2), channel_id=1, source_target_pairs={{0,16},{4,20},{8,24},{12,28},{16,0},{20,4},{24,8},{28,12},{1,17},{... | collective-permute-start | bytes 196616 | tf_op jit(solution)/shard_map/ppermute | solution.py:239
  164.8 23.8 %collective-permute-start.13 = (f32[32,256]{1,0:T(8,128)S(1)}, f32[32,256]{1,0:T(8,128)S(1)}, u32[]{:S(2)}, u32[]{:S(2)}) collective-permute-start(f32[32,256]{1,0:T(8,128)S(1)} %constant_dynamic-slice_fusion.1), channel_id=1, source_target_pairs={{0,1},{1,0},{2,3},{3,2},{4,5},{5,4},{6,7},{7,6},{8,9},{9,8},{10,11... | collective-permute-start | bytes 98312 | tf_op jit(solution)/shard_map/ppermute | solution.py:239
  186.6 31.8 %collective-permute-start.6 = (f32[2,2,512,128]{3,2,1,0:T(8,128)S(1)}, f32[2,2,512,128]{3,2,1,0:T(8,128)S(1)}, u32[]{:S(2)}, u32[]{:S(2)}) collective-permute-start(f32[2,2,512,128]{3,2,1,0:T(8,128)S(1)} %get-tuple-element.105), channel_id=1, source_target_pairs={{0,1},{1,2},{2,3},{4,5},{5,6},{6,7},{8,9},{9,10},{10,11},{12,13},{... | collective-permute-start | bytes 3145736 | tf_op jit(solution)/shard_map/ppermute | solution.py:224
  188.7 21.3 %collective-permute-start.14 = (f32[16,256]{1,0:T(8,128)S(1)}, f32[16,256]{1,0:T(8,128)S(1)}, u32[]{:S(2)}, u32[]{:S(2)}) collective-permute-start(f32[16,256]{1,0:T(8,128)S(1)} %constant_dynamic-slice_fusion), channel_id=1, source_target_pairs={{0,2},{1,3},{2,0},{3,1},{4,6},{5,7},{6,4},{7,5},{8,10},{9,11},{10,... | collective-permute-start | bytes 49160 | tf_op jit(solution)/shard_map/ppermute | solution.py:239
  191.0 29.3 %collective-permute-start.7 = (f32[2,2,512,128]{3,2,1,0:T(8,128)S(1)}, f32[2,2,512,128]{3,2,1,0:T(8,128)}, u32[]{:S(2)}, u32[]{:S(2)}) collective-permute-start(f32[2,2,512,128]{3,2,1,0:T(8,128)S(1)} %get-tuple-element.106), channel_id=1, source_target_pairs={{1,0},{2,1},{3,2},{5,4},{6,5},{7,6},{9,8},{10,9},{11,10},{13,12},{... | collective-permute-start | bytes 3145736 | tf_op jit(solution)/shard_map/ppermute | solution.py:224
  210.0 4.7 %collective-permute-start.15 = (f32[16,256]{1,0:T(8,128)S(1)}, f32[16,256]{1,0:T(8,128)S(1)}, u32[]{:S(2)}, u32[]{:S(2)}) collective-permute-start(f32[16,256]{1,0:T(8,128)S(1)} %dynamic-slice_add_fusion.4), channel_id=1, source_target_pairs={{0,2},{1,3},{2,0},{3,1},{4,6},{5,7},{6,4},{7,5},{8,10},{9,11},{10,... | collective-permute-start | bytes 49160 | tf_op jit(solution)/shard_map/ppermute | solution.py:243
  214.7 3.6 %collective-permute-start.16 = (f32[32,256]{1,0:T(8,128)S(1)}, f32[32,256]{1,0:T(8,128)S(1)}, u32[]{:S(2)}, u32[]{:S(2)}) collective-permute-start(f32[32,256]{1,0:T(8,128)S(1)} %pad_maximum_fusion.3), channel_id=1, source_target_pairs={{0,1},{1,0},{2,3},{3,2},{4,5},{5,4},{6,7},{7,6},{8,9},{9,8},{10,11... | collective-permute-start | bytes 98312 | tf_op jit(solution)/shard_map/ppermute | solution.py:243
  222.4 71.9 %collective-permute-start.8 = (f32[2,2,128,1024]{3,2,1,0:T(8,128)}, f32[2,2,128,1024]{3,2,1,0:T(8,128)S(1)}, u32[]{:S(2)}, u32[]{:S(2)}) collective-permute-start(f32[2,2,128,1024]{3,2,1,0:T(8,128)} %get-tuple-element.117), channel_id=1, source_target_pairs={{0,4},{4,8},{8,12},{12,16},{16,20},{20,24},{24,28},{1,5},{5,9},{9,... | collective-permute-start | bytes 6291464 | tf_op jit(solution)/shard_map/ppermute | solution.py:224
  230.6 24.2 %collective-permute-start.17 = (f32[64,256]{1,0:T(8,128)S(1)}, f32[64,256]{1,0:T(8,128)S(1)}, u32[]{:S(2)}, u32[]{:S(2)}) collective-permute-start(f32[64,256]{1,0:T(8,128)S(1)} %pad_maximum_fusion.2), channel_id=1, source_target_pairs={{0,16},{4,20},{8,24},{12,28},{16,0},{20,4},{24,8},{28,12},{1,17},{... | collective-permute-start | bytes 196616 | tf_op jit(solution)/shard_map/ppermute | solution.py:243
  254.8 42.9 %collective-permute-start.9 = (f32[2,2,128,1024]{3,2,1,0:T(8,128)}, f32[2,2,128,1024]{3,2,1,0:T(8,128)}, u32[]{:S(2)}, u32[]{:S(2)}) collective-permute-start(f32[2,2,128,1024]{3,2,1,0:T(8,128)} %get-tuple-element.116), channel_id=1, source_target_pairs={{4,0},{8,4},{12,8},{16,12},{20,16},{24,20},{28,24},{5,1},{9,5},{13... | collective-permute-start | bytes 6291464 | tf_op jit(solution)/shard_map/ppermute | solution.py:224
  256.8 4.8 %collective-permute-start.18 = (f32[128,256]{1,0:T(8,128)S(1)}, f32[128,256]{1,0:T(8,128)}, u32[]{:S(2)}, u32[]{:S(2)}) collective-permute-start(f32[128,256]{1,0:T(8,128)S(1)} %pad_maximum_fusion.1), channel_id=1, source_target_pairs={{0,8},{4,12},{8,0},{12,4},{16,24},{20,28},{24,16},{28,20},{1,9},{5... | collective-permute-start | bytes 393224 | tf_op jit(solution)/shard_map/ppermute | solution.py:243
  263.2 25.3 %collective-permute-start.19 = (f32[256,256]{1,0:T(8,128)}, f32[256,256]{1,0:T(8,128)}, u32[]{:S(2)}, u32[]{:S(2)}) collective-permute-start(f32[256,256]{1,0:T(8,128)} %pad_maximum_fusion), channel_id=1, source_target_pairs={{0,4},{4,0},{8,12},{12,8},{16,20},{20,16},{24,28},{28,24},{1,5},{5... | collective-permute-start | bytes 786440 | tf_op jit(solution)/shard_map/ppermute | solution.py:243
where the time goes:
time: 304 us; the launch traced here: 302 us
  starting transfers between devices  97.5 us (32%)
  waiting for transfers between devices  96 us (32%)
  local copies, waits for them, and re-layouts  75.7 us (25%)
  other arithmetic  20.5 us (7%)
  Pallas kernels  10.4 us (3%)
    ppermute x5, starting transfers between devices, sum_everywhere(): flat = mine + lax.ppermute(other, axis, pairs)  40.5 us
    ppermute x10, waiting for transfers between devices, send(): lax.ppermute(x, axis, [(i, i + step) for i in range(count) if 0 <= i + st...  38.3 us
    transpose x1, local copies, waits for them, and re-layouts, per_device(): jnp.sqrt(patterns).reshape(slots, rim, 2, rim, 2).transpose(0, 2, 1, 4, 3)  36.3 us
    ppermute x5, waiting for transfers between devices, sum_everywhere(): other = lax.ppermute(flat, axis, pairs)  33.1 us
    ppermute x10, starting transfers between devices, send(): lax.ppermute(x, axis, [(i, i + step) for i in range(count) if 0 <= i + st...  28.9 us
    ppermute x5, starting transfers between devices, sum_everywhere(): other = lax.ppermute(flat, axis, pairs)  28.1 us
    ppermute x5, waiting for transfers between devices, sum_everywhere(): flat = mine + lax.ppermute(other, axis, pairs)  24.6 us
    sqrt x2, local copies, waits for them, and re-layouts, per_device(): jnp.sqrt(patterns).reshape(slots, rim, 2, rim, 2).transpose(0, 2, 1, 4, 3)  21 us
  transfers between devices with their start and end apart: 20, of which 11 were waited for; matrix products, arithmetic and copies ran while one was open for 26% of the time, Pallas kernels for 0%

commit v1 on v0

v1 whole, which is shorter than its diff:
```python
import math

import jax
import jax.numpy as jnp
import ml_dtypes
import numpy as np
from jax import lax
from jax.experimental import pallas as pl
from jax.experimental.pallas import tpu as pltpu
from jax.sharding import PartitionSpec as P

KAPPA = 40.0
F32 = jnp.float32
FWD, INV, PROP, ADJ = 0, 1, 2, 3
LEFT = {FWD: (0, 2), INV: (1, 3), PROP: (4, 6), ADJ: (5, 7)}
RIGHT = {FWD: (1, 3), INV: (0, 2), PROP: (5, 7), ADJ: (4, 6)}


def tables(width):
    half = width // 2
    n = np.arange(half)
    freq = ((np.arange(width) + half) % width - half) / width
    factor = np.exp(-1j * math.pi * KAPPA * freq * freq)
    turn = 2j * np.pi / width
    scale = 1.0 / math.sqrt(width)
    even = np.exp(-turn * ((2 * n[:, None] * n[None, :]) % width)) * scale
    odd = np.exp(-turn * (((2 * n[:, None] + 1) * n[None, :]) % width)) * scale

    def combined(freqs):
        apart = n[:, None] - n[None, :]
        total = np.zeros((half, half), complex)
        for k in freqs:
            total += factor[k] * np.exp(turn * ((k * apart) % width))
        return total / width

    lefts, rights = [], []
    for c in (even, odd, combined(range(0, width, 2)), combined(range(1, width, 2))):
        real = np.block([[c.real, -c.imag], [c.imag, c.real]])
        for m in (real, real.T):
            hi = m.astype(ml_dtypes.bfloat16)
            lo = (m - hi.astype(np.float64)).astype(ml_dtypes.bfloat16)
            lefts.append(np.concatenate([hi, hi, lo], axis=1))
            rights.append(np.concatenate([hi, hi, lo], axis=0))
    return jnp.asarray(np.stack(lefts)), jnp.asarray(np.stack(rights))


def split(x):
    hi = x.astype(jnp.bfloat16)
    return hi, (x - hi.astype(F32)).astype(jnp.bfloat16)


def pair(x, y, axis):
    return jnp.concatenate([x, y], axis=axis)


def one_side(re, im, kind, axis, table):
    half = re.shape[axis] // 2

    def halves(x):
        return (x[:half], x[half:]) if axis == 0 else (x[:, :half], x[:, half:])

    a, b = halves(re)
    c, d = halves(im)
    if kind != INV:
        a, b, c, d = a + b, a - b, c + d, c - d

    def product(x, index):
        hi, lo = split(x)
        stacked = jnp.concatenate([hi, lo, hi], axis=axis)
        if axis == 0:
            return jnp.dot(table[index], stacked, preferred_element_type=F32)
        return jnp.dot(stacked, table[index], preferred_element_type=F32)

    even, odd = (LEFT if axis == 0 else RIGHT)[kind]
    a, c = halves(product(pair(a, c, axis), even))
    b, d = halves(product(pair(b, d, axis), odd))
    if kind == FWD:
        return pair(a, b, axis), pair(c, d, axis)
    return pair(a + b, a - b, axis), pair(c + d, c - d, axis)


def transform(re, im, kind, lefts, rights):
    re, im = one_side(re, im, kind, 1, rights)
    return one_side(re, im, kind, 0, lefts)


def times(a, b, c, d):
    return a * c - b * d, a * d + b * c


def conj_times(a, b, c, d):
    return a * c + b * d, a * d - b * c


def field_loop(wanted, place, rows, cols, counts, patterns, probe, lefts, rights, obj, acc, g_probe):
    width = probe.shape[-1]
    row_index = lax.broadcasted_iota(jnp.int32, (width, width), 0)
    col_index = lax.broadcasted_iota(jnp.int32, (width, width), 1)

    def visit(slot):
        row, col = rows[slot], cols[slot]
        block = place(col // width)
        shift = col % width
        below = row_index < row
        beside = col_index < shift

        def cut(level, part):
            upper = jnp.where(beside, obj[block + 1, level, part, :width], obj[block, level, part, :width])
            lower = jnp.where(beside, obj[block + 1, level, part, width:], obj[block, level, part, width:])
            return jnp.where(below, lower, upper)

        def deposit(level, part, term):
            zero = jnp.zeros_like(term)
            upper = jnp.where(below, zero, term)
            lower = jnp.where(below, term, zero)
            acc[block, level, part, :width] += jnp.where(beside, zero, upper)
            acc[block, level, part, width:] += jnp.where(beside, zero, lower)
            acc[block + 1, level, part, :width] += jnp.where(beside, upper, zero)
            acc[block + 1, level, part, width:] += jnp.where(beside, lower, zero)

        def rolled(x, down, along):
            return pltpu.roll(pltpu.roll(x, down, 0), along, 1)

        u0 = rolled(probe[0], row, shift), rolled(probe[1], row, shift)
        o0 = cut(0, 0), cut(0, 1)
        u1 = transform(*times(*u0, *o0), PROP, lefts, rights)
        o1 = cut(1, 0), cut(1, 1)
        far_re, far_im = transform(*times(*u1, *o1), FWD, lefts, rights)
        factor = 1.0 - patterns[slot] * lax.rsqrt(far_re * far_re + far_im * far_im + 1.0)
        chi = transform(far_re * factor, far_im * factor, INV, lefts, rights)
        for part, term in enumerate(conj_times(*u1, *chi)):
            deposit(1, part, term)
        chi = transform(*conj_times(*o1, *chi), ADJ, lefts, rights)
        for part, term in enumerate(conj_times(*u0, *chi)):
            deposit(0, part, term)
        up, back = (width - row) % width, (width - shift) % width
        for part, term in enumerate(conj_times(*o0, *chi)):
            g_probe[part] += rolled(term, up, back)

    def step(slot, _):
        pl.when(wanted(cols[slot] // width))(lambda: visit(slot))
        return 0

    lax.fori_loop(0, counts[0], step, 0)


def run_all(pairs, sem):
    copies = [pltpu.make_async_copy(a, b, sem.at[i]) for i, (a, b) in enumerate(pairs)]
    for copy in copies:
        copy.start()
    return copies


def wait_all(copies):
    for copy in copies:
        copy.wait()


def chosen_copy(flag, other, usual, target, sem):
    pl.when(flag == 1)(lambda: pltpu.make_async_copy(other, target, sem).start())
    pl.when(flag != 1)(lambda: pltpu.make_async_copy(usual, target, sem).start())
    return pltpu.make_async_copy(usual, target, sem)


def outer_body(
    rows, cols, counts, tile, top_ends, bottom_ends, top_quarters, bottom_quarters, relayed, left, left_ends, right,
    right_ends, patterns, probe, lefts, rights,
    g_tile_ends, g_top_ends, g_bottom_ends, g_left, g_right, g_quarters, g_probe, obj, acc, sem,
):
    width = probe.shape[-1]
    rim = width // 2
    tile_rows, tile_cols = tile.shape[2], tile.shape[3]
    full = tile_rows + 2 * rim
    last_block = (tile_cols + 2 * rim) // width - 2
    own = slice(rim, rim + tile_rows)
    below = slice(rim + tile_rows, full)
    one, two = slice(0, rim), slice(rim, width)
    pairs = []
    for k, lanes, first in ((0, two, 0), (1, slice(0, width), rim), (2, slice(0, width), tile_cols - rim - width), (3, one, tile_cols - rim)):
        span = lanes.stop - lanes.start
        pairs.append((tile.at[:, :, :, first : first + span], obj.at[k, :, :, own, lanes]))
    for k, lanes, first in ((0, two, 0), (3, one, rim)):
        pairs.append((top_ends.at[:, :, :, first : first + rim], obj.at[k, :, :, :rim, lanes]))
        pairs.append((bottom_ends.at[:, :, :, first : first + rim], obj.at[k, :, :, below, lanes]))
    for k, lanes, side, ends in ((0, one, left, left_ends), (3, two, right, right_ends)):
        pairs.append((side, obj.at[k, :, :, own, lanes]))
        pairs.append((ends.at[:, :, :rim], obj.at[k, :, :, :rim, lanes]))
        pairs.append((ends.at[:, :, rim:], obj.at[k, :, :, below, lanes]))
    copies = run_all(pairs, sem)
    at = len(copies)
    for k in (0, 1):
        lanes = slice(k * width, (k + 1) * width)
        for flag, usual, place in ((1, top_quarters, slice(0, rim)), (2, bottom_quarters, below)):
            copies.append(chosen_copy(counts[flag], relayed.at[:, :, :, lanes], usual.at[:, :, :, lanes], obj.at[1 + k, :, :, place], sem.at[at]))
            at += 1
    acc[...] = jnp.zeros_like(acc)
    g_probe[...] = jnp.zeros_like(g_probe)
    wait_all(copies)

    field_loop(
        lambda block: (block == 0) | (block == last_block), lambda block: jnp.where(block == 0, 0, 2),
        rows, cols, counts, patterns, probe, lefts, rights, obj, acc, g_probe,
    )

    pairs = [(acc.at[0, :, :, :, one], g_left), (acc.at[3, :, :, :, two], g_right), (acc.at[1:3], g_quarters)]
    for k, lanes, half in ((0, two, one), (3, one, two)):
        pairs.append((acc.at[k, :, :, own, lanes], g_tile_ends.at[:, :, :, half]))
        pairs.append((acc.at[k, :, :, :rim, lanes], g_top_ends.at[:, :, :, half]))
        pairs.append((acc.at[k, :, :, below, lanes], g_bottom_ends.at[:, :, :, half]))
    wait_all(run_all(pairs, sem))


def inner_body(
    rows, cols, counts, tile, top_quarters, bottom_quarters, relayed, top_mid, bottom_mid, patterns, probe, lefts, rights,
    carried, carried_probe,
    g_tile, g_top_quarters, g_bottom_quarters, g_relay, g_top_mid, g_bottom_mid, g_probe, obj, acc, sem,
):
    width = probe.shape[-1]
    rim = width // 2
    tile_rows, tile_cols = tile.shape[2], tile.shape[3]
    full = tile_rows + 2 * rim
    blocks = (tile_cols - 2 * rim) // width
    own = slice(rim, rim + tile_rows)
    below = slice(rim + tile_rows, full)
    last = blocks - 1
    pairs = [(carried.at[0], acc.at[0]), (carried.at[1], acc.at[last])]
    for k in range(blocks):
        pairs.append((tile.at[:, :, :, rim + k * width : rim + (k + 1) * width], obj.at[k, :, :, own]))
    for k in range(1, last):
        lanes = slice((k - 1) * width, k * width)
        pairs.append((top_mid.at[:, :, :, lanes], obj.at[k, :, :, :rim]))
        pairs.append((bottom_mid.at[:, :, :, lanes], obj.at[k, :, :, below]))
    copies = run_all(pairs, sem)
    at = len(copies)
    for k, block in ((0, 0), (1, last)):
        lanes = slice(k * width, (k + 1) * width)
        for flag, usual, place in ((1, top_quarters, slice(0, rim)), (2, bottom_quarters, below)):
            copies.append(chosen_copy(counts[flag], relayed.at[:, :, :, lanes], usual.at[:, :, :, lanes], obj.at[block, :, :, place], sem.at[at]))
            at += 1
    for k in range(1, last):
        acc[k] = jnp.zeros_like(acc[k])
    g_probe[...] = carried_probe[...]
    wait_all(copies)

    field_loop(
        lambda block: (block > 0) & (block < blocks), lambda block: block - 1,
        rows, cols, counts, patterns, probe, lefts, rights, obj, acc, g_probe,
    )

    pairs = []
    for k in range(blocks):
        pairs.append((acc.at[k, :, :, own], g_tile.at[:, :, :, k * width : (k + 1) * width]))
    for k, block in ((0, 0), (1, last)):
        lanes = slice(k * width, (k + 1) * width)
        pairs.append((acc.at[block, :, :, :rim], g_top_quarters.at[:, :, :, lanes]))
        pairs.append((acc.at[block, :, :, below], g_bottom_quarters.at[:, :, :, lanes]))
    for k in range(1, last):
        lanes = slice((k - 1) * width, k * width)
        pairs.append((acc.at[k, :, :, :rim], g_top_mid.at[:, :, :, lanes]))
        pairs.append((acc.at[k, :, :, below], g_bottom_mid.at[:, :, :, lanes]))
    copies = run_all(pairs, sem)
    at = len(copies)
    for k, block in ((0, 0), (1, last)):
        lanes = slice(k * width, (k + 1) * width)
        copies.append(chosen_copy(counts[1], acc.at[block, :, :, :rim], acc.at[block, :, :, below], g_relay.at[:, :, :, lanes], sem.at[at]))
        at += 1
    wait_all(copies)


SMEM = pl.BlockSpec(memory_space=pltpu.SMEM)
VMEM = pl.BlockSpec(memory_space=pltpu.VMEM)
HBM = pl.BlockSpec(memory_space=pl.ANY)


def shape(*dims):
    return jax.ShapeDtypeStruct(dims, F32)


def field_call(body, blocks, scalars, arrays, fields, extra, outs, probe, tile_rows, flops):
    width = probe.shape[-1]
    padded = (blocks, 2, 2, tile_rows + width, width)
    return pl.pallas_call(
        body,
        out_shape=tuple(outs) + (jax.ShapeDtypeStruct(probe.shape, F32),),
        in_specs=[SMEM] * len(scalars) + [HBM] * len(arrays) + [VMEM] * len(fields) + [HBM, VMEM][: len(extra)],
        out_specs=(HBM,) * len(outs) + (VMEM,),
        scratch_shapes=[pltpu.VMEM(padded, F32), pltpu.VMEM(padded, F32), pltpu.SemaphoreType.DMA((32,))],
        compiler_params=pltpu.CompilerParams(vmem_limit_bytes=48 * 2**20),
        cost_estimate=pl.CostEstimate(flops=flops, bytes_accessed=2 * 10**7, transcendentals=0),
    )(*scalars, *arrays, *fields, *extra)


def amplitude_body(counts, patterns, pick, out):
    def work():
        hi, lo = split(jnp.sqrt(patterns[0]))
        both = jnp.dot(pick[0], pair(hi, lo, 1), preferred_element_type=F32).astype(jnp.bfloat16)
        out[0] = jnp.dot(pair(both[:, : hi.shape[1]], both[:, hi.shape[1] :], 1), pick[1:].reshape(-1, hi.shape[1]), preferred_element_type=F32)

    pl.when(pl.program_id(0) < counts[0])(work)


def amplitudes_of(counts, patterns):
    width = patterns.shape[-1]
    pick = np.zeros((width, width))
    pick[np.arange(width), np.concatenate([np.arange(0, width, 2), np.arange(1, width, 2)])] = 1
    pick = jnp.asarray(np.stack([pick, pick.T, pick.T]).astype(ml_dtypes.bfloat16))
    block = pl.BlockSpec((1, width, width), lambda i: (i, 0, 0))
    return pl.pallas_call(
        amplitude_body,
        grid=(patterns.shape[0],),
        out_shape=jax.ShapeDtypeStruct(patterns.shape, F32),
        in_specs=[SMEM, block, VMEM],
        out_specs=block,
        cost_estimate=pl.CostEstimate(flops=10**9, bytes_accessed=2 * patterns.size * 4, transcendentals=0),
    )(counts, patterns, pick)


def total_body(counts, ends, mids, left, right, above_ends, below_ends, above_q, below_q, relay, above_mid, below_mid, out):
    rim = left.shape[-1]
    rows = ends.shape[2]
    cols = out.shape[3]
    mid = cols - 2 * rim
    quarter = above_q.shape[3] // 2
    for first, count, x_ends, x_q, x_mid, flag in (
        (0, rim, above_ends, above_q, above_mid, 1), (rows - rim, rim, below_ends, below_q, below_mid, 2),
    ):
        here = slice(first, first + count)
        there = slice(rim + first, rim + first + count)
        out[:, :, here, :rim] = ends[:, :, here, :rim] + left[:, :, there] + x_ends[:, :, :, :rim]
        out[:, :, here, cols - rim :] = ends[:, :, here, rim:] + right[:, :, there] + x_ends[:, :, :, rim:]
        side = jnp.where(counts[flag] == 1, relay[...], x_q[...])
        out[:, :, here, rim : rim + quarter] = mids[:, :, here, :quarter] + side[:, :, :, :quarter]
        out[:, :, here, cols - rim - quarter : cols - rim] = mids[:, :, here, mid - quarter :] + side[:, :, :, quarter:]
        out[:, :, here, rim + quarter : cols - rim - quarter] = mids[:, :, here, quarter : mid - quarter] + x_mid[...]


def total_of(counts, parts, tile_shape):
    def block(dims):
        return pl.BlockSpec((1, 1) + tuple(dims[2:]), lambda i, j: (i, j, 0, 0))

    return pl.pallas_call(
        total_body,
        grid=tile_shape[:2],
        out_shape=jax.ShapeDtypeStruct(tile_shape, F32),
        in_specs=[SMEM] + [block(x.shape) for x in parts],
        out_specs=block(tile_shape),
        compiler_params=pltpu.CompilerParams(vmem_limit_bytes=32 * 2**20),
        cost_estimate=pl.CostEstimate(flops=10**7, bytes_accessed=2 * 10**7, transcendentals=0),
    )(counts, *parts)


def send(x, axis, step, skip=None):
    count = lax.axis_size(axis)
    return lax.ppermute(x, axis, [(i, i + step) for i in range(count) if 0 <= i + step < count and i != skip])


def relay(x):
    count = lax.axis_size("tx")
    low = count // 2 - 1
    x = lax.ppermute(x, "tx", [(low, count - 1), (low + 1, 0)])
    return lax.ppermute(x, "tx", [(count - 1, low + 1), (0, low)])


def sum_everywhere(x):
    flat = x.reshape(-1, x.shape[-1])
    done = []
    count = lax.axis_size("tx")
    apart = 1
    while apart < count:
        bit = (lax.axis_index("tx") // apart) % 2
        half = flat.shape[0] // 2
        pairs = [(i, i ^ apart) for i in range(count)]
        mine = lax.dynamic_slice_in_dim(flat, bit * half, half, 0)
        other = lax.dynamic_slice_in_dim(flat, (1 - bit) * half, half, 0)
        flat = mine + lax.ppermute(other, "tx", pairs)
        done.append((pairs, bit))
        apart *= 2
    count = lax.axis_size("ty")
    held = flat
    for step in range(1, count):
        flat = flat + lax.ppermute(held, "ty", [(i, (i + step) % count) for i in range(count)])
    for pairs, bit in reversed(done):
        other = lax.ppermute(flat, "tx", pairs)
        low = jnp.where(bit == 0, flat, other)
        high = jnp.where(bit == 0, other, flat)
        flat = jnp.concatenate([low, high], axis=0)
    return flat.reshape(x.shape)


def per_device(object_slab, probe, patterns, centers, counts):
    slices, _, tile_rows, tile_cols = object_slab.shape
    width = probe.shape[-1]
    rim = width // 2
    row_index = lax.axis_index("tx")
    col_index = lax.axis_index("ty")
    middle = lax.axis_size("tx") // 2
    my_count = counts[row_index * lax.axis_size("ty") + col_index]
    flags = jnp.stack([my_count, (row_index == middle).astype(jnp.int32), (row_index == middle - 1).astype(jnp.int32)])
    rows = centers[:, 0] - row_index * tile_rows
    cols = centers[:, 1] - col_index * tile_cols
    quarter = rim + width
    low, high = object_slab[:, :, :rim], object_slab[:, :, tile_rows - rim :]

    def ends_of(x):
        return jnp.concatenate([x[..., :rim], x[..., tile_cols - rim :]], axis=3)

    def quarters_of(x):
        return jnp.concatenate([x[..., rim:quarter], x[..., tile_cols - quarter : tile_cols - rim]], axis=3)

    def mid_of(x):
        return x[..., quarter : tile_cols - quarter]

    top_ends = send(ends_of(high), "tx", 1)
    bottom_ends = send(ends_of(low), "tx", -1)
    left = send(object_slab[..., tile_cols - rim :], "ty", 1)
    right = send(object_slab[..., :rim], "ty", -1)
    facing = lax.dynamic_slice_in_dim(object_slab, jnp.where(row_index < middle, tile_rows - rim, 0), rim, 2)
    relayed = relay(quarters_of(facing))
    top_quarters = send(quarters_of(high), "tx", 1, middle - 1)
    bottom_quarters = send(quarters_of(low), "tx", -1, middle)
    ends = jnp.concatenate([top_ends, bottom_ends], axis=2)
    left_ends = send(ends[..., rim:], "ty", 1)
    right_ends = send(ends[..., :rim], "ty", -1)
    top_mid = send(mid_of(high), "tx", 1)
    bottom_mid = send(mid_of(low), "tx", -1)

    scalars = (rows, cols, flags)
    fields = (amplitudes_of(flags, patterns), probe) + tables(width)
    full = tile_rows + width
    mid_cols = tile_cols - 2 * quarter
    ends_shape = shape(slices, 2, rim, width)
    quarters_shape = shape(slices, 2, rim, 2 * width)
    mid_shape = shape(slices, 2, rim, mid_cols)
    side_shape = shape(slices, 2, full, rim)
    g_tile_ends, g_top_ends, g_bottom_ends, g_left, g_right, g_quarters, g_probe = field_call(
        outer_body, 4, scalars,
        (object_slab, top_ends, bottom_ends, top_quarters, bottom_quarters, relayed, left, left_ends, right, right_ends),
        fields, (),
        (shape(slices, 2, tile_rows, width), ends_shape, ends_shape, side_shape, side_shape, shape(2, slices, 2, full, width)),
        probe, tile_rows, 8 * 10**9,
    )
    from_left = send(g_right, "ty", 1)
    from_right = send(g_left, "ty", -1)
    g_tile, g_top_quarters, g_bottom_quarters, g_relay, g_top_mid, g_bottom_mid, g_probe = field_call(
        inner_body, (tile_cols - 2 * rim) // width, scalars,
        (object_slab, top_quarters, bottom_quarters, relayed, top_mid, bottom_mid),
        fields, (g_quarters, g_probe),
        (shape(slices, 2, tile_rows, tile_cols - 2 * rim), quarters_shape, quarters_shape, quarters_shape, mid_shape, mid_shape),
        probe, tile_rows, 8 * 10**9,
    )
    back = relay(g_relay)
    below_quarters = send(g_top_quarters, "tx", -1, middle)
    above_quarters = send(g_bottom_quarters, "tx", 1, middle - 1)
    below_mid = send(g_top_mid, "tx", -1)
    above_mid = send(g_bottom_mid, "tx", 1)

    def with_sides(x, first, last):
        return x + jnp.concatenate([from_left[:, :, first:last], from_right[:, :, first:last]], axis=3)

    below_ends = send(with_sides(g_top_ends, 0, rim), "tx", -1)
    above_ends = send(with_sides(g_bottom_ends, full - rim, full), "tx", 1)
    probe_sum = sum_everywhere(g_probe)
    inner = total_of(
        flags,
        (g_tile_ends, g_tile, from_left, from_right, above_ends, below_ends, above_quarters, below_quarters, back, above_mid, below_mid),
        object_slab.shape,
    )
    positions = jnp.maximum(jnp.sum(counts), 1).astype(F32)
    return (inner, probe_sum / jnp.sqrt(positions))


def solution(mesh):
    placed = (
        P(None, None, "tx", "ty"),
        P(),
        P(("tx", "ty"), None, None),
        P(("tx", "ty"), None),
        P(),
    )
    return jax.shard_map(
        per_device,
        mesh=mesh,
        in_specs=placed,
        out_specs=(P(None, None, "tx", "ty"), P()),
        check_vma=False,
    )
```

time: 304 us -> 213 us (0.70)
  the two profiles are of different devices: /device:TPU:1 before, /device:TPU:22 now
where the time goes in v1:
time: 213 us; the launch traced here: 212 us
  starting transfers between devices  105 us (49%)
  waiting for transfers between devices  40.6 us (19%)
  Pallas kernels  35.6 us (17%)
  local copies, waits for them, and re-layouts  18.3 us (9%)
  other arithmetic  11 us (5%)
    ppermute x18, starting transfers between devices, send(): lax.ppermute(x, axis, [(i, i + step) for i in range(count) if 0 <= i + st...  50.4 us
    ppermute x18, waiting for transfers between devices, send(): lax.ppermute(x, axis, [(i, i + step) for i in range(count) if 0 <= i + st...  31.5 us
    ppermute x3, starting transfers between devices, sum_everywhere(): flat = mine + lax.ppermute(other, 'tx', pairs)  30.4 us
    pallas_call x2, Pallas kernels, field_call(): pl.pallas_call(body, out_shape=tuple(outs) + (jax.ShapeDtypeStruct(probe....  23.9 us
    unnamed x37, local copies, waits for them, and re-layouts  10.5 us
    ppermute x3, starting transfers between devices, sum_everywhere(): lax.ppermute(held, 'ty', [(i, (i + step) % count) for i in range(count)])  9.58 us
    ppermute x3, waiting for transfers between devices, sum_everywhere(): flat = mine + lax.ppermute(other, 'tx', pairs)  7.74 us
    ppermute x3, starting transfers between devices, sum_everywhere(): other = lax.ppermute(flat, 'tx', pairs)  7.65 us
  transfers between devices with their start and end apart: 31, of which 11 were waited for; matrix products, arithmetic and copies ran while one was open for 7% of the time, Pallas kernels for 7%

profile of v1, /device:TPU:22, one launch (start us, length us, event | category | flops | bytes accessed | tf_op | source)
XLA Modules:
  0.0 212.0 jit_solution(1891588194827466340)
XLA Ops:
  0.7 3.7 %fusion = (f32[2,2,128,256]{3,2,1,0:T(8,128)}, f32[2,2,128,256]{3,2,1,0:T(8,128)S(1)}, f32[2,2,128,256]{3,2,1,0:T(8,128)}, f32[2,2,128,256]{3,2,1,0:T(8,128)S(1)...) fusion(f32[2,2,256,1024]{3,2,1,0:T(8,128)} %tile.3, ...), kind=kLoop, calls=%fused_computation.30 | loop fusion | bytes 8388620 | tf_op jit(solution)/shard_map/slice | solution.py:411
  4.5 1.7 collective-permute-start.4
  6.4 1.9 collective-permute-start
  8.3 3.6 %collective-permute-start.1 = (f32[2,2,128,256]{3,2,1,0:T(8,128)S(1)}, f32[2,2,128,256]{3,2,1,0:T(8,128)S(1)}, u32[]{:S(2)}, u32[]{:S(2)}) collective-permute-start(f32[2,2,128,256]{3,2,1,0:T(8,128)S(1)} %pad_maximum_fusion.4), channel_id=1, source_target_pairs={{4,0},{8,4},{12,8},{16,12},{20,16},{24,20},{28,24},{5,1},{9,5},{13... | collective-permute-start | bytes 1572872 | tf_op jit(solution)/shard_map/ppermute | solution.py:354
  12.0 1.2 pad_maximum_fusion.1
  13.2 2.6 %collective-permute-start.3 = (f32[2,2,128,512]{3,2,1,0:T(8,128)}, f32[2,2,128,512]{3,2,1,0:T(8,128)}, u32[]{:S(2)}, u32[]{:S(2)}) collective-permute-start(f32[2,2,128,512]{3,2,1,0:T(8,128)} %pad_maximum_fusion.1), channel_id=1, source_target_pairs={{4,0},{8,4},{12,8},{20,16},{24,20},{28,24},{5,1},{9,5},{13,9},{21,... | collective-permute-start | bytes 3145736 | tf_op jit(solution)/shard_map/ppermute | solution.py:354
  15.8 1.1 pad_maximum_fusion
  16.9 2.7 %collective-permute-start.2 = (f32[2,2,128,512]{3,2,1,0:T(8,128)}, f32[2,2,128,512]{3,2,1,0:T(8,128)}, u32[]{:S(2)}, u32[]{:S(2)}) collective-permute-start(f32[2,2,128,512]{3,2,1,0:T(8,128)} %pad_maximum_fusion), channel_id=1, source_target_pairs={{0,4},{4,8},{8,12},{16,20},{20,24},{24,28},{1,5},{5,9},{9,13},{17,... | collective-permute-start | bytes 3145736 | tf_op jit(solution)/shard_map/ppermute | solution.py:354
  19.7 3.5 %collective-permute-start.6 = (f32[2,2,256,128]{3,2,1,0:T(8,128)S(1)}, f32[2,2,256,128]{3,2,1,0:T(8,128)S(1)}, u32[]{:S(2)}, u32[]{:S(2)}) collective-permute-start(f32[2,2,256,128]{3,2,1,0:T(8,128)S(1)} %get-tuple-element.39), channel_id=1, source_target_pairs={{0,1},{1,2},{2,3},{4,5},{5,6},{6,7},{8,9},{9,10},{10,11},{12,13},{... | collective-permute-start | bytes 1572872 | tf_op jit(solution)/shard_map/ppermute | solution.py:354
  23.3 2.5 %collective-permute-start.8 = (f32[2,2,256,128]{3,2,1,0:T(8,128)S(1)}, f32[2,2,256,128]{3,2,1,0:T(8,128)S(1)}, u32[]{:S(2)}, u32[]{:S(2)}) collective-permute-start(f32[2,2,256,128]{3,2,1,0:T(8,128)S(1)} %get-tuple-element.38), channel_id=1, source_target_pairs={{1,0},{2,1},{3,2},{5,4},{6,5},{7,6},{9,8},{10,9},{11,10},{13,12},{... | collective-permute-start | bytes 1572872 | tf_op jit(solution)/shard_map/ppermute | solution.py:354
  25.8 1.7 collective-permute-start.5
  28.5 6.3 %collective-permute-done.6.left = f32[2,2,256,128]{3,2,1,0:T(8,128)S(1)} collective-permute-done((f32[2,2,256,128]{3,2,1,0:T(8,128)S(1)}, f32[2,2,256,128]{3,2,1,0:T(8,128)S(1)}, u32[]{:S(2)}, u32[]{:S(2)}) %collective-permute-start.6) | collective-permute-done | bytes 524320 | tf_op jit(solution)/shard_map/ppermute | solution.py:354
  34.8 3.5 %collective-permute-start.7 = (f32[2,2,256,128]{3,2,1,0:T(8,128)}, f32[2,2,256,128]{3,2,1,0:T(8,128)S(1)}, u32[]{:S(2)}, u32[]{:S(2)}) collective-permute-start(f32[2,2,256,128]{3,2,1,0:T(8,128)} %get-tuple-element.49), channel_id=1, source_target_pairs={{0,1},{1,2},{2,3},{4,5},{5,6},{6,7},{8,9},{9,10},{10,11},{12,13},{... | collective-permute-start | bytes 1572872 | tf_op jit(solution)/shard_map/ppermute | solution.py:354
  38.3 2.4 %collective-permute-start.9 = (f32[2,2,256,128]{3,2,1,0:T(8,128)}, f32[2,2,256,128]{3,2,1,0:T(8,128)}, u32[]{:S(2)}, u32[]{:S(2)}) collective-permute-start(f32[2,2,256,128]{3,2,1,0:T(8,128)} %get-tuple-element.48), channel_id=1, source_target_pairs={{1,0},{2,1},{3,2},{5,4},{6,5},{7,6},{9,8},{10,9},{11,10},{13,12},{... | collective-permute-start | bytes 1572872 | tf_op jit(solution)/shard_map/ppermute | solution.py:354
  41.3 1.2 pad_add_fusion.counts
  42.5 6.2 %shard_map.95.patterns = f32[8,256,256]{2,1,0:T(8,128)} custom-call(s32[3]{0:T(128)} %pad_add_fusion.counts, f32[8,256,256]{2,1,0:T(8,128)} %patterns.1, bf16[3,256,256]{2,1,0:T(8,128)(2,1)} %constant.82.clone.pick), custom_call_target="tpu_custom_call" | custom-call | flops 1000000000 | bytes 4194304 | tf_op jit(solution)/shard_map/pallas_call | solution.py:308
  48.7 1.9 collective-permute-start.10
  50.7 3.6 %collective-permute-start.11 = (f32[2,2,128,256]{3,2,1,0:T(8,128)}, f32[2,2,128,256]{3,2,1,0:T(8,128)S(1)}, u32[]{:S(2)}, u32[]{:S(2)}) collective-permute-start(f32[2,2,128,256]{3,2,1,0:T(8,128)} %get-tuple-element.30), channel_id=1, source_target_pairs={{4,0},{8,4},{12,8},{16,12},{20,16},{24,20},{28,24},{5,1},{9,5},{13... | collective-permute-start | bytes 1572872 | tf_op jit(solution)/shard_map/ppermute | solution.py:354
  54.4 9.6 %shard_map.96 = (f32[2,2,256,256]{3,2,1,0:T(8,128)}, f32[2,2,128,256]{3,2,1,0:T(8,128)S(1)}, f32[2,2,128,256]{3,2,1,0:T(8,128)S(1)}, f32[2,2,512,128]{3,2,1,0:T(...) custom-call(s32[8]{0:T(128)S(1)} %get-tuple-element.57.rows, ...), custom_call_target="tpu_custom_call" | custom-call | flops 8000000000 | bytes 20000000 | tf_op jit(solution)/shard_map/pallas_call | solution.py:282
  65.6 14.4 %shard_map.97 = (f32[2,2,256,768]{3,2,1,0:T(8,128)}, f32[2,2,128,512]{3,2,1,0:T(8,128)S(1)}, f32[2,2,128,512]{3,2,1,0:T(8,128)}, f32[2,2,128,512]{3,2,1,0:T(8,12...) custom-call(s32[8]{0:T(128)S(1)} %get-tuple-element.57.rows, ...), custom_call_target="tpu_custom_call" | custom-call | flops 8000000000 | bytes 20000000 | tf_op jit(solution)/shard_map/pallas_call | solution.py:282
  82.7 1.5 collective-permute-done.22
  84.3 22.9 %collective-permute-start.23 = (f32[128,256]{1,0:T(8,128)S(1)}, f32[128,256]{1,0:T(8,128)S(1)}, u32[]{:S(2)}, u32[]{:S(2)}) collective-permute-start(f32[128,256]{1,0:T(8,128)S(1)} %constant_dynamic-slice_fusion.2), channel_id=1, source_target_pairs={{0,8},{4,12},{8,0},{12,4},{16,24},{20,28},{24,16},{28,20},{1,9},{5... | collective-permute-start | bytes 393224 | tf_op jit(solution)/shard_map/ppermute | solution.py:375
  107.2 4.0 %collective-permute-done.23 = f32[128,256]{1,0:T(8,128)S(1)} collective-permute-done((f32[128,256]{1,0:T(8,128)S(1)}, f32[128,256]{1,0:T(8,128)S(1)}, u32[]{:S(2)}, u32[]{:S(2)}) %collective-permute-start.23) | collective-permute-done | bytes 131104 | tf_op jit(solution)/shard_map/ppermute | solution.py:375
  111.3 7.4 %collective-permute-start.24 = (f32[64,256]{1,0:T(8,128)S(1)}, f32[64,256]{1,0:T(8,128)S(1)}, u32[]{:S(2)}, u32[]{:S(2)}) collective-permute-start(f32[64,256]{1,0:T(8,128)S(1)} %constant_dynamic-slice_fusion.1), channel_id=1, source_target_pairs={{0,16},{4,20},{8,24},{12,28},{16,0},{20,4},{24,8},{28,12},{1,17},{... | collective-permute-start | bytes 196616 | tf_op jit(solution)/shard_map/ppermute | solution.py:375
  118.7 2.2 %collective-permute-done.24 = f32[64,256]{1,0:T(8,128)S(1)} collective-permute-done((f32[64,256]{1,0:T(8,128)S(1)}, f32[64,256]{1,0:T(8,128)S(1)}, u32[]{:S(2)}, u32[]{:S(2)}) %collective-permute-start.24) | collective-permute-done | bytes 65568 | tf_op jit(solution)/shard_map/ppermute | solution.py:375
  121.0 9.5 %collective-permute-start.26 = (f32[64,256]{1,0:T(8,128)S(1)}, f32[64,256]{1,0:T(8,128)S(1)}, u32[]{:S(2)}, u32[]{:S(2)}) collective-permute-start(f32[64,256]{1,0:T(8,128)S(1)} %dynamic-slice_add_fusion.2), channel_id=1, source_target_pairs={{0,2},{1,3},{2,0},{3,1},{4,6},{5,7},{6,4},{7,5},{8,10},{9,11},{10,... | collective-permute-start | bytes 196616 | tf_op jit(solution)/shard_map/ppermute | solution.py:381
  130.5 3.9 %collective-permute-start.12 = (f32[2,2,512,128]{3,2,1,0:T(8,128)}, f32[2,2,512,128]{3,2,1,0:T(8,128)}, u32[]{:S(2)}, u32[]{:S(2)}) collective-permute-start(f32[2,2,512,128]{3,2,1,0:T(8,128)} %get-tuple-element.20), channel_id=1, source_target_pairs={{0,1},{1,2},{2,3},{4,5},{5,6},{6,7},{8,9},{9,10},{10,11},{12,13},{... | collective-permute-start | bytes 3145736 | tf_op jit(solution)/shard_map/ppermute | solution.py:354
  134.9 2.8 %collective-permute-start.13 = (f32[2,2,512,128]{3,2,1,0:T(8,128)}, f32[2,2,512,128]{3,2,1,0:T(8,128)}, u32[]{:S(2)}, u32[]{:S(2)}) collective-permute-start(f32[2,2,512,128]{3,2,1,0:T(8,128)} %get-tuple-element.21), channel_id=1, source_target_pairs={{1,0},{2,1},{3,2},{5,4},{6,5},{7,6},{9,8},{10,9},{11,10},{13,12},{... | collective-permute-start | bytes 3145736 | tf_op jit(solution)/shard_map/ppermute | solution.py:354
  137.7 1.7 collective-permute-start.18
  139.4 5.0 %collective-permute-start.29 = (f32[128,256]{1,0:T(8,128)S(1)}, f32[128,256]{1,0:T(8,128)S(1)}, u32[]{:S(2)}, u32[]{:S(2)}) collective-permute-start(f32[128,256]{1,0:T(8,128)S(1)} %pad_maximum_fusion.6), channel_id=1, source_target_pairs={{0,8},{4,12},{8,0},{12,4},{16,24},{20,28},{24,16},{28,20},{1,9},{5... | collective-permute-start | bytes 393224 | tf_op jit(solution)/shard_map/ppermute | solution.py:383
  144.5 1.9 collective-permute-start.16
  148.1 2.2 %collective-permute-start.20 = (f32[2,2,128,256]{3,2,1,0:T(8,128)}, f32[2,2,128,256]{3,2,1,0:T(8,128)S(1)}, u32[]{:S(2)}, u32[]{:S(2)}) collective-permute-start(f32[2,2,128,256]{3,2,1,0:T(8,128)} %copy-done.12), channel_id=1, source_target_pairs={{0,4},{4,8},{8,12},{12,16},{16,20},{20,24},{24,28},{1,5},{5,9},{9,... | collective-permute-start | bytes 1572872 | tf_op jit(solution)/shard_map/ppermute | solution.py:354
  151.2 5.9 %collective-permute-done.12.left = f32[2,2,512,128]{3,2,1,0:T(8,128)} collective-permute-done((f32[2,2,512,128]{3,2,1,0:T(8,128)}, f32[2,2,512,128]{3,2,1,0:T(8,128)}, u32[]{:S(2)}, u32[]{:S(2)}) %collective-permute-start.12) | collective-permute-done | bytes 1048608 | tf_op jit(solution)/shard_map/ppermute | solution.py:354
  157.1 1.9 collective-permute-start.17
  159.0 1.1 fusion.3
  160.1 3.4 %collective-permute-start.21 = (f32[2,2,128,256]{3,2,1,0:T(8,128)}, f32[2,2,128,256]{3,2,1,0:T(8,128)S(1)}, u32[]{:S(2)}, u32[]{:S(2)}) collective-permute-start(f32[2,2,128,256]{3,2,1,0:T(8,128)} %copy-done.11), channel_id=1, source_target_pairs={{4,0},{8,4},{12,8},{16,12},{20,16},{24,20},{28,24},{5,1},{9,5},{13... | collective-permute-start | bytes 1572872 | tf_op jit(solution)/shard_map/ppermute | solution.py:354
  163.6 1.7 collective-permute-start.19
  165.2 1.1 fusion.4
  167.2 2.5 %collective-permute-start.30 = (f32[256,256]{1,0:T(8,128)S(1)}, f32[256,256]{1,0:T(8,128)S(1)}, u32[]{:S(2)}, u32[]{:S(2)}) collective-permute-start(f32[256,256]{1,0:T(8,128)S(1)} %pad_maximum_fusion.5), channel_id=1, source_target_pairs={{0,4},{4,0},{8,12},{12,8},{16,20},{20,16},{24,28},{28,24},{1,5},{5... | collective-permute-start | bytes 786440 | tf_op jit(solution)/shard_map/ppermute | solution.py:383
  169.7 1.9 maximum_add_fusion.1
  171.7 1.9 maximum_add_fusion
  173.6 13.3 %collective-permute-done.21.below_mid = f32[2,2,128,256]{3,2,1,0:T(8,128)S(1)} collective-permute-done((f32[2,2,128,256]{3,2,1,0:T(8,128)}, f32[2,2,128,256]{3,2,1,0:T(8,128)S(1)}, u32[]{:S(2)}, u32[]{:S(2)}) %collective-permute-start.21) | collective-permute-done | bytes 524320 | tf_op jit(solution)/shard_map/ppermute | solution.py:354
  187.7 4.1 %collective-permute-start.15 = (f32[2,2,128,256]{3,2,1,0:T(8,128)}, f32[2,2,128,256]{3,2,1,0:T(8,128)}, u32[]{:S(2)}, u32[]{:S(2)}) collective-permute-start(f32[2,2,128,256]{3,2,1,0:T(8,128)} %maximum_add_fusion.1), channel_id=1, source_target_pairs={{4,0},{8,4},{12,8},{16,12},{20,16},{24,20},{28,24},{5,1},{9,5},{13... | collective-permute-start | bytes 1572872 | tf_op jit(solution)/shard_map/ppermute | solution.py:354
  192.5 1.9 collective-permute-start.14
  197.4 1.3 collective-permute-done.15.below_ends
  198.8 4.5 %collective-permute-done.14.above_ends = f32[2,2,128,256]{3,2,1,0:T(8,128)} collective-permute-done((f32[2,2,128,256]{3,2,1,0:T(8,128)}, f32[2,2,128,256]{3,2,1,0:T(8,128)}, u32[]{:S(2)}, u32[]{:S(2)}) %collective-permute-start.14) | collective-permute-done | bytes 524320 | tf_op jit(solution)/shard_map/ppermute | solution.py:354
  203.3 1.2 copy-done.1
  206.6 5.4 %shard_map.98 = f32[2,2,256,1024]{3,2,1,0:T(8,128)} custom-call(s32[3]{0:T(128)S(1)} %copy-done.8, f32[2,2,256,256]{3,2,1,0:T(8,128)S(1)} %copy-done.1, f32[2,2,256,768]{3,2,1,0:T(8,128)S(1)} %copy-done, f32[2,2,512,128]{3,2,1,0:T(8,128)} %collective-permute-done.12.left, f32[2,2,512,128]{3,2,1,0:T(8,128)} %collective-permute-done.13.right, ...), custom_call_target="tpu_custom_call" | custom-call | flops 10000000 | bytes 20000000 | tf_op jit(solution)/shard_map/pallas_call | solution.py:341
  (86 shorter events, 16.6 us)
Async XLA Ops:
  0.6 5.6 %copy-start.13 = (f32[2,2,256,1024]{3,2,1,0:T(8,128)S(1)}, f32[2,2,256,1024]{3,2,1,0:T(8,128)}, u32[]{:S(2)}) copy-start(f32[2,2,256,1024]{3,2,1,0:T(8,128)} %tile.3) | copy-start | bytes 12582916
  4.5 21.2 %collective-permute-start.4 = (f32[2,2,128,512]{3,2,1,0:T(8,128)S(1)}, f32[2,2,128,512]{3,2,1,0:T(8,128)}, u32[]{:S(2)}, u32[]{:S(2)}) collective-permute-start(f32[2,2,128,512]{3,2,1,0:T(8,128)S(1)} %pad_maximum_fusion.2), channel_id=1, source_target_pairs={{12,28},{16,0},{13,29},{17,1},{14,30},{18,2},{15,31},{19,3}} | collective-permute-start | bytes 3145736 | tf_op jit(solution)/shard_map/ppermute | solution.py:360
  6.4 13.3 %collective-permute-start = (f32[2,2,128,256]{3,2,1,0:T(8,128)S(1)}, f32[2,2,128,256]{3,2,1,0:T(8,128)S(1)}, u32[]{:S(2)}, u32[]{:S(2)}) collective-permute-start(f32[2,2,128,256]{3,2,1,0:T(8,128)S(1)} %pad_maximum_fusion.3), channel_id=1, source_target_pairs={{0,4},{4,8},{8,12},{12,16},{16,20},{20,24},{24,28},{1,5},{5,9},{9,... | collective-permute-start | bytes 1572872 | tf_op jit(solution)/shard_map/ppermute | solution.py:354
  8.3 14.9 %collective-permute-start.1 = (f32[2,2,128,256]{3,2,1,0:T(8,128)S(1)}, f32[2,2,128,256]{3,2,1,0:T(8,128)S(1)}, u32[]{:S(2)}, u32[]{:S(2)}) collective-permute-start(f32[2,2,128,256]{3,2,1,0:T(8,128)S(1)} %pad_maximum_fusion.4), channel_id=1, source_target_pairs={{4,0},{8,4},{12,8},{16,12},{20,16},{24,20},{28,24},{5,1},{9,5},{13... | collective-permute-start | bytes 1572872 | tf_op jit(solution)/shard_map/ppermute | solution.py:354
  13.2 35.5 %collective-permute-start.3 = (f32[2,2,128,512]{3,2,1,0:T(8,128)}, f32[2,2,128,512]{3,2,1,0:T(8,128)}, u32[]{:S(2)}, u32[]{:S(2)}) collective-permute-start(f32[2,2,128,512]{3,2,1,0:T(8,128)} %pad_maximum_fusion.1), channel_id=1, source_target_pairs={{4,0},{8,4},{12,8},{20,16},{24,20},{28,24},{5,1},{9,5},{13,9},{21,... | collective-permute-start | bytes 3145736 | tf_op jit(solution)/shard_map/ppermute | solution.py:354
  15.8 24.9 %copy-start.17 = (s32[32]{0:T(128)S(1)}, s32[32]{0:T(128)}, u32[]{:S(2)}) copy-start(s32[32]{0:T(128)} %param.12) | copy-start | bytes 388
  16.9 33.8 %collective-permute-start.2 = (f32[2,2,128,512]{3,2,1,0:T(8,128)}, f32[2,2,128,512]{3,2,1,0:T(8,128)}, u32[]{:S(2)}, u32[]{:S(2)}) collective-permute-start(f32[2,2,128,512]{3,2,1,0:T(8,128)} %pad_maximum_fusion), channel_id=1, source_target_pairs={{0,4},{4,8},{8,12},{16,20},{20,24},{24,28},{1,5},{5,9},{9,13},{17,... | collective-permute-start | bytes 3145736 | tf_op jit(solution)/shard_map/ppermute | solution.py:354
  19.7 15.1 %collective-permute-start.6 = (f32[2,2,256,128]{3,2,1,0:T(8,128)S(1)}, f32[2,2,256,128]{3,2,1,0:T(8,128)S(1)}, u32[]{:S(2)}, u32[]{:S(2)}) collective-permute-start(f32[2,2,256,128]{3,2,1,0:T(8,128)S(1)} %get-tuple-element.39), channel_id=1, source_target_pairs={{0,1},{1,2},{2,3},{4,5},{5,6},{6,7},{8,9},{9,10},{10,11},{12,13},{... | collective-permute-start | bytes 1572872 | tf_op jit(solution)/shard_map/ppermute | solution.py:354
  23.2 25.5 %copy-start.16 = (s32[8,2]{0,1:T(2,128)S(1)}, s32[8,2]{0,1:T(2,128)}, u32[]{:S(2)}) copy-start(s32[8,2]{0,1:T(2,128)} %param.11) | copy-start | bytes 196
  23.2 31.1 %copy-start.10 = (f32[2,256,256]{2,1,0:T(8,128)S(1)}, f32[2,256,256]{2,1,0:T(8,128)}, u32[]{:S(2)}) copy-start(f32[2,256,256]{2,1,0:T(8,128)} %probe.3) | copy-start | bytes 1572868
  23.3 15.1 %collective-permute-start.8 = (f32[2,2,256,128]{3,2,1,0:T(8,128)S(1)}, f32[2,2,256,128]{3,2,1,0:T(8,128)S(1)}, u32[]{:S(2)}, u32[]{:S(2)}) collective-permute-start(f32[2,2,256,128]{3,2,1,0:T(8,128)S(1)} %get-tuple-element.38), channel_id=1, source_target_pairs={{1,0},{2,1},{3,2},{5,4},{6,5},{7,6},{9,8},{10,9},{11,10},{13,12},{... | collective-permute-start | bytes 1572872 | tf_op jit(solution)/shard_map/ppermute | solution.py:354
  25.8 28.6 %collective-permute-start.5 = (f32[2,2,128,512]{3,2,1,0:T(8,128)}, f32[2,2,128,512]{3,2,1,0:T(8,128)}, u32[]{:S(2)}, u32[]{:S(2)}) collective-permute-start(f32[2,2,128,512]{3,2,1,0:T(8,128)} %collective-permute-done.4), channel_id=1, source_target_pairs={{28,16},{0,12},{29,17},{1,13},{30,18},{2,14},{31,19},{3,15}} | collective-permute-start | bytes 3145736 | tf_op jit(solution)/shard_map/ppermute | solution.py:361
  34.8 19.5 %collective-permute-start.7 = (f32[2,2,256,128]{3,2,1,0:T(8,128)}, f32[2,2,256,128]{3,2,1,0:T(8,128)S(1)}, u32[]{:S(2)}, u32[]{:S(2)}) collective-permute-start(f32[2,2,256,128]{3,2,1,0:T(8,128)} %get-tuple-element.49), channel_id=1, source_target_pairs={{0,1},{1,2},{2,3},{4,5},{5,6},{6,7},{8,9},{9,10},{10,11},{12,13},{... | collective-permute-start | bytes 1572872 | tf_op jit(solution)/shard_map/ppermute | solution.py:354
  38.3 16.0 %collective-permute-start.9 = (f32[2,2,256,128]{3,2,1,0:T(8,128)}, f32[2,2,256,128]{3,2,1,0:T(8,128)}, u32[]{:S(2)}, u32[]{:S(2)}) collective-permute-start(f32[2,2,256,128]{3,2,1,0:T(8,128)} %get-tuple-element.48), channel_id=1, source_target_pairs={{1,0},{2,1},{3,2},{5,4},{6,5},{7,6},{9,8},{10,9},{11,10},{13,12},{... | collective-permute-start | bytes 1572872 | tf_op jit(solution)/shard_map/ppermute | solution.py:354
  42.5 11.9 %copy-start.8 = (s32[3]{0:T(128)S(1)}, s32[3]{0:T(128)}, u32[]{:S(2)}) copy-start(s32[3]{0:T(128)} %pad_add_fusion.counts) | copy-start | bytes 40
  48.7 16.9 %collective-permute-start.10 = (f32[2,2,128,256]{3,2,1,0:T(8,128)}, f32[2,2,128,256]{3,2,1,0:T(8,128)S(1)}, u32[]{:S(2)}, u32[]{:S(2)}) collective-permute-start(f32[2,2,128,256]{3,2,1,0:T(8,128)} %get-tuple-element.32), channel_id=1, source_target_pairs={{0,4},{4,8},{8,12},{12,16},{16,20},{20,24},{24,28},{1,5},{5,9},{9,... | collective-permute-start | bytes 1572872 | tf_op jit(solution)/shard_map/ppermute | solution.py:354
  50.7 14.9 %collective-permute-start.11 = (f32[2,2,128,256]{3,2,1,0:T(8,128)}, f32[2,2,128,256]{3,2,1,0:T(8,128)S(1)}, u32[]{:S(2)}, u32[]{:S(2)}) collective-permute-start(f32[2,2,128,256]{3,2,1,0:T(8,128)} %get-tuple-element.30), channel_id=1, source_target_pairs={{4,0},{8,4},{12,8},{16,12},{20,16},{24,20},{28,24},{5,1},{9,5},{13... | collective-permute-start | bytes 1572872 | tf_op jit(solution)/shard_map/ppermute | solution.py:354
  63.9 0.8 copy-start.2
  64.8 0.8 copy-start.3
  80.0 1.0 copy-start.9
  81.0 0.8 copy-start.11
  81.8 0.8 copy-start.12
  82.6 1.6 collective-permute-start.22
  84.3 26.9 %collective-permute-start.23 = (f32[128,256]{1,0:T(8,128)S(1)}, f32[128,256]{1,0:T(8,128)S(1)}, u32[]{:S(2)}, u32[]{:S(2)}) collective-permute-start(f32[128,256]{1,0:T(8,128)S(1)} %constant_dynamic-slice_fusion.2), channel_id=1, source_target_pairs={{0,8},{4,12},{8,0},{12,4},{16,24},{20,28},{24,16},{28,20},{1,9},{5... | collective-permute-start | bytes 393224 | tf_op jit(solution)/shard_map/ppermute | solution.py:375
  111.3 9.7 %collective-permute-start.24 = (f32[64,256]{1,0:T(8,128)S(1)}, f32[64,256]{1,0:T(8,128)S(1)}, u32[]{:S(2)}, u32[]{:S(2)}) collective-permute-start(f32[64,256]{1,0:T(8,128)S(1)} %constant_dynamic-slice_fusion.1), channel_id=1, source_target_pairs={{0,16},{4,20},{8,24},{12,28},{16,0},{20,4},{24,8},{28,12},{1,17},{... | collective-permute-start | bytes 196616 | tf_op jit(solution)/shard_map/ppermute | solution.py:375
  120.9 13.5 %collective-permute-start.25 = (f32[64,256]{1,0:T(8,128)S(1)}, f32[64,256]{1,0:T(8,128)S(1)}, u32[]{:S(2)}, u32[]{:S(2)}) collective-permute-start(f32[64,256]{1,0:T(8,128)S(1)} %dynamic-slice_add_fusion.2), channel_id=1, source_target_pairs={{0,1},{1,2},{2,3},{3,0},{4,5},{5,6},{6,7},{7,4},{8,9},{9,10},{10,1... | collective-permute-start | bytes 196616 | tf_op jit(solution)/shard_map/ppermute | solution.py:381
  121.0 13.5 %collective-permute-start.26 = (f32[64,256]{1,0:T(8,128)S(1)}, f32[64,256]{1,0:T(8,128)S(1)}, u32[]{:S(2)}, u32[]{:S(2)}) collective-permute-start(f32[64,256]{1,0:T(8,128)S(1)} %dynamic-slice_add_fusion.2), channel_id=1, source_target_pairs={{0,2},{1,3},{2,0},{3,1},{4,6},{5,7},{6,4},{7,5},{8,10},{9,11},{10,... | collective-permute-start | bytes 196616 | tf_op jit(solution)/shard_map/ppermute | solution.py:381
  130.5 4.3 %collective-permute-start.27 = (f32[64,256]{1,0:T(8,128)S(1)}, f32[64,256]{1,0:T(8,128)S(1)}, u32[]{:S(2)}, u32[]{:S(2)}) collective-permute-start(f32[64,256]{1,0:T(8,128)S(1)} %dynamic-slice_add_fusion.2), channel_id=1, source_target_pairs={{0,3},{1,0},{2,1},{3,2},{4,7},{5,4},{6,5},{7,6},{8,11},{9,8},{10,9... | collective-permute-start | bytes 196616 | tf_op jit(solution)/shard_map/ppermute | solution.py:381
  130.5 26.6 %collective-permute-start.12 = (f32[2,2,512,128]{3,2,1,0:T(8,128)}, f32[2,2,512,128]{3,2,1,0:T(8,128)}, u32[]{:S(2)}, u32[]{:S(2)}) collective-permute-start(f32[2,2,512,128]{3,2,1,0:T(8,128)} %get-tuple-element.20), channel_id=1, source_target_pairs={{0,1},{1,2},{2,3},{4,5},{5,6},{6,7},{8,9},{9,10},{10,11},{12,13},{... | collective-permute-start | bytes 3145736 | tf_op jit(solution)/shard_map/ppermute | solution.py:354
  134.8 4.6 %collective-permute-start.28 = (f32[64,256]{1,0:T(8,128)S(1)}, f32[64,256]{1,0:T(8,128)S(1)}, u32[]{:S(2)}, u32[]{:S(2)}) collective-permute-start(f32[64,256]{1,0:T(8,128)S(1)} %add_add_fusion), channel_id=1, source_target_pairs={{0,16},{4,20},{8,24},{12,28},{16,0},{20,4},{24,8},{28,12},{1,17},{... | collective-permute-start | bytes 196616 | tf_op jit(solution)/shard_map/ppermute | solution.py:383
  134.9 25.2 %collective-permute-start.13 = (f32[2,2,512,128]{3,2,1,0:T(8,128)}, f32[2,2,512,128]{3,2,1,0:T(8,128)}, u32[]{:S(2)}, u32[]{:S(2)}) collective-permute-start(f32[2,2,512,128]{3,2,1,0:T(8,128)} %get-tuple-element.21), channel_id=1, source_target_pairs={{1,0},{2,1},{3,2},{5,4},{6,5},{7,6},{9,8},{10,9},{11,10},{13,12},{... | collective-permute-start | bytes 3145736 | tf_op jit(solution)/shard_map/ppermute | solution.py:354
  137.7 25.8 %collective-permute-start.18 = (f32[2,2,128,512]{3,2,1,0:T(8,128)}, f32[2,2,128,512]{3,2,1,0:T(8,128)}, u32[]{:S(2)}, u32[]{:S(2)}) collective-permute-start(f32[2,2,128,512]{3,2,1,0:T(8,128)} %get-tuple-element.26), channel_id=1, source_target_pairs={{12,28},{16,0},{13,29},{17,1},{14,30},{18,2},{15,31},{19,3}} | collective-permute-start | bytes 3145736 | tf_op jit(solution)/shard_map/ppermute | solution.py:360
  139.4 8.0 %collective-permute-start.29 = (f32[128,256]{1,0:T(8,128)S(1)}, f32[128,256]{1,0:T(8,128)S(1)}, u32[]{:S(2)}, u32[]{:S(2)}) collective-permute-start(f32[128,256]{1,0:T(8,128)S(1)} %pad_maximum_fusion.6), channel_id=1, source_target_pairs={{0,8},{4,12},{8,0},{12,4},{16,24},{20,28},{24,16},{28,20},{1,9},{5... | collective-permute-start | bytes 393224 | tf_op jit(solution)/shard_map/ppermute | solution.py:383
  144.5 53.0 %collective-permute-start.16 = (f32[2,2,128,512]{3,2,1,0:T(8,128)}, f32[2,2,128,512]{3,2,1,0:T(8,128)}, u32[]{:S(2)}, u32[]{:S(2)}) collective-permute-start(f32[2,2,128,512]{3,2,1,0:T(8,128)} %get-tuple-element.24), channel_id=1, source_target_pairs={{0,4},{4,8},{8,12},{16,20},{20,24},{24,28},{1,5},{5,9},{9,13},{17,... | collective-permute-start | bytes 3145736 | tf_op jit(solution)/shard_map/ppermute | solution.py:354
  148.1 55.2 %copy-start = (f32[2,2,256,768]{3,2,1,0:T(8,128)S(1)}, f32[2,2,256,768]{3,2,1,0:T(8,128)}, u32[]{:S(2)}) copy-start(f32[2,2,256,768]{3,2,1,0:T(8,128)} %get-tuple-element.19.mids) | copy-start | bytes 9437188
  148.1 18.3 %collective-permute-start.20 = (f32[2,2,128,256]{3,2,1,0:T(8,128)}, f32[2,2,128,256]{3,2,1,0:T(8,128)S(1)}, u32[]{:S(2)}, u32[]{:S(2)}) collective-permute-start(f32[2,2,128,256]{3,2,1,0:T(8,128)} %copy-done.12), channel_id=1, source_target_pairs={{0,4},{4,8},{8,12},{12,16},{16,20},{20,24},{24,28},{1,5},{5,9},{9,... | collective-permute-start | bytes 1572872 | tf_op jit(solution)/shard_map/ppermute | solution.py:354
  157.1 40.3 %collective-permute-start.17 = (f32[2,2,128,512]{3,2,1,0:T(8,128)}, f32[2,2,128,512]{3,2,1,0:T(8,128)}, u32[]{:S(2)}, u32[]{:S(2)}) collective-permute-start(f32[2,2,128,512]{3,2,1,0:T(8,128)} %copy-done.9), channel_id=1, source_target_pairs={{4,0},{8,4},{12,8},{20,16},{24,20},{28,24},{5,1},{9,5},{13,9},{21,... | collective-permute-start | bytes 3145736 | tf_op jit(solution)/shard_map/ppermute | solution.py:354
  160.1 26.8 %collective-permute-start.21 = (f32[2,2,128,256]{3,2,1,0:T(8,128)}, f32[2,2,128,256]{3,2,1,0:T(8,128)S(1)}, u32[]{:S(2)}, u32[]{:S(2)}) collective-permute-start(f32[2,2,128,256]{3,2,1,0:T(8,128)} %copy-done.11), channel_id=1, source_target_pairs={{4,0},{8,4},{12,8},{16,12},{20,16},{24,20},{28,24},{5,1},{9,5},{13... | collective-permute-start | bytes 1572872 | tf_op jit(solution)/shard_map/ppermute | solution.py:354
  163.6 39.7 %collective-permute-start.19 = (f32[2,2,128,512]{3,2,1,0:T(8,128)}, f32[2,2,128,512]{3,2,1,0:T(8,128)}, u32[]{:S(2)}, u32[]{:S(2)}) collective-permute-start(f32[2,2,128,512]{3,2,1,0:T(8,128)} %collective-permute-done.18), channel_id=1, source_target_pairs={{28,16},{0,12},{29,17},{1,13},{30,18},{2,14},{31,19},{3,15}} | collective-permute-start | bytes 3145736 | tf_op jit(solution)/shard_map/ppermute | solution.py:361
  166.4 0.8 copy-start.4
  167.2 24.6 %collective-permute-start.30 = (f32[256,256]{1,0:T(8,128)S(1)}, f32[256,256]{1,0:T(8,128)S(1)}, u32[]{:S(2)}, u32[]{:S(2)}) collective-permute-start(f32[256,256]{1,0:T(8,128)S(1)} %pad_maximum_fusion.5), channel_id=1, source_target_pairs={{0,4},{4,0},{8,12},{12,8},{16,20},{20,16},{24,28},{28,24},{1,5},{5... | collective-permute-start | bytes 786440 | tf_op jit(solution)/shard_map/ppermute | solution.py:383
  186.9 0.8 copy-start.6
  187.7 11.1 %collective-permute-start.15 = (f32[2,2,128,256]{3,2,1,0:T(8,128)}, f32[2,2,128,256]{3,2,1,0:T(8,128)}, u32[]{:S(2)}, u32[]{:S(2)}) collective-permute-start(f32[2,2,128,256]{3,2,1,0:T(8,128)} %maximum_add_fusion.1), channel_id=1, source_target_pairs={{4,0},{8,4},{12,8},{16,12},{20,16},{24,20},{28,24},{5,1},{9,5},{13... | collective-permute-start | bytes 1572872 | tf_op jit(solution)/shard_map/ppermute | solution.py:354
  191.8 0.7 copy-start.14
  192.5 10.8 %collective-permute-start.14 = (f32[2,2,128,256]{3,2,1,0:T(8,128)}, f32[2,2,128,256]{3,2,1,0:T(8,128)}, u32[]{:S(2)}, u32[]{:S(2)}) collective-permute-start(f32[2,2,128,256]{3,2,1,0:T(8,128)} %maximum_add_fusion), channel_id=1, source_target_pairs={{0,4},{4,8},{8,12},{12,16},{16,20},{20,24},{24,28},{1,5},{5,9},{9,... | collective-permute-start | bytes 1572872 | tf_op jit(solution)/shard_map/ppermute | solution.py:354
  203.3 1.2 copy-start.1
  204.5 1.0 copy-start.5
  205.6 1.0 copy-start.7
  (1 other events, 0.7 us)

commit v2 on v0

v2 whole, which is shorter than its diff:
```python
import functools
import math

import jax
import jax.numpy as jnp
import ml_dtypes
import numpy as np
from jax import lax
from jax.experimental import pallas as pl
from jax.experimental.pallas import tpu as pltpu
from jax.sharding import PartitionSpec as P

KAPPA = 40.0
F32 = jnp.float32
FWD, INV, PROP, ADJ = 0, 1, 2, 3
LEFT = {FWD: (0, 2), INV: (1, 3), PROP: (4, 6), ADJ: (5, 7)}
RIGHT = {FWD: (1, 3), INV: (0, 2), PROP: (5, 7), ADJ: (4, 6)}


def tables(width):
    half = width // 2
    n = np.arange(half)
    freq = ((np.arange(width) + half) % width - half) / width
    factor = np.exp(-1j * math.pi * KAPPA * freq * freq)
    turn = 2j * np.pi / width
    scale = 1.0 / math.sqrt(width)
    even = np.exp(-turn * ((2 * n[:, None] * n[None, :]) % width)) * scale
    odd = np.exp(-turn * (((2 * n[:, None] + 1) * n[None, :]) % width)) * scale

    def combined(freqs):
        apart = n[:, None] - n[None, :]
        total = np.zeros((half, half), complex)
        for k in freqs:
            total += factor[k] * np.exp(turn * ((k * apart) % width))
        return total / width

    parts = []
    for c in (even, odd, combined(range(0, width, 2)), combined(range(1, width, 2))):
        real = np.block([[c.real, -c.imag], [c.imag, c.real]])
        for m in (real, real.T):
            hi = m.astype(ml_dtypes.bfloat16)
            lo = (m - hi.astype(np.float64)).astype(ml_dtypes.bfloat16)
            parts.append(np.concatenate([hi, lo], axis=0))
    return jnp.asarray(np.stack(parts))


def split(x):
    hi = x.astype(jnp.bfloat16)
    return hi, (x - hi.astype(F32)).astype(jnp.bfloat16)


def pair(x, y, axis):
    return jnp.concatenate([x, y], axis=axis)


def product(x, both, axis):
    size = both.shape[1]
    hi, lo = split(x)
    if axis == 0:
        first = jnp.dot(both, hi, preferred_element_type=F32)
        return first[:size] + first[size:] + jnp.dot(both[:size], lo, preferred_element_type=F32)
    first = jnp.dot(pair(hi, lo, 0), both[:size], preferred_element_type=F32)
    return first[: x.shape[0]] + first[x.shape[0] :] + jnp.dot(hi, both[size:], preferred_element_type=F32)


def one_side(re, im, kind, axis, table):
    half = re.shape[axis] // 2

    def halves(x):
        return (x[:half], x[half:]) if axis == 0 else (x[:, :half], x[:, half:])

    a, b = halves(re)
    c, d = halves(im)
    if kind != INV:
        a, b, c, d = a + b, a - b, c + d, c - d
    even, odd = (LEFT if axis == 0 else RIGHT)[kind]
    a, c = halves(product(pair(a, c, axis), table[even], axis))
    b, d = halves(product(pair(b, d, axis), table[odd], axis))
    if kind == FWD:
        return pair(a, b, axis), pair(c, d, axis)
    return pair(a + b, a - b, axis), pair(c + d, c - d, axis)


def transform(re, im, kind, table):
    re, im = one_side(re, im, kind, 1, table)
    return one_side(re, im, kind, 0, table)


def times(a, b, c, d):
    return a * c - b * d, a * d + b * c


def conj_times(a, b, c, d):
    return a * c + b * d, a * d - b * c


def visit(start, block, amplitude, probe, table, obj, acc, g_probe):
    width = probe.shape[-1]
    row, shift = start[0], start[1] % width
    below = lax.broadcasted_iota(jnp.int32, (width, width), 0) < row
    beside = lax.broadcasted_iota(jnp.int32, (width, width), 1) < shift

    def cut(level, part):
        upper = jnp.where(beside, obj[block + 1, level, part, :width], obj[block, level, part, :width])
        lower = jnp.where(beside, obj[block + 1, level, part, width:], obj[block, level, part, width:])
        return jnp.where(below, lower, upper)

    def deposit(level, part, term):
        zero = jnp.zeros_like(term)
        upper = jnp.where(below, zero, term)
        lower = jnp.where(below, term, zero)
        acc[block, level, part, :width] += jnp.where(beside, zero, upper)
        acc[block, level, part, width:] += jnp.where(beside, zero, lower)
        acc[block + 1, level, part, :width] += jnp.where(beside, upper, zero)
        acc[block + 1, level, part, width:] += jnp.where(beside, lower, zero)

    def rolled(x, down, along):
        return pltpu.roll(pltpu.roll(x, down, 0), along, 1)

    u0 = rolled(probe[0], row, shift), rolled(probe[1], row, shift)
    o0 = cut(0, 0), cut(0, 1)
    u1 = transform(*times(*u0, *o0), PROP, table)
    o1 = cut(1, 0), cut(1, 1)
    far_re, far_im = transform(*times(*u1, *o1), FWD, table)
    factor = 1.0 - amplitude() * lax.rsqrt(far_re * far_re + far_im * far_im + 1.0)
    chi = transform(far_re * factor, far_im * factor, INV, table)
    for part, term in enumerate(conj_times(*u1, *chi)):
        deposit(1, part, term)
    chi = transform(*conj_times(*o1, *chi), ADJ, table)
    for part, term in enumerate(conj_times(*u0, *chi)):
        deposit(0, part, term)
    up, back = (width - row) % width, (width - shift) % width
    for part, term in enumerate(conj_times(*o0, *chi)):
        g_probe[part] += rolled(term, up, back)


class Place:
    def __init__(self, axes, scalars, tile_rows, tile_cols, rim):
        down, along, self.centers, counts = scalars
        tx, ty = down[0], along[0]
        odd = tx % 2
        self.count = counts[tx * axes[1] + ty]
        self.relayed = (tx == axes[0] // 2) | (tx == axes[0] // 2 - 1)
        self.first = tx * tile_rows, ty * tile_cols
        inner = tile_rows - rim
        self.on_tile, self.off_tile = rows_at((1 - odd) * inner, rim), rows_at(odd * inner, rim)
        outer = tile_rows + rim
        self.on, self.off = rows_at((1 - odd) * outer, rim), rows_at(odd * outer, rim)

    def start(self, slot):
        return self.centers[slot, 0] - self.first[0], self.centers[slot, 1] - self.first[1]


def rows_at(first, count):
    return pl.ds(pl.multiple_of(first, count), count)


def start_all(pairs, sem, at):
    copies = [pltpu.make_async_copy(a, b, sem.at[at + i]) for i, (a, b) in enumerate(pairs)]
    for copy in copies:
        copy.start()
    return copies


def run_all(pairs, sem):
    return start_all(pairs, sem, 0)


def wait_all(copies):
    for copy in copies:
        copy.wait()


def start_chosen(flag, other, usual, pairs, sem, at):
    for k, (lanes, target) in enumerate(pairs):
        for here, source in ((flag, other), (jnp.logical_not(flag), usual)):
            pl.when(here)(lambda s=source.at[:, :, :, lanes], t=target, i=at + k: pltpu.make_async_copy(s, t, sem.at[i]).start())
    return [pltpu.make_async_copy(usual.at[:, :, :, lanes], target, sem.at[at + k]) for k, (lanes, target) in enumerate(pairs)]


def two_groups(here, firsts, step, loads, stores, amplitudes, amps, amp_sem, sem, probe, table, obj, acc, g_probe):
    width = probe.shape[-1]

    def mine(slot, g):
        return here.start(slot)[1] // width == jnp.where(g == 0, firsts[0], firsts[1])

    def amplitude_copy(slot):
        return pltpu.make_async_copy(amplitudes.at[slot], amps.at[slot], amp_sem.at[slot])

    def fetch(slot, _):
        pl.when(mine(slot, 0) | mine(slot, 1))(lambda: amplitude_copy(slot).start())
        return 0

    lax.fori_loop(0, here.count, fetch, 0)

    def group(g, _):
        for k in (0, 1):
            pl.when(g == k)(functools.partial(wait_all, loads[k]))

        def work(slot):
            def amplitude():
                amplitude_copy(slot).wait()
                return amps[slot]

            visit(here.start(slot), step * g, amplitude, probe, table, obj, acc, g_probe)

        def each(slot, _):
            pl.when(mine(slot, g))(lambda: work(slot))
            return 0

        lax.fori_loop(0, here.count, each, 0)
        for k in (0, 1):
            pl.when(g == k)(lambda k=k: start_all(stores[k], sem, k * len(stores[0])) and None)
        return 0

    lax.fori_loop(0, 2, group, 0)
    for k in (0, 1):
        wait_all([pltpu.make_async_copy(a, b, sem.at[k * len(stores[0]) + i]) for i, (a, b) in enumerate(stores[k])])


def inner_body(
    axes, tx, ty, centers, counts, tile, on, off_quarters, relayed, off_mid, amplitudes, probe_in, table_in,
    g_quarters, g_tile_mid, g_on_mid, g_off_mid, g_probe, obj, acc, probe, table, amps, sem, out_sem, amp_sem,
):
    width = probe.shape[-1]
    rim = width // 2
    tile_rows, tile_cols = tile.shape[2], tile.shape[3]
    here = Place(axes, (tx, ty, centers, counts), tile_rows, tile_cols, rim)
    own = slice(rim, rim + tile_rows)
    loads = ([(probe_in, probe), (table_in, table)], [])
    for k in range(3):
        there = slice(rim + k * width, rim + (k + 1) * width)
        loads[k // 2].append((tile.at[:, :, :, there], obj.at[k, :, :, own]))
        loads[k // 2].append((on.at[:, :, :, (k + 1) * width : (k + 2) * width], obj.at[k, :, :, here.on]))
    loads[0].append((off_mid, obj.at[1, :, :, here.off]))
    waits = []
    for k in (0, 1):
        at = 16 * k
        started = start_all(loads[k], sem, at)
        lanes = slice(k * width, (k + 1) * width)
        waits.append(started + start_chosen(here.relayed, relayed, off_quarters, [(lanes, obj.at[2 * k, :, :, here.off])], sem, at + len(started)))
    acc[...] = jnp.zeros_like(acc)
    g_probe[...] = jnp.zeros_like(g_probe)
    stores = (
        [(acc.at[0], g_quarters.at[0])],
        [
            (acc.at[2], g_quarters.at[1]),
            (acc.at[1, :, :, own], g_tile_mid),
            (acc.at[1, :, :, here.on], g_on_mid),
            (acc.at[1, :, :, here.off], g_off_mid),
        ],
    )
    two_groups(here, (1, 2), 1, waits, stores, amplitudes, amps, amp_sem, out_sem, probe, table, obj, acc, g_probe)


def outer_body(
    axes, tx, ty, centers, counts, tile, on, off_quarters, relayed, off_ends, left, right, carried, carried_probe, amplitudes, probe_in, table_in,
    g_tile_ends, g_tile_quarters, g_on_ends, g_on_quarters, g_off_ends, g_off_quarters, g_left, g_right, g_probe,
    obj, acc, probe, table, amps, sem, out_sem, amp_sem,
):
    width = probe.shape[-1]
    rim = width // 2
    tile_rows, tile_cols = tile.shape[2], tile.shape[3]
    here = Place(axes, (tx, ty, centers, counts), tile_rows, tile_cols, rim)
    own = slice(rim, rim + tile_rows)
    one, two = slice(0, rim), slice(rim, width)
    waits, stores = [], []
    for k, (end, quarter, near, far, half, side, g_side) in enumerate((
        (0, 1, two, slice(0, rim), one, left, g_left),
        (3, 2, one, slice(tile_cols - rim, tile_cols), two, right, g_right),
    )):
        first = rim if k == 0 else tile_cols - rim - width
        there = slice(first, first + width)
        edge = k * tile_cols
        loads = [(probe_in, probe), (table_in, table), (carried_probe, g_probe)] if k == 0 else []
        loads += [
            (tile.at[:, :, :, far], obj.at[end, :, :, own, near]),
            (side, obj.at[end, :, :, own, half]),
            (on.at[:, :, :, edge : edge + width], obj.at[end, :, :, here.on]),
            (off_ends.at[:, :, :, k * width : (k + 1) * width], obj.at[end, :, :, here.off]),
            (tile.at[:, :, :, there], obj.at[quarter, :, :, own]),
            (on.at[:, :, :, first + rim : first + rim + width], obj.at[quarter, :, :, here.on]),
            (carried.at[k], acc.at[quarter]),
        ]
        started = start_all(loads, sem, 16 * k)
        lanes = slice(k * width, (k + 1) * width)
        waits.append(started + start_chosen(here.relayed, relayed, off_quarters, [(lanes, obj.at[quarter, :, :, here.off])], sem, 16 * k + len(started)))
        stores.append([
            (acc.at[end, :, :, own, near], g_tile_ends.at[:, :, :, half]),
            (acc.at[end, :, :, here.on, near], g_on_ends.at[:, :, :, half]),
            (acc.at[end, :, :, here.off, near], g_off_ends.at[:, :, :, half]),
            (acc.at[end, :, :, :, half], g_side),
            (acc.at[quarter, :, :, own], g_tile_quarters.at[:, :, :, lanes]),
            (acc.at[quarter, :, :, here.on], g_on_quarters.at[:, :, :, lanes]),
            (acc.at[quarter, :, :, here.off], g_off_quarters.at[:, :, :, lanes]),
        ])
    for end in (0, 3):
        acc[end] = jnp.zeros_like(acc[end])
    last_block = (tile_cols + 2 * rim) // width - 2
    two_groups(here, (0, last_block), 2, waits, stores, amplitudes, amps, amp_sem, out_sem, probe, table, obj, acc, g_probe)


SMEM = pl.BlockSpec(memory_space=pltpu.SMEM)
VMEM = pl.BlockSpec(memory_space=pltpu.VMEM)
HBM = pl.BlockSpec(memory_space=pl.ANY)
ROOM = pltpu.CompilerParams(vmem_limit_bytes=60 * 2**20)


def shape(*dims):
    return jax.ShapeDtypeStruct(dims, F32)


def costs(flops):
    return pl.CostEstimate(flops=flops, bytes_accessed=10**7, transcendentals=0)


def field_call(body, axes, blocks, scalars, arrays, amplitudes, probe, outs, tile_rows):
    width = probe.shape[-1]
    padded = (blocks, 2, 2, tile_rows + width, width)
    table = tables(width)
    return pl.pallas_call(
        functools.partial(body, axes),
        out_shape=tuple(outs) + (jax.ShapeDtypeStruct(probe.shape, F32),),
        in_specs=[SMEM] * len(scalars) + [HBM] * (len(arrays) + 3),
        out_specs=(HBM,) * len(outs) + (VMEM,),
        scratch_shapes=[
            pltpu.VMEM(padded, F32),
            pltpu.VMEM(padded, F32),
            pltpu.VMEM(probe.shape, F32),
            pltpu.VMEM(table.shape, table.dtype),
            pltpu.VMEM(amplitudes.shape, F32),
            pltpu.SemaphoreType.DMA((32,)),
            pltpu.SemaphoreType.DMA((16,)),
            pltpu.SemaphoreType.DMA((amplitudes.shape[0],)),
        ],
        compiler_params=ROOM,
        cost_estimate=costs(2 * 10**10),
    )(*scalars, *arrays, amplitudes, probe, table)


def pack_body(tx, tile, left, right, quarters, mid, sem):
    rim = left.shape[-1]
    width = 2 * rim
    tile_rows, tile_cols = tile.shape[2], tile.shape[3]
    rows = rows_at((tx[0] % 2) * (tile_rows - rim), rim)
    quarter = rim + width
    far = tile_cols - quarter
    wait_all(run_all([
        (tile.at[:, :, :, :rim], left),
        (tile.at[:, :, :, tile_cols - rim :], right),
        (tile.at[:, :, rows, rim:quarter], quarters.at[:, :, :, :width]),
        (tile.at[:, :, rows, far : far + width], quarters.at[:, :, :, width:]),
        (tile.at[:, :, rows, quarter:far], mid),
    ], sem))


def strips_body(tx, tile, left, right, on, ends, sem):
    rim = left.shape[-1]
    tile_rows, tile_cols = tile.shape[2], tile.shape[3]
    odd = tx[0] % 2
    inner = tile_rows - rim
    on_rows, off_rows = rows_at((1 - odd) * inner, rim), rows_at(odd * inner, rim)
    wait_all(run_all([
        (left.at[:, :, on_rows], on.at[:, :, :, :rim]),
        (tile.at[:, :, on_rows], on.at[:, :, :, rim : rim + tile_cols]),
        (right.at[:, :, on_rows], on.at[:, :, :, rim + tile_cols :]),
        (left.at[:, :, off_rows], ends.at[:, :, :, :rim]),
        (tile.at[:, :, off_rows, :rim], ends.at[:, :, :, rim : 2 * rim]),
        (tile.at[:, :, off_rows, tile_cols - rim :], ends.at[:, :, :, 2 * rim : 3 * rim]),
        (right.at[:, :, off_rows], ends.at[:, :, :, 3 * rim :]),
    ], sem))


def copies_call(body, scalars, arrays, outs, flops):
    return pl.pallas_call(
        body,
        out_shape=tuple(outs),
        in_specs=[SMEM] * len(scalars) + [HBM] * len(arrays),
        out_specs=(VMEM,) * len(outs),
        scratch_shapes=[pltpu.SemaphoreType.DMA((8,))],
        compiler_params=ROOM,
        cost_estimate=costs(flops),
    )(*scalars, *arrays)


def amplitude_body(axes, tx, ty, counts, patterns, pick, out):
    width = patterns.shape[-1]

    def work():
        hi, lo = split(jnp.sqrt(patterns[0]))
        both = jnp.dot(pick[0], pair(hi, lo, 1), preferred_element_type=F32).astype(jnp.bfloat16)
        out[0] = jnp.dot(both, pick[1:].reshape(-1, width), preferred_element_type=F32)

    pl.when(pl.program_id(0) < counts[tx[0] * axes[1] + ty[0]])(work)


def amplitudes_of(axes, scalars, patterns):
    width = patterns.shape[-1]
    pick = np.zeros((width, width))
    pick[np.arange(width), np.concatenate([np.arange(0, width, 2), np.arange(1, width, 2)])] = 1
    pick = jnp.asarray(np.stack([pick, pick.T, pick.T]).astype(ml_dtypes.bfloat16))
    block = pl.BlockSpec((1, width, width), lambda i: (i, 0, 0))
    return pl.pallas_call(
        functools.partial(amplitude_body, axes),
        grid=(patterns.shape[0],),
        out_shape=jax.ShapeDtypeStruct(patterns.shape, F32),
        in_specs=[SMEM, SMEM, SMEM, block, VMEM],
        out_specs=block,
        compiler_params=ROOM,
        cost_estimate=costs(10**11),
    )(*scalars, patterns, pick)


def merge_body(tx, on_ends, off_ends, left, right, quarters, mid, on, off, sides, sem):
    rim = left.shape[-1]
    width = 2 * rim
    below = left.shape[2] - rim
    odd = tx[0] % 2
    on_rows, off_rows = rows_at((1 - odd) * below, rim), rows_at(odd * below, rim)
    wait_all(run_all([
        (on_ends, on.at[:, :, :, :width]),
        (quarters, on.at[:, :, :, width : 3 * width]),
        (mid, on.at[:, :, :, 3 * width :]),
        (off_ends, off),
        (left.at[:, :, on_rows], sides.at[0, :, :, :, :rim]),
        (right.at[:, :, on_rows], sides.at[0, :, :, :, rim:]),
        (left.at[:, :, off_rows], sides.at[1, :, :, :, :rim]),
        (right.at[:, :, off_rows], sides.at[1, :, :, :, rim:]),
    ], sem))
    on[:, :, :, :width] += sides[0]
    off[...] += sides[1]


def merged(tx, on_ends, off_ends, left, right, quarters, mid):
    slices, _, rim, width = on_ends.shape
    cols = width + quarters.shape[3] + mid.shape[3]
    return pl.pallas_call(
        merge_body,
        out_shape=(shape(slices, 2, rim, cols), jax.ShapeDtypeStruct(off_ends.shape, F32)),
        in_specs=[SMEM] + [HBM] * 6,
        out_specs=(VMEM, VMEM),
        scratch_shapes=[pltpu.VMEM((2,) + on_ends.shape, F32), pltpu.SemaphoreType.DMA((8,))],
        compiler_params=ROOM,
        cost_estimate=costs(10**11),
    )(tx, on_ends, off_ends, left, right, quarters, mid)


def halves_body(tx, x, mine, other):
    half = mine.shape[0]
    bit = tx[0] % 2
    mine[...] = x[rows_at(bit * half, half)]
    other[...] = x[rows_at((1 - bit) * half, half)]


def halves_of(tx, x):
    half = shape(x.shape[0] // 2, x.shape[1])
    return pl.pallas_call(
        halves_body,
        out_shape=(half, half),
        in_specs=[SMEM, VMEM],
        out_specs=(VMEM, VMEM),
        compiler_params=ROOM,
        cost_estimate=costs(10**11),
    )(tx, x)


def scaled_body(counts, *refs):
    parts, out = refs[:-1], refs[-1]
    positions = lax.fori_loop(0, counts.shape[0], lambda i, n: n + counts[i], jnp.zeros((), jnp.int32))
    total = parts[0][...]
    for part in parts[1:]:
        total += part[...]
    out[...] = total / jnp.sqrt(jnp.full(out.shape, jnp.maximum(positions, 1).astype(F32)))


def scaled_sum(counts, parts):
    return pl.pallas_call(
        scaled_body,
        out_shape=jax.ShapeDtypeStruct(parts[0].shape, F32),
        in_specs=[SMEM] + [VMEM] * len(parts),
        out_specs=VMEM,
        compiler_params=ROOM,
        cost_estimate=costs(10**8),
    )(counts, *parts)


def total_body(tx, ends, quarters, mid, left, right, on, off_quarters, off_ends, off_mid, out):
    rim = left.shape[-1]
    rows, cols = out.shape[2:]
    width = 2 * rim
    one, five = slice(0, rim), slice(cols - rim, cols)
    two, four = slice(rim, rim + width), slice(cols - rim - width, cols - rim)
    three = slice(rim + width, cols - rim - width)
    odd = tx[0] % 2
    out[0, 0, :, one] = ends[0, 0, :, :rim] + left[0, 0, rim : rim + rows]
    out[0, 0, :, five] = ends[0, 0, :, rim:] + right[0, 0, rim : rim + rows]
    out[0, 0, :, two] = quarters[0, 0, :, :width]
    out[0, 0, :, four] = quarters[0, 0, :, width:]
    out[0, 0, :, three] = mid[0, 0]
    here = rows_at((1 - odd) * (rows - rim), rim)
    out[0, 0, here, one] += on[0, 0, :, :rim]
    out[0, 0, here, five] += on[0, 0, :, rim:width]
    out[0, 0, here, two] += on[0, 0, :, width : 2 * width]
    out[0, 0, here, four] += on[0, 0, :, 2 * width : 3 * width]
    out[0, 0, here, three] += on[0, 0, :, 3 * width :]
    here = rows_at(odd * (rows - rim), rim)
    out[0, 0, here, one] += off_ends[0, 0, :, :rim]
    out[0, 0, here, five] += off_ends[0, 0, :, rim:]
    out[0, 0, here, two] += off_quarters[0, 0, :, :width]
    out[0, 0, here, four] += off_quarters[0, 0, :, width:]
    out[0, 0, here, three] += off_mid[0, 0]


def total_of(tx, parts, tile_shape):
    def block(dims):
        return pl.BlockSpec((1, 1) + tuple(dims[2:]), lambda i, j: (i, j, 0, 0))

    return pl.pallas_call(
        total_body,
        grid=tile_shape[:2],
        out_shape=jax.ShapeDtypeStruct(tile_shape, F32),
        in_specs=[SMEM] + [block(x.shape) for x in parts],
        out_specs=block(tile_shape),
        compiler_params=ROOM,
        cost_estimate=costs(10**11),
    )(tx, *parts)


def along(x, step):
    count = lax.axis_size("ty")
    return lax.ppermute(x, "ty", [(i, i + step) for i in range(count) if 0 <= i + step < count])


def across(x, first, skip=None):
    pairs = []
    for i in range(first, lax.axis_size("tx") - 1, 2):
        if i != skip:
            pairs += [(i, i + 1), (i + 1, i)]
    return lax.ppermute(x, "tx", pairs)


def relay_out(x):
    count = lax.axis_size("tx")
    return lax.ppermute(x, "tx", [(count // 2 - 1, count - 1), (count // 2, 0)])


def relay_in(x):
    count = lax.axis_size("tx")
    return lax.ppermute(x, "tx", [(count - 1, count // 2), (0, count // 2 - 1)])


def after(x, *others):
    return lax.optimization_barrier((x,) + others)[0]


def halved(flat, apart):
    bit = (lax.axis_index("tx") // apart) % 2
    half = flat.shape[0] // 2
    pairs = [(i, i ^ apart) for i in range(lax.axis_size("tx"))]
    mine = lax.dynamic_slice_in_dim(flat, bit * half, half, 0)
    other = lax.dynamic_slice_in_dim(flat, (1 - bit) * half, half, 0)
    return mine + lax.ppermute(other, "tx", pairs)


def joined_body(apart, tx, *refs):
    pieces, out = refs[:-1], refs[-1]
    rows = out.shape[0] // len(pieces)
    mine = sum(((tx[0] // step) % 2) * 2**k for k, step in enumerate(apart))
    for i, piece in enumerate(pieces):
        out[rows_at((mine ^ i) * rows, rows)] = piece[...]


def spread(flat, apart, count):
    pieces = [flat]
    for i in range(1, 2 ** len(apart)):
        flip = sum(step for k, step in enumerate(apart) if i >> k & 1)
        pieces.append(lax.ppermute(flat, "tx", [(j, j ^ flip) for j in range(count)]))
    return pieces


def joined(tx, pieces, apart):
    rows, cols = pieces[0].shape
    return pl.pallas_call(
        functools.partial(joined_body, apart),
        out_shape=shape(rows * len(pieces), cols),
        in_specs=[SMEM] + [VMEM] * len(pieces),
        out_specs=VMEM,
        compiler_params=ROOM,
        cost_estimate=costs(10**8),
    )(tx, *pieces)


def per_device(object_slab, probe, patterns, centers, counts):
    slices, _, tile_rows, tile_cols = object_slab.shape
    width = probe.shape[-1]
    rim = width // 2
    axes = lax.axis_size("tx"), lax.axis_size("ty")
    middle = axes[0] // 2
    tx, ty = (lax.axis_index(axis).astype(jnp.int32).reshape(1) for axis in ("tx", "ty"))
    full = tile_rows + width
    mid_cols = tile_cols - 3 * width
    ends_shape = shape(slices, 2, rim, width)
    quarters_shape = shape(slices, 2, rim, 2 * width)
    mid_shape = shape(slices, 2, rim, mid_cols)
    side_shape = shape(slices, 2, full, rim)
    tile = object_slab

    column_shape = shape(slices, 2, tile_rows, rim)
    to_left, to_right, quarters, mid = copies_call(
        pack_body, (tx,), (tile,), (column_shape, column_shape, quarters_shape, mid_shape), 10**8
    )
    carried = relay_out(quarters)
    left, right = along(to_right, 1), along(to_left, -1)
    off_quarters = across(quarters, 1, middle - 1)
    off_mid = across(mid, 1)
    amplitudes = amplitudes_of(axes, (tx, ty, counts), after(patterns, to_left))
    on_shape = shape(slices, 2, rim, tile_cols + width)

    def strips(tile, left, right):
        on, ends = copies_call(strips_body, (tx,), (tile, left, right), (on_shape, quarters_shape), 10**8)
        return across(on, 0), ends

    def nothing(tile, left, right):
        return jnp.zeros(on_shape.shape, F32), jnp.zeros(quarters_shape.shape, F32)

    relayed = relay_in(carried)
    on, ends = lax.cond(counts[0] >= 0, strips, nothing, after(tile, amplitudes, carried), left, right)
    off_ends = across(ends, 1)

    scalars = (tx, ty, centers, counts)
    g_quarters, g_tile_mid, g_on_mid, g_off_mid, g_probe = field_call(
        inner_body, axes, 3, scalars, (tile, on, off_quarters, relayed, off_mid), amplitudes, probe,
        (shape(2, slices, 2, full, width), shape(slices, 2, tile_rows, mid_cols), mid_shape, mid_shape), tile_rows,
    )
    back_mid = across(g_off_mid, 1)
    g_tile_ends, g_tile_quarters, g_on_ends, g_on_quarters, g_off_ends, g_off_quarters, g_left, g_right, g_probe = field_call(
        outer_body, axes, 4, scalars, (tile, on, off_quarters, relayed, off_ends, left, right, g_quarters, g_probe), amplitudes, probe,
        (
            shape(slices, 2, tile_rows, width), shape(slices, 2, tile_rows, 2 * width), ends_shape, quarters_shape,
            ends_shape, quarters_shape, side_shape, side_shape,
        ),
        tile_rows,
    )
    from_left = along(g_right, 1)
    from_right = along(g_left, -1)
    back_quarters = across(g_off_quarters, 1)

    apart = [2**k for k in range(1, axes[0].bit_length() - 1)]
    mine, other = halves_of(tx, after(g_probe.reshape(-1, width), back_mid))
    flat = mine + lax.ppermute(other, "tx", [(i, i ^ 1) for i in range(axes[0])])
    for step in reversed(apart):
        flat = halved(flat, step)
    on_all, off_ends = merged(tx, after(g_on_ends, back_quarters, flat), g_off_ends, from_left, from_right, g_on_quarters, g_on_mid)
    back_ends = across(off_ends, 1)
    back_on = across(on_all, 0)
    flat = after(flat, on_all)
    others = [lax.ppermute(flat, "ty", [(i, (i + step) % axes[1]) for i in range(axes[1])]) for step in range(1, axes[1])]
    flat = after(scaled_sum(counts, (flat, *others)), back_ends, back_on)
    inner = total_of(
        tx,
        (g_tile_ends, g_tile_quarters, g_tile_mid, from_left, from_right, back_on, back_quarters, back_ends, back_mid),
        tile.shape,
    )
    pieces = spread(flat, apart[:2], axes[0])
    pieces = after(pieces[0], inner), *pieces[1:]
    while apart:
        flat = joined(tx, pieces, apart[:2])
        apart = apart[2:]
        pieces = spread(flat, apart[:2] or [1], axes[0])
    probe_sum = joined(tx, pieces, [1]).reshape(probe.shape)
    return (inner, probe_sum)


def solution(mesh):
    placed = (
        P(None, None, "tx", "ty"),
        P(),
        P(("tx", "ty"), None, None),
        P(("tx", "ty"), None),
        P(),
    )
    return jax.shard_map(
        per_device,
        mesh=mesh,
        in_specs=placed,
        out_specs=(P(None, None, "tx", "ty"), P()),
        check_vma=False,
    )
```

time: 304 us -> 172 us (0.57)
  local copies, waits for them, and re-layouts: 75.7 us -> 4.26 us
  Pallas kernels: 10.4 us -> 75 us
  waiting for transfers between devices: 96 us -> 32.3 us
  starting transfers between devices: 97.5 us -> 57.6 us
  other arithmetic: 20.5 us -> 1.01 us
    pallas_call x1 -> x11, Pallas kernels: 10.4 us -> 75 us  [the longest x2 44 us: field_call(): pl.pallas_call(functools.partial(body, axes), out_shape=tuple(outs) + (ja...]
    ppermute x20 -> x24, waiting for transfers between devices: 96 us -> 32.3 us  [the longest x2 13.3 us: halved(): return mine + lax.ppermute(other, 'tx', pairs)]
    ppermute x20 -> x24, starting transfers between devices: 97.5 us -> 57.6 us  [the longest x8 27.6 us: across(): return lax.ppermute(x, 'tx', pairs)]
    transpose x1 -> x0, local copies, waits for them, and re-layouts: 36.3 us -> none  [per_device(): jnp.sqrt(patterns).reshape(slots, rim, 2, rim, 2).transpose(0, 2, 1, 4, 3)]
    sqrt x2 -> x0, local copies, waits for them, and re-layouts: 21 us -> none  [per_device(): jnp.sqrt(patterns).reshape(slots, rim, 2, rim, 2).transpose(0, 2, 1, 4, 3)]
    scatter-add x6 -> x0, other arithmetic: 15.5 us -> none  [the longest x2 4.13 us: edges(): return x.at[:, :, :, tile_cols - rim:].add(from_right[:, :, first:last])]
    slice x3 -> x0, local copies, waits for them, and re-layouts: 5.91 us -> none  [the longest x1 2.54 us: per_device(): bottom = send(object_slab[:, :, :rim], 'tx', -1)]
    reshape x1 -> x0, local copies, waits for them, and re-layouts: 3.95 us -> none  [per_device(): jnp.sqrt(patterns).reshape(slots, rim, 2, rim, 2).transpose(0, 2, 1, 4, 3)]
  transfers between devices with their start and end apart: 20 -> 24, of which waited for: 11 -> 9; matrix products, arithmetic and copies ran while one was open for 26% -> 1% of each run, Pallas kernels for 0% -> 36%
where the time goes in v2:
time: 172 us; the launch traced here: 171 us
  Pallas kernels  75 us (44%)
  starting transfers between devices  57.6 us (33%)
  waiting for transfers between devices  32.3 us (19%)
  local copies, waits for them, and re-layouts  4.26 us (2%)
    pallas_call x2, Pallas kernels, field_call(): pl.pallas_call(functools.partial(body, axes), out_shape=tuple(outs) + (ja...  44 us
    ppermute x8, starting transfers between devices, across(): return lax.ppermute(x, 'tx', pairs)  27.6 us
    ppermute x4, starting transfers between devices, along(): lax.ppermute(x, 'ty', [(i, i + step) for i in range(count) if 0 <= i + st...  19.8 us
    ppermute x2, waiting for transfers between devices, halved(): return mine + lax.ppermute(other, 'tx', pairs)  13.3 us
    ppermute x8, waiting for transfers between devices, across(): return lax.ppermute(x, 'tx', pairs)  10.3 us
    pallas_call x1, Pallas kernels, amplitudes_of(): pl.pallas_call(functools.partial(amplitude_body, axes), grid=(patterns.sh...  7.08 us
    pallas_call x2, Pallas kernels, copies_call(): pl.pallas_call(body, out_shape=tuple(outs), in_specs=[SMEM] * len(scalars...  6.56 us
    pallas_call x1, Pallas kernels, total_of(): pl.pallas_call(total_body, grid=tile_shape[:2], out_shape=jax.ShapeDtypeS...  6.41 us
  transfers between devices with their start and end apart: 24, of which 9 were waited for; matrix products, arithmetic and copies ran while one was open for 1% of the time, Pallas kernels for 36%

profile of v2, /device:TPU:1, one launch (start us, length us, event | category | flops | bytes accessed | tf_op | source)
XLA Modules:
  0.0 171.4 jit_solution(12666030075726385270)
XLA Ops:
  0.6 3.3 %shard_map.95 = (f32[2,2,256,128]{3,2,1,0:T(8,128)}, f32[2,2,256,128]{3,2,1,0:T(8,128)}, f32[2,2,128,512]{3,2,1,0:T(8,128)}, f32[2,2,128,256]{3,2,1,0:T(8,128)}) custom-call(s32[1]{0:T(128)} %bitcast.tx, f32[2,2,256,1024]{3,2,1,0:T(8,128)} %tile.5), custom_call_target="tpu_custom_call" | custom-call | flops 100000000 | bytes 10000000 | tf_op jit(solution)/shard_map/pallas_call | solution.py:375
  3.9 1.7 collective-permute-start.1
  5.6 4.5 %collective-permute-start.4 = (f32[2,2,128,512]{3,2,1,0:T(8,128)}, f32[2,2,128,512]{3,2,1,0:T(8,128)S(1)}, u32[]{:S(2)}, u32[]{:S(2)}) collective-permute-start(f32[2,2,128,512]{3,2,1,0:T(8,128)} %get-tuple-element.49), channel_id=1, source_target_pairs={{4,8},{8,4},{20,24},{24,20},{5,9},{9,5},{21,25},{25,21},{6,10},{10... | collective-permute-start | bytes 3145736 | tf_op jit(solution)/shard_map/ppermute | solution.py:539
  10.1 1.3 collective-permute-start.3
  11.4 4.0 %collective-permute-start.2 = (f32[2,2,256,128]{3,2,1,0:T(8,128)}, f32[2,2,256,128]{3,2,1,0:T(8,128)S(1)}, u32[]{:S(2)}, u32[]{:S(2)}) collective-permute-start(f32[2,2,256,128]{3,2,1,0:T(8,128)} %get-tuple-element.51), channel_id=1, source_target_pairs={{0,1},{1,2},{2,3},{4,5},{5,6},{6,7},{8,9},{9,10},{10,11},{12,13},{... | collective-permute-start | bytes 1572872 | tf_op jit(solution)/shard_map/ppermute | solution.py:531
  15.4 2.5 %collective-permute-start.7 = (f32[2,2,128,256]{3,2,1,0:T(8,128)}, f32[2,2,128,256]{3,2,1,0:T(8,128)}, u32[]{:S(2)}, u32[]{:S(2)}) collective-permute-start(f32[2,2,128,256]{3,2,1,0:T(8,128)} %get-tuple-element.54), channel_id=1, source_target_pairs={{4,8},{8,4},{12,16},{16,12},{20,24},{24,20},{5,9},{9,5},{13,17},{1... | collective-permute-start | bytes 1572872 | tf_op jit(solution)/shard_map/ppermute | solution.py:539
  17.9 1.6 collective-permute-start.5
  19.6 7.1 %shard_map.96.amplitudes = f32[8,256,256]{2,1,0:T(8,128)} custom-call(s32[1]{0:T(128)} %bitcast.tx, s32[1]{0:T(128)} %bitcast.1.ty, s32[32]{0:T(128)} %counts.7, f32[8,256,256]{2,1,0:T(8,128)} %patterns, bf16[3,256,256]{2,1,0:T(8,128)(2,1)} %constant.64.clone.pick), custom_call_target="tpu_custom_call" | custom-call | flops 99999997952 | bytes 10000000 | tf_op jit(solution)/shard_map/pallas_call | solution.py:403
  26.7 0.7 copy.11.centers
  27.4 11.8 %conditional.1 = (f32[2,2,128,1280]{3,2,1,0:T(8,128)}, f32[2,2,128,512]{3,2,1,0:T(8,128)S(1)}) conditional(s32[]{:T(128)} %bitcast.2, () %tuple.23, (s32[1]{0:T(128)}, f32[2,2,256,1024]{3,2,1,0:T(8,128)}, f32[2,2,256,128]{3,2,1,0:T(8,128)S(1)}, f32[2,2,256,128]{3,2,1,0:T(8,128)S(1)}) %tuple.26), branch_computations={%region_0.0_spmd, %region_1.0_spmd} | conditional | flops 100000000 | bytes 20485816 | solution.py:627
  27.4 3.3 %branch_1_fun.1 = (f32[2,2,128,1280]{3,2,1,0:T(8,128)}, f32[2,2,128,512]{3,2,1,0:T(8,128)S(1)}) custom-call(s32[1]{0:T(128)} %get-tuple-element.8.tx, f32[2,2,256,1024]{3,2,1,0:T(8,128)} %get-tuple-element.9.tile, f32[2,2,256,128]{3,2,1,0:T(8,128)S(1)} %get-tuple-element.10.left, f32[2,2,256,128]{3,2,1,0:T(8,128)S(1)} %get-tuple-element.11.right), custom_call_target="tpu_custom_call" | custom-call | flops 100000000 | bytes 10000000 | tf_op jit(solution)/shard_map/cond/branch_1_fun/pallas_call | solution.py:375
  30.6 3.7 %collective-permute-start = (f32[2,2,128,1280]{3,2,1,0:T(8,128)}, f32[2,2,128,1280]{3,2,1,0:T(8,128)}, u32[]{:S(2)}, u32[]{:S(2)}) collective-permute-start(f32[2,2,128,1280]{3,2,1,0:T(8,128)} %get-tuple-element.12), channel_id=1, source_target_pairs={{0,4},{4,0},{8,12},{12,8},{16,20},{20,16},{24,28},{28,24},{1,5},{5... | collective-permute-start | bytes 7864328 | tf_op jit(solution)/shard_map/cond/branch_1_fun/ppermute | solution.py:539
  34.3 4.9 %collective-permute-done = f32[2,2,128,1280]{3,2,1,0:T(8,128)} collective-permute-done((f32[2,2,128,1280]{3,2,1,0:T(8,128)}, f32[2,2,128,1280]{3,2,1,0:T(8,128)}, u32[]{:S(2)}, u32[]{:S(2)}) %collective-permute-start) | collective-permute-done | bytes 2621472 | tf_op jit(solution)/shard_map/cond/branch_1_fun/ppermute | solution.py:539
  39.2 1.9 %collective-permute-start.6 = (f32[2,2,128,512]{3,2,1,0:T(8,128)S(1)}, f32[2,2,128,512]{3,2,1,0:T(8,128)}, u32[]{:S(2)}, u32[]{:S(2)}) collective-permute-start(f32[2,2,128,512]{3,2,1,0:T(8,128)S(1)} %get-tuple-element.53), channel_id=1, source_target_pairs={{4,8},{8,4},{12,16},{16,12},{20,24},{24,20},{5,9},{9,5},{13,17},{1... | collective-permute-start | bytes 3145736 | tf_op jit(solution)/shard_map/ppermute | solution.py:539
  41.2 1.0 copy-done.8
  42.1 20.2 %shard_map.97 = (f32[2,2,2,512,256]{4,3,2,1,0:T(8,128)}, f32[2,2,256,256]{3,2,1,0:T(8,128)}, f32[2,2,128,256]{3,2,1,0:T(8,128)}, f32[2,2,128,256]{3,2,1,0:T(8,128)}, f32[2,256,256]{2,1,0:T(8,128)}) custom-call(s32[1]{0:T(128)} %bitcast.tx, s32[1]{0:T(128)} %bitcast.1.ty, s32[8,2]{1,0:T(8,128)} %copy.11.centers, s32[32]{0:T(128)} %counts.7, ...), custom_call_target="tpu_custom_call" | custom-call | flops 20000000000 | bytes 10000000 | tf_op jit(solution)/shard_map/pallas_call | solution.py:321
  62.3 1.9 %collective-permute-start.11 = (f32[2,2,128,256]{3,2,1,0:T(8,128)}, f32[2,2,128,256]{3,2,1,0:T(8,128)S(1)}, u32[]{:S(2)}, u32[]{:S(2)}) collective-permute-start(f32[2,2,128,256]{3,2,1,0:T(8,128)} %get-tuple-element.65), channel_id=1, source_target_pairs={{4,8},{8,4},{12,16},{16,12},{20,24},{24,20},{5,9},{9,5},{13,17},{1... | collective-permute-start | bytes 1572872 | tf_op jit(solution)/shard_map/ppermute | solution.py:539
  64.2 1.0 collective-permute-done.6.off_ends
  65.2 23.9 %shard_map.98 = (f32[2,2,256,256]{3,2,1,0:T(8,128)}, f32[2,2,256,512]{3,2,1,0:T(8,128)}, f32[2,2,128,256]{3,2,1,0:T(8,128)}, f32[2,2,128,512]{3,2,1,0:T(8,128)},...) custom-call(s32[1]{0:T(128)} %bitcast.tx, ...), custom_call_target="tpu_custom_call" | custom-call | flops 20000000000 | bytes 10000000 | tf_op jit(solution)/shard_map/pallas_call | solution.py:321
  89.1 2.0 %shard_map.99 = (f32[256,256]{1,0:T(8,128)}, f32[256,256]{1,0:T(8,128)}) custom-call(s32[1]{0:T(128)} %bitcast.tx, f32[512,256]{1,0:T(8,128)} %bitcast.8), custom_call_target="tpu_custom_call" | custom-call | flops 99999997952 | bytes 10000000 | tf_op jit(solution)/shard_map/pallas_call | solution.py:457
  91.2 4.3 %collective-permute-start.10 = (f32[2,2,128,512]{3,2,1,0:T(8,128)}, f32[2,2,128,512]{3,2,1,0:T(8,128)S(1)}, u32[]{:S(2)}, u32[]{:S(2)}) collective-permute-start(f32[2,2,128,512]{3,2,1,0:T(8,128)} %get-tuple-element.63), channel_id=1, source_target_pairs={{4,8},{8,4},{12,16},{16,12},{20,24},{24,20},{5,9},{9,5},{13,17},{1... | collective-permute-start | bytes 3145736 | tf_op jit(solution)/shard_map/ppermute | solution.py:539
  95.5 13.2 %collective-permute-start.8 = (f32[2,2,512,128]{3,2,1,0:T(8,128)}, f32[2,2,512,128]{3,2,1,0:T(8,128)}, u32[]{:S(2)}, u32[]{:S(2)}) collective-permute-start(f32[2,2,512,128]{3,2,1,0:T(8,128)} %get-tuple-element.60), channel_id=1, source_target_pairs={{0,1},{1,2},{2,3},{4,5},{5,6},{6,7},{8,9},{9,10},{10,11},{12,13},{... | collective-permute-start | bytes 3145736 | tf_op jit(solution)/shard_map/ppermute | solution.py:531
  108.7 1.3 collective-permute-start.9
  110.0 1.0 add.30
  111.0 0.1 collective-permute-start.13
  111.2 10.2 %collective-permute-done.13 = f32[128,256]{1,0:T(8,128)S(1)} collective-permute-done((f32[128,256]{1,0:T(8,128)S(1)}, f32[128,256]{1,0:T(8,128)S(1)}, u32[]{:S(2)}, u32[]{:S(2)}) %collective-permute-start.13) | collective-permute-done | bytes 131104 | tf_op jit(solution)/shard_map/ppermute | solution.py:562
  121.4 0.1 collective-permute-start.14
  121.5 3.1 %collective-permute-done.14 = f32[64,256]{1,0:T(8,128)S(1)} collective-permute-done((f32[64,256]{1,0:T(8,128)S(1)}, f32[64,256]{1,0:T(8,128)S(1)}, u32[]{:S(2)}, u32[]{:S(2)}) %collective-permute-start.14) | collective-permute-done | bytes 65568 | tf_op jit(solution)/shard_map/ppermute | solution.py:562
  124.7 5.0 %collective-permute-done.9.right = f32[2,2,512,128]{3,2,1,0:T(8,128)} collective-permute-done((f32[2,2,512,128]{3,2,1,0:T(8,128)}, f32[2,2,512,128]{3,2,1,0:T(8,128)}, u32[]{:S(2)}, u32[]{:S(2)}) %collective-permute-start.9) | collective-permute-done | bytes 1048608 | tf_op jit(solution)/shard_map/ppermute | solution.py:531
  129.6 3.6 %shard_map.100 = (f32[2,2,128,1024]{3,2,1,0:T(8,128)}, f32[2,2,128,256]{3,2,1,0:T(8,128)}) custom-call(s32[1]{0:T(128)} %bitcast.tx, f32[2,2,128,256]{3,2,1,0:T(8,128)} %get-tuple-element.69.on_ends, f32[2,2,128,256]{3,2,1,0:T(8,128)} %get-tuple-element.70.off_ends, f32[2,2,512,128]{3,2,1,0:T(8,128)} %collective-permute-done.8.left, ...), custom_call_target="tpu_custom_call" | custom-call | flops 99999997952 | bytes 10000000 | tf_op jit(solution)/shard_map/pallas_call | solution.py:437
  133.3 0.1 collective-permute-start.15
  133.4 8.7 %collective-permute-start.16 = (f32[2,2,128,256]{3,2,1,0:T(8,128)}, f32[2,2,128,256]{3,2,1,0:T(8,128)S(1)}, u32[]{:S(2)}, u32[]{:S(2)}) collective-permute-start(f32[2,2,128,256]{3,2,1,0:T(8,128)} %get-tuple-element.74), channel_id=1, source_target_pairs={{4,8},{8,4},{12,16},{16,12},{20,24},{24,20},{5,9},{9,5},{13,17},{1... | collective-permute-start | bytes 1572872 | tf_op jit(solution)/shard_map/ppermute | solution.py:539
  142.2 0.1 collective-permute-start.18
  142.2 3.2 %collective-permute-start.19 = (f32[64,256]{1,0:T(8,128)S(1)}, f32[64,256]{1,0:T(8,128)S(1)}, u32[]{:S(2)}, u32[]{:S(2)}) collective-permute-start(f32[64,256]{1,0:T(8,128)S(1)} %dynamic-slice_add_fusion.1.refs_0_), channel_id=1, source_target_pairs={{0,3},{1,0},{2,1},{3,2},{4,7},{5,4},{6,5},{7,6},{8,11},{9,8},{10,9... | collective-permute-start | bytes 196616 | tf_op jit(solution)/shard_map/ppermute | solution.py:657
  145.4 1.7 collective-permute-done.17.refs_1_
  147.1 0.7 collective-permute-done.19.refs_3_
  147.8 0.6 copy-done.13
  148.4 1.8 %shard_map.102.refs_0_ = f32[64,256]{1,0:T(8,128)} custom-call(s32[32]{0:T(128)} %counts.7, f32[64,256]{1,0:T(8,128)} %copy-done.1, f32[64,256]{1,0:T(8,128)} %copy-done.11, f32[64,256]{1,0:T(8,128)} %copy-done.12, f32[64,256]{1,0:T(8,128)} %copy-done.13), custom_call_target="tpu_custom_call" | custom-call | flops 100000000 | bytes 10000000 | tf_op jit(solution)/shard_map/pallas_call | solution.py:477
  150.2 4.4 %collective-permute-done.16.off_ends = f32[2,2,128,256]{3,2,1,0:T(8,128)S(1)} collective-permute-done((f32[2,2,128,256]{3,2,1,0:T(8,128)}, f32[2,2,128,256]{3,2,1,0:T(8,128)S(1)}, u32[]{:S(2)}, u32[]{:S(2)}) %collective-permute-start.16) | collective-permute-done | bytes 524320 | tf_op jit(solution)/shard_map/ppermute | solution.py:539
  154.7 2.6 %collective-permute-start.22 = (f32[64,256]{1,0:T(8,128)}, f32[64,256]{1,0:T(8,128)S(1)}, u32[]{:S(2)}, u32[]{:S(2)}) collective-permute-start(f32[64,256]{1,0:T(8,128)} %shard_map.102.refs_0_), channel_id=1, source_target_pairs={{0,24},{4,28},{8,16},{12,20},{16,8},{20,12},{24,0},{28,4},{1,25},{... | collective-permute-start | bytes 196616 | tf_op jit(solution)/shard_map/ppermute | solution.py:577
  157.3 6.4 %shard_map.101 = f32[2,2,256,1024]{3,2,1,0:T(8,128)} custom-call(s32[1]{0:T(128)} %bitcast.tx, f32[2,2,256,256]{3,2,1,0:T(8,128)} %get-tuple-element.57.ends, f32[2,2,256,512]{3,2,1,0:T(8,128)} %get-tuple-element.58.quarters, f32[2,2,256,256]{3,2,1,0:T(8,128)} %get-tuple-element.59.mid, f32[2,2,512,128]{3,2,1,0:T(8,128)} %collective-permute-done.8.left, ...), custom_call_target="tpu_custom_call" | custom-call | flops 99999997952 | bytes 10000000 | tf_op jit(solution)/shard_map/pallas_call | solution.py:518
  163.7 0.6 copy-done.2
  164.3 0.6 copy-done.4
  165.0 1.7 shard_map.103.refs_0_
  166.6 0.8 collective-permute-start.23
  167.4 1.4 collective-permute-done.23.refs_1_
  168.8 0.7 copy-done
  169.5 1.9 %shard_map.104 = f32[512,256]{1,0:T(8,128)} custom-call(s32[1]{0:T(128)} %bitcast.tx, f32[256,256]{1,0:T(8,128)} %shard_map.103.refs_0_, f32[256,256]{1,0:T(8,128)} %copy-done), custom_call_target="tpu_custom_call" | custom-call | flops 100000000 | bytes 10000000 | tf_op jit(solution)/shard_map/pallas_call | solution.py:583
  (48 shorter events, 0.4 us)
Async XLA Ops:
  3.9 14.0 %collective-permute-start.1 = (f32[2,2,128,512]{3,2,1,0:T(8,128)}, f32[2,2,128,512]{3,2,1,0:T(8,128)}, u32[]{:S(2)}, u32[]{:S(2)}) collective-permute-start(f32[2,2,128,512]{3,2,1,0:T(8,128)} %get-tuple-element.49), channel_id=1, source_target_pairs={{12,28},{16,0},{13,29},{17,1},{14,30},{18,2},{15,31},{19,3}} | collective-permute-start | bytes 3145736 | tf_op jit(solution)/shard_map/ppermute | solution.py:544
  5.6 35.5 %collective-permute-start.4 = (f32[2,2,128,512]{3,2,1,0:T(8,128)}, f32[2,2,128,512]{3,2,1,0:T(8,128)S(1)}, u32[]{:S(2)}, u32[]{:S(2)}) collective-permute-start(f32[2,2,128,512]{3,2,1,0:T(8,128)} %get-tuple-element.49), channel_id=1, source_target_pairs={{4,8},{8,4},{20,24},{24,20},{5,9},{9,5},{21,25},{25,21},{6,10},{10... | collective-permute-start | bytes 3145736 | tf_op jit(solution)/shard_map/ppermute | solution.py:539
  10.1 17.3 %collective-permute-start.3 = (f32[2,2,256,128]{3,2,1,0:T(8,128)}, f32[2,2,256,128]{3,2,1,0:T(8,128)S(1)}, u32[]{:S(2)}, u32[]{:S(2)}) collective-permute-start(f32[2,2,256,128]{3,2,1,0:T(8,128)} %get-tuple-element.47), channel_id=1, source_target_pairs={{1,0},{2,1},{3,2},{5,4},{6,5},{7,6},{9,8},{10,9},{11,10},{13,12},{... | collective-permute-start | bytes 1572872 | tf_op jit(solution)/shard_map/ppermute | solution.py:531
  11.4 16.0 %collective-permute-start.2 = (f32[2,2,256,128]{3,2,1,0:T(8,128)}, f32[2,2,256,128]{3,2,1,0:T(8,128)S(1)}, u32[]{:S(2)}, u32[]{:S(2)}) collective-permute-start(f32[2,2,256,128]{3,2,1,0:T(8,128)} %get-tuple-element.51), channel_id=1, source_target_pairs={{0,1},{1,2},{2,3},{4,5},{5,6},{6,7},{8,9},{9,10},{10,11},{12,13},{... | collective-permute-start | bytes 1572872 | tf_op jit(solution)/shard_map/ppermute | solution.py:531
  15.4 25.7 %collective-permute-start.7 = (f32[2,2,128,256]{3,2,1,0:T(8,128)}, f32[2,2,128,256]{3,2,1,0:T(8,128)}, u32[]{:S(2)}, u32[]{:S(2)}) collective-permute-start(f32[2,2,128,256]{3,2,1,0:T(8,128)} %get-tuple-element.54), channel_id=1, source_target_pairs={{4,8},{8,4},{12,16},{16,12},{20,24},{24,20},{5,9},{9,5},{13,17},{1... | collective-permute-start | bytes 1572872 | tf_op jit(solution)/shard_map/ppermute | solution.py:539
  17.9 23.2 %collective-permute-start.5 = (f32[2,2,128,512]{3,2,1,0:T(8,128)}, f32[2,2,128,512]{3,2,1,0:T(8,128)}, u32[]{:S(2)}, u32[]{:S(2)}) collective-permute-start(f32[2,2,128,512]{3,2,1,0:T(8,128)} %collective-permute-done.1), channel_id=1, source_target_pairs={{28,16},{0,12},{29,17},{1,13},{30,18},{2,14},{31,19},{3,15}} | collective-permute-start | bytes 3145736 | tf_op jit(solution)/shard_map/ppermute | solution.py:549
  19.6 7.1 %copy-start.14 = (s32[32]{0:T(128)S(1)}, s32[32]{0:T(128)}, u32[]{:S(2)}) copy-start(s32[32]{0:T(128)} %counts.7) | copy-start | bytes 388
  19.6 7.1 %copy-start.5 = (s32[8,2]{0,1:T(2,128)S(1)}, s32[8,2]{0,1:T(2,128)}, u32[]{:S(2)}) copy-start(s32[8,2]{0,1:T(2,128)} %param.13) | copy-start | bytes 196
  30.6 8.6 %collective-permute-start = (f32[2,2,128,1280]{3,2,1,0:T(8,128)}, f32[2,2,128,1280]{3,2,1,0:T(8,128)}, u32[]{:S(2)}, u32[]{:S(2)}) collective-permute-start(f32[2,2,128,1280]{3,2,1,0:T(8,128)} %get-tuple-element.12), channel_id=1, source_target_pairs={{0,4},{4,0},{8,12},{12,8},{16,20},{20,16},{24,28},{28,24},{1,5},{5... | collective-permute-start | bytes 7864328 | tf_op jit(solution)/shard_map/cond/branch_1_fun/ppermute | solution.py:539
  39.2 26.0 %collective-permute-start.6 = (f32[2,2,128,512]{3,2,1,0:T(8,128)S(1)}, f32[2,2,128,512]{3,2,1,0:T(8,128)}, u32[]{:S(2)}, u32[]{:S(2)}) collective-permute-start(f32[2,2,128,512]{3,2,1,0:T(8,128)S(1)} %get-tuple-element.53), channel_id=1, source_target_pairs={{4,8},{8,4},{12,16},{16,12},{20,24},{24,20},{5,9},{9,5},{13,17},{1... | collective-permute-start | bytes 3145736 | tf_op jit(solution)/shard_map/ppermute | solution.py:539
  41.1 1.0 copy-start.8
  62.3 26.8 %collective-permute-start.11 = (f32[2,2,128,256]{3,2,1,0:T(8,128)}, f32[2,2,128,256]{3,2,1,0:T(8,128)S(1)}, u32[]{:S(2)}, u32[]{:S(2)}) collective-permute-start(f32[2,2,128,256]{3,2,1,0:T(8,128)} %get-tuple-element.65), channel_id=1, source_target_pairs={{4,8},{8,4},{12,16},{16,12},{20,24},{24,20},{5,9},{9,5},{13,17},{1... | collective-permute-start | bytes 1572872 | tf_op jit(solution)/shard_map/ppermute | solution.py:539
  89.1 2.1 %copy-start.9 = (f32[2,2,128,256]{3,2,1,0:T(8,128)}, f32[2,2,128,256]{3,2,1,0:T(8,128)S(1)}, u32[]{:S(2)}) copy-start(f32[2,2,128,256]{3,2,1,0:T(8,128)S(1)} %collective-permute-done.11.off_mid) | copy-start | bytes 1572868
  91.2 18.8 %collective-permute-start.12 = (f32[256,256]{1,0:T(8,128)}, f32[256,256]{1,0:T(8,128)S(1)}, u32[]{:S(2)}, u32[]{:S(2)}) collective-permute-start(f32[256,256]{1,0:T(8,128)} %get-tuple-element.68), channel_id=1, source_target_pairs={{0,4},{4,0},{8,12},{12,8},{16,20},{20,16},{24,28},{28,24},{1,5},{5... | collective-permute-start | bytes 786440 | tf_op jit(solution)/shard_map/ppermute | solution.py:650
  91.2 33.5 %collective-permute-start.10 = (f32[2,2,128,512]{3,2,1,0:T(8,128)}, f32[2,2,128,512]{3,2,1,0:T(8,128)S(1)}, u32[]{:S(2)}, u32[]{:S(2)}) collective-permute-start(f32[2,2,128,512]{3,2,1,0:T(8,128)} %get-tuple-element.63), channel_id=1, source_target_pairs={{4,8},{8,4},{12,16},{16,12},{20,24},{24,20},{5,9},{9,5},{13,17},{1... | collective-permute-start | bytes 3145736 | tf_op jit(solution)/shard_map/ppermute | solution.py:539
  95.5 29.2 %collective-permute-start.8 = (f32[2,2,512,128]{3,2,1,0:T(8,128)}, f32[2,2,512,128]{3,2,1,0:T(8,128)}, u32[]{:S(2)}, u32[]{:S(2)}) collective-permute-start(f32[2,2,512,128]{3,2,1,0:T(8,128)} %get-tuple-element.60), channel_id=1, source_target_pairs={{0,1},{1,2},{2,3},{4,5},{5,6},{6,7},{8,9},{9,10},{10,11},{12,13},{... | collective-permute-start | bytes 3145736 | tf_op jit(solution)/shard_map/ppermute | solution.py:531
  108.7 21.0 %collective-permute-start.9 = (f32[2,2,512,128]{3,2,1,0:T(8,128)}, f32[2,2,512,128]{3,2,1,0:T(8,128)}, u32[]{:S(2)}, u32[]{:S(2)}) collective-permute-start(f32[2,2,512,128]{3,2,1,0:T(8,128)} %get-tuple-element.61), channel_id=1, source_target_pairs={{1,0},{2,1},{3,2},{5,4},{6,5},{7,6},{9,8},{10,9},{11,10},{13,12},{... | collective-permute-start | bytes 3145736 | tf_op jit(solution)/shard_map/ppermute | solution.py:531
  111.0 10.4 %collective-permute-start.13 = (f32[128,256]{1,0:T(8,128)S(1)}, f32[128,256]{1,0:T(8,128)S(1)}, u32[]{:S(2)}, u32[]{:S(2)}) collective-permute-start(f32[128,256]{1,0:T(8,128)S(1)} %constant_dynamic-slice_fusion.1), channel_id=1, source_target_pairs={{0,16},{4,20},{8,24},{12,28},{16,0},{20,4},{24,8},{28,12},{1,17},{... | collective-permute-start | bytes 393224 | tf_op jit(solution)/shard_map/ppermute | solution.py:562
  121.4 3.2 %collective-permute-start.14 = (f32[64,256]{1,0:T(8,128)S(1)}, f32[64,256]{1,0:T(8,128)S(1)}, u32[]{:S(2)}, u32[]{:S(2)}) collective-permute-start(f32[64,256]{1,0:T(8,128)S(1)} %constant_dynamic-slice_fusion), channel_id=1, source_target_pairs={{0,8},{4,12},{8,0},{12,4},{16,24},{20,28},{24,16},{28,20},{1,9},{5... | collective-permute-start | bytes 196616 | tf_op jit(solution)/shard_map/ppermute | solution.py:562
  124.6 17.6 %copy-start.1 = (f32[64,256]{1,0:T(8,128)}, f32[64,256]{1,0:T(8,128)S(1)}, u32[]{:S(2)}) copy-start(f32[64,256]{1,0:T(8,128)S(1)} %dynamic-slice_add_fusion.1.refs_0_) | copy-start | bytes 196612
  124.7 8.6 %copy-start.7 = (f32[2,2,128,512]{3,2,1,0:T(8,128)}, f32[2,2,128,512]{3,2,1,0:T(8,128)S(1)}, u32[]{:S(2)}) copy-start(f32[2,2,128,512]{3,2,1,0:T(8,128)S(1)} %collective-permute-done.10.off_quarters) | copy-start | bytes 3145732
  133.3 21.3 %collective-permute-start.15 = (f32[2,2,128,1024]{3,2,1,0:T(8,128)}, f32[2,2,128,1024]{3,2,1,0:T(8,128)S(1)}, u32[]{:S(2)}, u32[]{:S(2)}) collective-permute-start(f32[2,2,128,1024]{3,2,1,0:T(8,128)} %get-tuple-element.73), channel_id=1, source_target_pairs={{0,4},{4,0},{8,12},{12,8},{16,20},{20,16},{24,28},{28,24},{1,5},{5... | collective-permute-start | bytes 6291464 | tf_op jit(solution)/shard_map/ppermute | solution.py:539
  133.4 21.2 %collective-permute-start.16 = (f32[2,2,128,256]{3,2,1,0:T(8,128)}, f32[2,2,128,256]{3,2,1,0:T(8,128)S(1)}, u32[]{:S(2)}, u32[]{:S(2)}) collective-permute-start(f32[2,2,128,256]{3,2,1,0:T(8,128)} %get-tuple-element.74), channel_id=1, source_target_pairs={{4,8},{8,4},{12,16},{16,12},{20,24},{24,20},{5,9},{9,5},{13,17},{1... | collective-permute-start | bytes 1572872 | tf_op jit(solution)/shard_map/ppermute | solution.py:539
  142.1 5.0 %collective-permute-start.17 = (f32[64,256]{1,0:T(8,128)S(1)}, f32[64,256]{1,0:T(8,128)S(1)}, u32[]{:S(2)}, u32[]{:S(2)}) collective-permute-start(f32[64,256]{1,0:T(8,128)S(1)} %dynamic-slice_add_fusion.1.refs_0_), channel_id=1, source_target_pairs={{0,1},{1,2},{2,3},{3,0},{4,5},{5,6},{6,7},{7,4},{8,9},{9,10},{10,1... | collective-permute-start | bytes 196616 | tf_op jit(solution)/shard_map/ppermute | solution.py:657
  142.2 4.9 %collective-permute-start.18 = (f32[64,256]{1,0:T(8,128)S(1)}, f32[64,256]{1,0:T(8,128)S(1)}, u32[]{:S(2)}, u32[]{:S(2)}) collective-permute-start(f32[64,256]{1,0:T(8,128)S(1)} %dynamic-slice_add_fusion.1.refs_0_), channel_id=1, source_target_pairs={{0,2},{1,3},{2,0},{3,1},{4,6},{5,7},{6,4},{7,5},{8,10},{9,11},{10,... | collective-permute-start | bytes 196616 | tf_op jit(solution)/shard_map/ppermute | solution.py:657
  142.2 5.5 %collective-permute-start.19 = (f32[64,256]{1,0:T(8,128)S(1)}, f32[64,256]{1,0:T(8,128)S(1)}, u32[]{:S(2)}, u32[]{:S(2)}) collective-permute-start(f32[64,256]{1,0:T(8,128)S(1)} %dynamic-slice_add_fusion.1.refs_0_), channel_id=1, source_target_pairs={{0,3},{1,0},{2,1},{3,2},{4,7},{5,4},{6,5},{7,6},{8,11},{9,8},{10,9... | collective-permute-start | bytes 196616 | tf_op jit(solution)/shard_map/ppermute | solution.py:657
  147.1 0.7 copy-start.11
  147.1 0.7 copy-start.12
  147.8 0.6 copy-start.13
  154.6 2.7 %copy-start.10 = (f32[2,2,128,256]{3,2,1,0:T(8,128)}, f32[2,2,128,256]{3,2,1,0:T(8,128)S(1)}, u32[]{:S(2)}) copy-start(f32[2,2,128,256]{3,2,1,0:T(8,128)S(1)} %collective-permute-done.16.off_ends) | copy-start | bytes 1572868
  154.6 2.7 %copy-start.6 = (f32[2,2,128,1024]{3,2,1,0:T(8,128)}, f32[2,2,128,1024]{3,2,1,0:T(8,128)S(1)}, u32[]{:S(2)}) copy-start(f32[2,2,128,1024]{3,2,1,0:T(8,128)S(1)} %collective-permute-done.15.on) | copy-start | bytes 6291460
  154.6 9.1 %collective-permute-start.20 = (f32[64,256]{1,0:T(8,128)}, f32[64,256]{1,0:T(8,128)S(1)}, u32[]{:S(2)}, u32[]{:S(2)}) collective-permute-start(f32[64,256]{1,0:T(8,128)} %shard_map.102.refs_0_), channel_id=1, source_target_pairs={{0,8},{4,12},{8,0},{12,4},{16,24},{20,28},{24,16},{28,20},{1,9},{5... | collective-permute-start | bytes 196616 | tf_op jit(solution)/shard_map/ppermute | solution.py:577
  154.6 9.1 %collective-permute-start.21 = (f32[64,256]{1,0:T(8,128)}, f32[64,256]{1,0:T(8,128)S(1)}, u32[]{:S(2)}, u32[]{:S(2)}) collective-permute-start(f32[64,256]{1,0:T(8,128)} %shard_map.102.refs_0_), channel_id=1, source_target_pairs={{0,16},{4,20},{8,24},{12,28},{16,0},{20,4},{24,8},{28,12},{1,17},{... | collective-permute-start | bytes 196616 | tf_op jit(solution)/shard_map/ppermute | solution.py:577
  154.7 9.0 %collective-permute-start.22 = (f32[64,256]{1,0:T(8,128)}, f32[64,256]{1,0:T(8,128)S(1)}, u32[]{:S(2)}, u32[]{:S(2)}) collective-permute-start(f32[64,256]{1,0:T(8,128)} %shard_map.102.refs_0_), channel_id=1, source_target_pairs={{0,24},{4,28},{8,16},{12,20},{16,8},{20,12},{24,0},{28,4},{1,25},{... | collective-permute-start | bytes 196616 | tf_op jit(solution)/shard_map/ppermute | solution.py:577
  163.7 0.6 copy-start.2
  163.7 0.6 copy-start.3
  164.3 0.6 copy-start.4
  166.6 2.1 %collective-permute-start.23 = (f32[256,256]{1,0:T(8,128)}, f32[256,256]{1,0:T(8,128)S(1)}, u32[]{:S(2)}, u32[]{:S(2)}) collective-permute-start(f32[256,256]{1,0:T(8,128)} %shard_map.103.refs_0_), channel_id=1, source_target_pairs={{0,4},{4,0},{8,12},{12,8},{16,20},{20,16},{24,28},{28,24},{1,5},{5... | collective-permute-start | bytes 786440 | tf_op jit(solution)/shard_map/ppermute | solution.py:577
  168.8 0.7 copy-start

commit v3 on v2

--- a/solution.py
+++ b/solution.py
@@ -94,44 +94,65 @@
     return a * c + b * d, a * d - b * c
 
 
-def visit(start, block, amplitude, probe, table, obj, acc, g_probe):
-    width = probe.shape[-1]
-    row, shift = start[0], start[1] % width
-    below = lax.broadcasted_iota(jnp.int32, (width, width), 0) < row
-    beside = lax.broadcasted_iota(jnp.int32, (width, width), 1) < shift
-
-    def cut(level, part):
-        upper = jnp.where(beside, obj[block + 1, level, part, :width], obj[block, level, part, :width])
-        lower = jnp.where(beside, obj[block + 1, level, part, width:], obj[block, level, part, width:])
-        return jnp.where(below, lower, upper)
-
-    def deposit(level, part, term):
-        zero = jnp.zeros_like(term)
-        upper = jnp.where(below, zero, term)
-        lower = jnp.where(below, term, zero)
-        acc[block, level, part, :width] += jnp.where(beside, zero, upper)
-        acc[block, level, part, width:] += jnp.where(beside, zero, lower)
-        acc[block + 1, level, part, :width] += jnp.where(beside, upper, zero)
-        acc[block + 1, level, part, width:] += jnp.where(beside, lower, zero)
-
-    def rolled(x, down, along):
-        return pltpu.roll(pltpu.roll(x, down, 0), along, 1)
-
-    u0 = rolled(probe[0], row, shift), rolled(probe[1], row, shift)
-    o0 = cut(0, 0), cut(0, 1)
-    u1 = transform(*times(*u0, *o0), PROP, table)
-    o1 = cut(1, 0), cut(1, 1)
-    far_re, far_im = transform(*times(*u1, *o1), FWD, table)
-    factor = 1.0 - amplitude() * lax.rsqrt(far_re * far_re + far_im * far_im + 1.0)
-    chi = transform(far_re * factor, far_im * factor, INV, table)
-    for part, term in enumerate(conj_times(*u1, *chi)):
-        deposit(1, part, term)
-    chi = transform(*conj_times(*o1, *chi), ADJ, table)
-    for part, term in enumerate(conj_times(*u0, *chi)):
-        deposit(0, part, term)
-    up, back = (width - row) % width, (width - shift) % width
-    for part, term in enumerate(conj_times(*o0, *chi)):
-        g_probe[part] += rolled(term, up, back)
+class Slot:
+    def __init__(self, start, block, amplitude, obj, acc):
+        width = obj.shape[-1]
+        self.width, self.block, self.amplitude, self.obj, self.acc = width, block, amplitude, obj, acc
+        self.row, self.shift = start[0], start[1] % width
+        self.below = lax.broadcasted_iota(jnp.int32, (width, width), 0) < self.row
+        self.beside = lax.broadcasted_iota(jnp.int32, (width, width), 1) < self.shift
+
+    def cut(self, level):
+        width, block, obj = self.width, self.block, self.obj
+
+        def part(k):
+            upper = jnp.where(self.beside, obj[block + 1, level, k, :width], obj[block, level, k, :width])
+            lower = jnp.where(self.beside, obj[block + 1, level, k, width:], obj[block, level, k, width:])
+            return jnp.where(self.below, lower, upper)
+
+        return part(0), part(1)
+
+    def deposit(self, level, terms):
+        width, block, acc = self.width, self.block, self.acc
+        for k, term in enumerate(terms):
+            zero = jnp.zeros_like(term)
+            upper = jnp.where(self.below, zero, term)
+            lower = jnp.where(self.below, term, zero)
+            acc[block, level, k, :width] += jnp.where(self.beside, zero, upper)
+            acc[block, level, k, width:] += jnp.where(self.beside, zero, lower)
+            acc[block + 1, level, k, :width] += jnp.where(self.beside, upper, zero)
+            acc[block + 1, level, k, width:] += jnp.where(self.beside, lower, zero)
+
+    def rolled(self, x):
+        return pltpu.roll(pltpu.roll(x, self.row, 0), self.shift, 1)
+
+    def rolled_back(self, x):
+        width = self.width
+        return pltpu.roll(pltpu.roll(x, (width - self.row) % width, 0), (width - self.shift) % width, 1)
+
+
+def visit(slots, probe, table, g_probe):
+    def transformed(fields, kind):
+        for axis in (1, 0):
+            fields = [one_side(*field, kind, axis, table) for field in fields]
+        return fields
+
+    u0 = [(slot.rolled(probe[0]), slot.rolled(probe[1])) for slot in slots]
+    o0 = [slot.cut(0) for slot in slots]
+    u1 = transformed([times(*u, *o) for u, o in zip(u0, o0)], PROP)
+    o1 = [slot.cut(1) for slot in slots]
+    far = transformed([times(*u, *o) for u, o in zip(u1, o1)], FWD)
+    factors = [1.0 - slot.amplitude() * lax.rsqrt(re * re + im * im + 1.0) for slot, (re, im) in zip(slots, far)]
+    chi = transformed([(re * factor, im * factor) for factor, (re, im) in zip(factors, far)], INV)
+    back = [conj_times(*o, *x) for o, x in zip(o1, chi)]
+    for slot, u, x in zip(slots, u1, chi):
+        slot.deposit(1, conj_times(*u, *x))
+    chi = transformed(back, ADJ)
+    for slot, u, x in zip(slots, u0, chi):
+        slot.deposit(0, conj_times(*u, *x))
+    for slot, o, x in zip(slots, o0, chi):
+        for part, term in enumerate(conj_times(*o, *x)):
+            g_probe[part] += slot.rolled_back(term)
 
 
 class Place:
@@ -171,56 +192,98 @@
         copy.wait()
 
 
-def start_chosen(flag, other, usual, pairs, sem, at):
-    for k, (lanes, target) in enumerate(pairs):
-        for here, source in ((flag, other), (jnp.logical_not(flag), usual)):
-            pl.when(here)(lambda s=source.at[:, :, :, lanes], t=target, i=at + k: pltpu.make_async_copy(s, t, sem.at[i]).start())
-    return [pltpu.make_async_copy(usual.at[:, :, :, lanes], target, sem.at[at + k]) for k, (lanes, target) in enumerate(pairs)]
-
-
-def two_groups(here, firsts, step, loads, stores, amplitudes, amps, amp_sem, sem, probe, table, obj, acc, g_probe):
+class Loads:
+    def __init__(self, pairs, sem, at):
+        self.pairs, self.sem, self.at = pairs, sem, at
+
+    def copies(self):
+        return [pltpu.make_async_copy(a, b, self.sem.at[self.at + i]) for i, (a, b) in enumerate(self.pairs)]
+
+    def start(self):
+        for copy in self.copies():
+            copy.start()
+
+    def wait(self):
+        wait_all(self.copies())
+
+
+class ChosenLoads(Loads):
+    def __init__(self, pairs, flag, other, sem, at):
+        super().__init__(pairs, sem, at)
+        self.flag, self.other = flag, other
+
+    def start(self):
+        copies = self.copies()
+        for copy in copies[:-1]:
+            copy.start()
+        place = self.sem.at[self.at + len(copies) - 1]
+        pl.when(self.flag)(lambda: pltpu.make_async_copy(self.other, self.pairs[-1][1], place).start())
+        pl.when(jnp.logical_not(self.flag))(lambda: copies[-1].start())
+
+
+def two_groups(here, firsts, step, loads, stores, amplitudes, amps, amp_sem, order, sem, probe, table, obj, acc, g_probe):
     width = probe.shape[-1]
 
-    def mine(slot, g):
-        return here.start(slot)[1] // width == jnp.where(g == 0, firsts[0], firsts[1])
+    def listed(g, count):
+        def look(slot, n):
+            order[n] = slot
+            return n + (here.start(slot)[1] // width == firsts[g]).astype(jnp.int32)
+
+        return lax.fori_loop(0, here.count, look, count)
+
+    first = listed(0, jnp.zeros((), jnp.int32))
+    count = listed(1, first)
 
     def amplitude_copy(slot):
         return pltpu.make_async_copy(amplitudes.at[slot], amps.at[slot], amp_sem.at[slot])
 
-    def fetch(slot, _):
-        pl.when(mine(slot, 0) | mine(slot, 1))(lambda: amplitude_copy(slot).start())
+    def fetch(i, _):
+        amplitude_copy(order[i]).start()
         return 0
 
-    lax.fori_loop(0, here.count, fetch, 0)
-
-    def group(g, _):
-        for k in (0, 1):
-            pl.when(g == k)(functools.partial(wait_all, loads[k]))
-
-        def work(slot):
-            def amplitude():
-                amplitude_copy(slot).wait()
-                return amps[slot]
-
-            visit(here.start(slot), step * g, amplitude, probe, table, obj, acc, g_probe)
-
-        def each(slot, _):
-            pl.when(mine(slot, g))(lambda: work(slot))
-            return 0
-
-        lax.fori_loop(0, here.count, each, 0)
-        for k in (0, 1):
-            pl.when(g == k)(lambda k=k: start_all(stores[k], sem, k * len(stores[0])) and None)
+    lax.fori_loop(0, count, fetch, 0)
+
+    def store(g):
+        start_all(stores[g], sem, g * len(stores[0]))
+
+    def slot_at(i):
+        slot = order[i]
+
+        def amplitude():
+            amplitude_copy(slot).wait()
+            return amps[slot]
+
+        return Slot(here.start(slot), step * (i >= first).astype(jnp.int32), amplitude, obj, acc)
+
+    def after_first(i):
+        pl.when((i < first) & (first <= i + 2))(lambda: store(0))
+
+    def two(p, _):
+        i = 2 * p
+        pl.when((i + 1 >= first) & (i - 1 < first))(loads[1].wait)
+        visit([slot_at(i), slot_at(i + 1)], probe, table, g_probe)
+        after_first(i)
         return 0
 
-    lax.fori_loop(0, 2, group, 0)
-    for k in (0, 1):
-        wait_all([pltpu.make_async_copy(a, b, sem.at[k * len(stores[0]) + i]) for i, (a, b) in enumerate(stores[k])])
+    def one():
+        visit([slot_at(count - 1)], probe, table, g_probe)
+        after_first(count - 1)
+
+    loads[0].wait()
+    loads[1].start()
+    pl.when(first == 0)(lambda: store(0))
+    pairs = count // 2
+    lax.fori_loop(0, pairs, two, 0)
+    pl.when(2 * pairs - 1 < first)(loads[1].wait)
+    pl.when(count % 2 == 1)(one)
+    store(1)
+    for g in (0, 1):
+        wait_all([pltpu.make_async_copy(a, b, sem.at[g * len(stores[0]) + i]) for i, (a, b) in enumerate(stores[g])])
 
 
 def inner_body(
     axes, tx, ty, centers, counts, tile, on, off_quarters, relayed, off_mid, amplitudes, probe_in, table_in,
-    g_quarters, g_tile_mid, g_on_mid, g_off_mid, g_probe, obj, acc, probe, table, amps, sem, out_sem, amp_sem,
+    g_quarters, g_tile_mid, g_on_mid, g_off_mid, g_probe, obj, acc, probe, table, amps, order, sem, out_sem, amp_sem,
 ):
     width = probe.shape[-1]
     rim = width // 2
@@ -235,10 +298,10 @@
     loads[0].append((off_mid, obj.at[1, :, :, here.off]))
     waits = []
     for k in (0, 1):
-        at = 16 * k
-        started = start_all(loads[k], sem, at)
         lanes = slice(k * width, (k + 1) * width)
-        waits.append(started + start_chosen(here.relayed, relayed, off_quarters, [(lanes, obj.at[2 * k, :, :, here.off])], sem, at + len(started)))
+        loads[k].append((off_quarters.at[:, :, :, lanes], obj.at[2 * k, :, :, here.off]))
+        waits.append(ChosenLoads(loads[k], here.relayed, relayed.at[:, :, :, lanes], sem, 16 * k))
+    waits[0].start()
     acc[...] = jnp.zeros_like(acc)
     g_probe[...] = jnp.zeros_like(g_probe)
     stores = (
@@ -250,13 +313,14 @@
             (acc.at[1, :, :, here.off], g_off_mid),
         ],
     )
-    two_groups(here, (1, 2), 1, waits, stores, amplitudes, amps, amp_sem, out_sem, probe, table, obj, acc, g_probe)
+    two_groups(here, (1, 2), 1, waits, stores, amplitudes, amps, amp_sem, order, out_sem, probe, table, obj, acc, g_probe)
 
 
 def outer_body(
     axes, tx, ty, centers, counts, tile, on, off_quarters, relayed, off_ends, left, right, carried, carried_probe, amplitudes, probe_in, table_in,
-    g_tile_ends, g_tile_quarters, g_on_ends, g_on_quarters, g_off_ends, g_off_quarters, g_left, g_right, g_probe,
-    obj, acc, probe, table, amps, sem, out_sem, amp_sem,
+    g_tile_ends, g_tile_quarters, g_on_ends, g_on_quarters, g_off_ends, g_off_quarters,
+    g_left, g_left_corners, g_right, g_right_corners, g_probe,
+    obj, acc, probe, table, amps, order, sem, out_sem, amp_sem,
 ):
     width = probe.shape[-1]
     rim = width // 2
@@ -265,9 +329,9 @@
     own = slice(rim, rim + tile_rows)
     one, two = slice(0, rim), slice(rim, width)
     waits, stores = [], []
-    for k, (end, quarter, near, far, half, side, g_side) in enumerate((
-        (0, 1, two, slice(0, rim), one, left, g_left),
-        (3, 2, one, slice(tile_cols - rim, tile_cols), two, right, g_right),
+    for k, (end, quarter, near, far, half, side, g_side, g_corners) in enumerate((
+        (0, 1, two, slice(0, rim), one, left, g_left, g_left_corners),
+        (3, 2, one, slice(tile_cols - rim, tile_cols), two, right, g_right, g_right_corners),
     )):
         first = rim if k == 0 else tile_cols - rim - width
         there = slice(first, first + width)
@@ -282,22 +346,25 @@
             (on.at[:, :, :, first + rim : first + rim + width], obj.at[quarter, :, :, here.on]),
             (carried.at[k], acc.at[quarter]),
         ]
-        started = start_all(loads, sem, 16 * k)
         lanes = slice(k * width, (k + 1) * width)
-        waits.append(started + start_chosen(here.relayed, relayed, off_quarters, [(lanes, obj.at[quarter, :, :, here.off])], sem, 16 * k + len(started)))
+        loads.append((off_quarters.at[:, :, :, lanes], obj.at[quarter, :, :, here.off]))
+        waits.append(ChosenLoads(loads, here.relayed, relayed.at[:, :, :, lanes], sem, 16 * k))
         stores.append([
             (acc.at[end, :, :, own, near], g_tile_ends.at[:, :, :, half]),
             (acc.at[end, :, :, here.on, near], g_on_ends.at[:, :, :, half]),
             (acc.at[end, :, :, here.off, near], g_off_ends.at[:, :, :, half]),
-            (acc.at[end, :, :, :, half], g_side),
+            (acc.at[end, :, :, own, half], g_side),
+            (acc.at[end, :, :, here.on, half], g_corners.at[:, :, :rim]),
+            (acc.at[end, :, :, here.off, half], g_corners.at[:, :, rim:]),
             (acc.at[quarter, :, :, own], g_tile_quarters.at[:, :, :, lanes]),
             (acc.at[quarter, :, :, here.on], g_on_quarters.at[:, :, :, lanes]),
             (acc.at[quarter, :, :, here.off], g_off_quarters.at[:, :, :, lanes]),
         ])
+    waits[0].start()
     for end in (0, 3):
         acc[end] = jnp.zeros_like(acc[end])
     last_block = (tile_cols + 2 * rim) // width - 2
-    two_groups(here, (0, last_block), 2, waits, stores, amplitudes, amps, amp_sem, out_sem, probe, table, obj, acc, g_probe)
+    two_groups(here, (0, last_block), 2, waits, stores, amplitudes, amps, amp_sem, order, out_sem, probe, table, obj, acc, g_probe)
 
 
 SMEM = pl.BlockSpec(memory_space=pltpu.SMEM)
@@ -329,8 +396,9 @@
             pltpu.VMEM(probe.shape, F32),
             pltpu.VMEM(table.shape, table.dtype),
             pltpu.VMEM(amplitudes.shape, F32),
+            pltpu.SMEM((amplitudes.shape[0] + 1,), jnp.int32),
             pltpu.SemaphoreType.DMA((32,)),
-            pltpu.SemaphoreType.DMA((16,)),
+            pltpu.SemaphoreType.DMA((18,)),
             pltpu.SemaphoreType.DMA((amplitudes.shape[0],)),
         ],
         compiler_params=ROOM,
@@ -411,77 +479,35 @@
     )(*scalars, patterns, pick)
 
 
-def merge_body(tx, on_ends, off_ends, left, right, quarters, mid, on, off, sides, sem):
+def merge_body(on_ends, off_ends, left, right, quarters, mid, on, off, sides, sem):
     rim = left.shape[-1]
     width = 2 * rim
-    below = left.shape[2] - rim
-    odd = tx[0] % 2
-    on_rows, off_rows = rows_at((1 - odd) * below, rim), rows_at(odd * below, rim)
     wait_all(run_all([
         (on_ends, on.at[:, :, :, :width]),
+        (off_ends, off),
+        (left.at[:, :, :rim], sides.at[0, :, :, :, :rim]),
+        (right.at[:, :, :rim], sides.at[0, :, :, :, rim:]),
+        (left.at[:, :, rim:], sides.at[1, :, :, :, :rim]),
+        (right.at[:, :, rim:], sides.at[1, :, :, :, rim:]),
         (quarters, on.at[:, :, :, width : 3 * width]),
         (mid, on.at[:, :, :, 3 * width :]),
-        (off_ends, off),
-        (left.at[:, :, on_rows], sides.at[0, :, :, :, :rim]),
-        (right.at[:, :, on_rows], sides.at[0, :, :, :, rim:]),
-        (left.at[:, :, off_rows], sides.at[1, :, :, :, :rim]),
-        (right.at[:, :, off_rows], sides.at[1, :, :, :, rim:]),
     ], sem))
     on[:, :, :, :width] += sides[0]
     off[...] += sides[1]
 
 
-def merged(tx, on_ends, off_ends, left, right, quarters, mid):
+def merged(on_ends, off_ends, left, right, quarters, mid):
     slices, _, rim, width = on_ends.shape
     cols = width + quarters.shape[3] + mid.shape[3]
     return pl.pallas_call(
         merge_body,
         out_shape=(shape(slices, 2, rim, cols), jax.ShapeDtypeStruct(off_ends.shape, F32)),
-        in_specs=[SMEM] + [HBM] * 6,
+        in_specs=[HBM] * 6,
         out_specs=(VMEM, VMEM),
         scratch_shapes=[pltpu.VMEM((2,) + on_ends.shape, F32), pltpu.SemaphoreType.DMA((8,))],
         compiler_params=ROOM,
-        cost_estimate=costs(10**11),
-    )(tx, on_ends, off_ends, left, right, quarters, mid)
-
-
-def halves_body(tx, x, mine, other):
-    half = mine.shape[0]
-    bit = tx[0] % 2
-    mine[...] = x[rows_at(bit * half, half)]
-    other[...] = x[rows_at((1 - bit) * half, half)]
-
-
-def halves_of(tx, x):
-    half = shape(x.shape[0] // 2, x.shape[1])
-    return pl.pallas_call(
-        halves_body,
-        out_shape=(half, half),
-        in_specs=[SMEM, VMEM],
-        out_specs=(VMEM, VMEM),
-        compiler_params=ROOM,
-        cost_estimate=costs(10**11),
-    )(tx, x)
-
-
-def scaled_body(counts, *refs):
-    parts, out = refs[:-1], refs[-1]
-    positions = lax.fori_loop(0, counts.shape[0], lambda i, n: n + counts[i], jnp.zeros((), jnp.int32))
-    total = parts[0][...]
-    for part in parts[1:]:
-        total += part[...]
-    out[...] = total / jnp.sqrt(jnp.full(out.shape, jnp.maximum(positions, 1).astype(F32)))
-
-
-def scaled_sum(counts, parts):
-    return pl.pallas_call(
-        scaled_body,
-        out_shape=jax.ShapeDtypeStruct(parts[0].shape, F32),
-        in_specs=[SMEM] + [VMEM] * len(parts),
-        out_specs=VMEM,
-        compiler_params=ROOM,
-        cost_estimate=costs(10**8),
-    )(counts, *parts)
+        cost_estimate=pl.CostEstimate(flops=10**6, bytes_accessed=10**5, transcendentals=0),
+    )(on_ends, off_ends, left, right, quarters, mid)
 
 
 def total_body(tx, ends, quarters, mid, left, right, on, off_quarters, off_ends, off_mid, out):
@@ -492,8 +518,8 @@
     two, four = slice(rim, rim + width), slice(cols - rim - width, cols - rim)
     three = slice(rim + width, cols - rim - width)
     odd = tx[0] % 2
-    out[0, 0, :, one] = ends[0, 0, :, :rim] + left[0, 0, rim : rim + rows]
-    out[0, 0, :, five] = ends[0, 0, :, rim:] + right[0, 0, rim : rim + rows]
+    out[0, 0, :, one] = ends[0, 0, :, :rim] + left[0, 0]
+    out[0, 0, :, five] = ends[0, 0, :, rim:] + right[0, 0]
     out[0, 0, :, two] = quarters[0, 0, :, :width]
     out[0, 0, :, four] = quarters[0, 0, :, width:]
     out[0, 0, :, three] = mid[0, 0]
@@ -562,32 +588,13 @@
     return mine + lax.ppermute(other, "tx", pairs)
 
 
-def joined_body(apart, tx, *refs):
-    pieces, out = refs[:-1], refs[-1]
-    rows = out.shape[0] // len(pieces)
-    mine = sum(((tx[0] // step) % 2) * 2**k for k, step in enumerate(apart))
-    for i, piece in enumerate(pieces):
-        out[rows_at((mine ^ i) * rows, rows)] = piece[...]
-
-
-def spread(flat, apart, count):
-    pieces = [flat]
-    for i in range(1, 2 ** len(apart)):
-        flip = sum(step for k, step in enumerate(apart) if i >> k & 1)
-        pieces.append(lax.ppermute(flat, "tx", [(j, j ^ flip) for j in range(count)]))
-    return pieces
-
-
-def joined(tx, pieces, apart):
-    rows, cols = pieces[0].shape
-    return pl.pallas_call(
-        functools.partial(joined_body, apart),
-        out_shape=shape(rows * len(pieces), cols),
-        in_specs=[SMEM] + [VMEM] * len(pieces),
-        out_specs=VMEM,
-        compiler_params=ROOM,
-        cost_estimate=costs(10**8),
-    )(tx, *pieces)
+def doubled(flat, apart):
+    bit = (lax.axis_index("tx") // apart) % 2
+    return joined(flat, lax.ppermute(flat, "tx", [(i, i ^ apart) for i in range(lax.axis_size("tx"))]), bit)
+
+
+def joined(flat, other, bit):
+    return jnp.concatenate([jnp.where(bit == 0, flat, other), jnp.where(bit == 0, other, flat)], axis=0)
 
 
 def per_device(object_slab, probe, patterns, centers, counts):
@@ -613,8 +620,8 @@
     left, right = along(to_right, 1), along(to_left, -1)
     off_quarters = across(quarters, 1, middle - 1)
     off_mid = across(mid, 1)
+    on_shape = shape(slices, 2, rim, tile_cols + width)
     amplitudes = amplitudes_of(axes, (tx, ty, counts), after(patterns, to_left))
-    on_shape = shape(slices, 2, rim, tile_cols + width)
 
     def strips(tile, left, right):
         on, ends = copies_call(strips_body, (tx,), (tile, left, right), (on_shape, quarters_shape), 10**8)
@@ -633,41 +640,49 @@
         (shape(2, slices, 2, full, width), shape(slices, 2, tile_rows, mid_cols), mid_shape, mid_shape), tile_rows,
     )
     back_mid = across(g_off_mid, 1)
-    g_tile_ends, g_tile_quarters, g_on_ends, g_on_quarters, g_off_ends, g_off_quarters, g_left, g_right, g_probe = field_call(
+    (
+        g_tile_ends, g_tile_quarters, g_on_ends, g_on_quarters, g_off_ends, g_off_quarters,
+        g_left, g_left_corners, g_right, g_right_corners, g_probe,
+    ) = field_call(
         outer_body, axes, 4, scalars, (tile, on, off_quarters, relayed, off_ends, left, right, g_quarters, g_probe), amplitudes, probe,
         (
             shape(slices, 2, tile_rows, width), shape(slices, 2, tile_rows, 2 * width), ends_shape, quarters_shape,
-            ends_shape, quarters_shape, side_shape, side_shape,
+            ends_shape, quarters_shape, column_shape, column_shape, column_shape, column_shape,
         ),
         tile_rows,
     )
-    from_left = along(g_right, 1)
-    from_right = along(g_left, -1)
+    g_off_quarters, g_left_corners, g_right_corners, g_probe, _ = lax.optimization_barrier(
+        (g_off_quarters, g_left_corners, g_right_corners, g_probe, back_mid)
+    )
+    corners_left, corners_right = along(g_right_corners, 1), along(g_left_corners, -1)
     back_quarters = across(g_off_quarters, 1)
-
-    apart = [2**k for k in range(1, axes[0].bit_length() - 1)]
-    mine, other = halves_of(tx, after(g_probe.reshape(-1, width), back_mid))
-    flat = mine + lax.ppermute(other, "tx", [(i, i ^ 1) for i in range(axes[0])])
-    for step in reversed(apart):
-        flat = halved(flat, step)
-    on_all, off_ends = merged(tx, after(g_on_ends, back_quarters, flat), g_off_ends, from_left, from_right, g_on_quarters, g_on_mid)
+    apart = [1] + [2**k for k in range(axes[0].bit_length() - 2, 1, -1)]
+    shard = g_probe.size // width // 2 ** len(apart)
+
+    def shared(flat):
+        for step in apart:
+            flat = halved(flat, step)
+        for step in (2**k for k in range(axes[1].bit_length() - 1)):
+            flat = flat + lax.ppermute(flat, "ty", [(i, i ^ step) for i in range(axes[1])])
+        return flat / jnp.sqrt(jnp.maximum(jnp.sum(counts), 1).astype(F32))
+
+    flat = lax.cond(counts[0] >= 0, shared, lambda x: x[:shard], g_probe.reshape(-1, width))
+    other = lax.ppermute(flat, "tx", [(i, i ^ 2) for i in range(axes[0])])
+    on_all, off_ends = merged(after(g_on_ends, flat, back_quarters), g_off_ends, corners_left, corners_right, g_on_quarters, g_on_mid)
     back_ends = across(off_ends, 1)
     back_on = across(on_all, 0)
-    flat = after(flat, on_all)
-    others = [lax.ppermute(flat, "ty", [(i, (i + step) % axes[1]) for i in range(axes[1])]) for step in range(1, axes[1])]
-    flat = after(scaled_sum(counts, (flat, *others)), back_ends, back_on)
+    from_left, from_right = along(g_right, 1), along(g_left, -1)
+    flat = after(flat + other, on_all)
+    for step in reversed(apart[1:]):
+        flat = doubled(flat, step)
+    flat = after(flat, from_left, from_right)
+    last = lax.ppermute(flat, "tx", [(i, i ^ 1) for i in range(axes[0])])
     inner = total_of(
         tx,
         (g_tile_ends, g_tile_quarters, g_tile_mid, from_left, from_right, back_on, back_quarters, back_ends, back_mid),
         tile.shape,
     )
-    pieces = spread(flat, apart[:2], axes[0])
-    pieces = after(pieces[0], inner), *pieces[1:]
-    while apart:
-        flat = joined(tx, pieces, apart[:2])
-        apart = apart[2:]
-        pieces = spread(flat, apart[:2] or [1], axes[0])
-    probe_sum = joined(tx, pieces, [1]).reshape(probe.shape)
+    probe_sum = joined(flat, after(last, inner), lax.axis_index("tx") % 2).reshape(probe.shape)
     return (inner, probe_sum)
 
 

time: 172 us -> 161 us (0.936)
  Pallas kernels: 75 us -> 42.4 us
  starting transfers between devices: 57.6 us -> 71.6 us
  waiting for transfers between devices: 32.3 us -> 38.6 us
    pallas_call x2, Pallas kernels: 44 us -> 20.3 us  [field_call(): pl.pallas_call(functools.partial(body, axes), out_shape=tuple(outs) + (ja...]
    ppermute x8 -> x5, waiting for transfers between devices: 3.72 us -> 13 us  [the longest x2 7.14 us: shared(): lax.ppermute(flat, 'ty', [(i, i ^ step) for i in range(axes[1])])]
    ppermute x4 -> x6, starting transfers between devices: 19.8 us -> 28.6 us  [along(): lax.ppermute(x, 'ty', [(i, i + step) for i in range(count) if 0 <= i + st...]
    ppermute x2, waiting for transfers between devices: 13.3 us -> 5.05 us  [halved(): return mine + lax.ppermute(other, 'tx', pairs)]
    pallas_call x4 -> x0, Pallas kernels: 7.37 us -> none  [the longest x2 3.54 us: joined(): pl.pallas_call(functools.partial(joined_body, apart), out_shape=shape(row...]
    ppermute x8 -> x5, starting transfers between devices: 6.75 us -> 11.8 us  [the longest x1 6.55 us: per_device(): other = lax.ppermute(flat, 'tx', [(i, i ^ 2) for i in range(axes[0])])]
    ppermute x8, waiting for transfers between devices: 10.3 us -> 14.6 us  [across(): return lax.ppermute(x, 'tx', pairs)]
    ppermute x2, starting transfers between devices: 0.14 us -> 3.11 us  [halved(): return mine + lax.ppermute(other, 'tx', pairs)]
  transfers between devices with their start and end apart: 24 -> 23, of which waited for: 9 -> 9; matrix products, arithmetic and copies ran while one was open for 1% -> 1% of each run, Pallas kernels for 36% -> 22%
where the time goes in v3:
time: 161 us; the launch traced here: 160 us
  starting transfers between devices  71.6 us (44%)
  Pallas kernels  42.4 us (26%)
  waiting for transfers between devices  38.6 us (24%)
  local copies, waits for them, and re-layouts  4.11 us (3%)
  other arithmetic  1.64 us (1%)
    ppermute x6, starting transfers between devices, along(): lax.ppermute(x, 'ty', [(i, i + step) for i in range(count) if 0 <= i + st...  28.6 us
    ppermute x8, starting transfers between devices, across(): return lax.ppermute(x, 'tx', pairs)  24.8 us
    pallas_call x2, Pallas kernels, field_call(): pl.pallas_call(functools.partial(body, axes), out_shape=tuple(outs) + (ja...  20.3 us
    ppermute x8, waiting for transfers between devices, across(): return lax.ppermute(x, 'tx', pairs)  14.6 us
    ppermute x2, waiting for transfers between devices, shared(): lax.ppermute(flat, 'ty', [(i, i ^ step) for i in range(axes[1])])  7.14 us
    ppermute x1, starting transfers between devices, per_device(): other = lax.ppermute(flat, 'tx', [(i, i ^ 2) for i in range(axes[0])])  6.55 us
    pallas_call x2, Pallas kernels, copies_call(): pl.pallas_call(body, out_shape=tuple(outs), in_specs=[SMEM] * len(scalars...  6.53 us
    pallas_call x1, Pallas kernels, total_of(): pl.pallas_call(total_body, grid=tile_shape[:2], out_shape=jax.ShapeDtypeS...  6.15 us
  transfers between devices with their start and end apart: 23, of which 9 were waited for; matrix products, arithmetic and copies ran while one was open for 1% of the time, Pallas kernels for 22%

profile of v3, /device:TPU:1, one launch (start us, length us, event | category | flops | bytes accessed | tf_op | source)
XLA Modules:
  0.0 160.1 jit_solution(1888044004738561602)
XLA Ops:
  0.6 3.3 %shard_map.95 = (f32[2,2,256,128]{3,2,1,0:T(8,128)}, f32[2,2,256,128]{3,2,1,0:T(8,128)}, f32[2,2,128,512]{3,2,1,0:T(8,128)}, f32[2,2,128,256]{3,2,1,0:T(8,128)}) custom-call(s32[1]{0:T(128)} %bitcast.tx, f32[2,2,256,1024]{3,2,1,0:T(8,128)} %tile.5), custom_call_target="tpu_custom_call" | custom-call | flops 100000000 | bytes 10000000 | tf_op jit(solution)/shard_map/pallas_call | solution.py:443
  3.9 1.7 %collective-permute-start.5 = (f32[2,2,128,512]{3,2,1,0:T(8,128)}, f32[2,2,128,512]{3,2,1,0:T(8,128)}, u32[]{:S(2)}, u32[]{:S(2)}) collective-permute-start(f32[2,2,128,512]{3,2,1,0:T(8,128)} %get-tuple-element.62), channel_id=1, source_target_pairs={{12,28},{16,0},{13,29},{17,1},{14,30},{18,2},{15,31},{19,3}} | collective-permute-start | bytes 3145736 | tf_op jit(solution)/shard_map/ppermute | solution.py:570
  5.6 4.5 %collective-permute-start.8 = (f32[2,2,128,512]{3,2,1,0:T(8,128)}, f32[2,2,128,512]{3,2,1,0:T(8,128)S(1)}, u32[]{:S(2)}, u32[]{:S(2)}) collective-permute-start(f32[2,2,128,512]{3,2,1,0:T(8,128)} %get-tuple-element.62), channel_id=1, source_target_pairs={{4,8},{8,4},{20,24},{24,20},{5,9},{9,5},{21,25},{25,21},{6,10},{10... | collective-permute-start | bytes 3145736 | tf_op jit(solution)/shard_map/ppermute | solution.py:565
  10.1 1.3 collective-permute-start.7
  11.4 4.0 %collective-permute-start.6 = (f32[2,2,256,128]{3,2,1,0:T(8,128)}, f32[2,2,256,128]{3,2,1,0:T(8,128)S(1)}, u32[]{:S(2)}, u32[]{:S(2)}) collective-permute-start(f32[2,2,256,128]{3,2,1,0:T(8,128)} %get-tuple-element.64), channel_id=1, source_target_pairs={{0,1},{1,2},{2,3},{4,5},{5,6},{6,7},{8,9},{9,10},{10,11},{12,13},{... | collective-permute-start | bytes 1572872 | tf_op jit(solution)/shard_map/ppermute | solution.py:557
  15.4 2.5 %collective-permute-start.11 = (f32[2,2,128,256]{3,2,1,0:T(8,128)}, f32[2,2,128,256]{3,2,1,0:T(8,128)}, u32[]{:S(2)}, u32[]{:S(2)}) collective-permute-start(f32[2,2,128,256]{3,2,1,0:T(8,128)} %get-tuple-element.67), channel_id=1, source_target_pairs={{4,8},{8,4},{12,16},{16,12},{20,24},{24,20},{5,9},{9,5},{13,17},{1... | collective-permute-start | bytes 1572872 | tf_op jit(solution)/shard_map/ppermute | solution.py:565
  17.9 1.6 %collective-permute-start.9 = (f32[2,2,128,512]{3,2,1,0:T(8,128)}, f32[2,2,128,512]{3,2,1,0:T(8,128)}, u32[]{:S(2)}, u32[]{:S(2)}) collective-permute-start(f32[2,2,128,512]{3,2,1,0:T(8,128)} %collective-permute-done.5), channel_id=1, source_target_pairs={{28,16},{0,12},{29,17},{1,13},{30,18},{2,14},{31,19},{3,15}} | collective-permute-start | bytes 3145736 | tf_op jit(solution)/shard_map/ppermute | solution.py:575
  19.5 5.8 %shard_map.96.amplitudes = f32[8,256,256]{2,1,0:T(8,128)} custom-call(s32[1]{0:T(128)} %bitcast.tx, s32[1]{0:T(128)} %bitcast.1.ty, s32[32]{0:T(128)S(1)} %copy-done.7, f32[8,256,256]{2,1,0:T(8,128)} %patterns, bf16[3,256,256]{2,1,0:T(8,128)(2,1)} %constant.97.clone.pick), custom_call_target="tpu_custom_call" | custom-call | flops 99999997952 | bytes 10000000 | tf_op jit(solution)/shard_map/pallas_call | solution.py:471
  25.4 0.7 copy.11.centers
  26.1 13.9 %conditional.2 = (f32[2,2,128,1280]{3,2,1,0:T(8,128)}, f32[2,2,128,512]{3,2,1,0:T(8,128)S(1)}) conditional(s32[]{:T(128)} %bitcast.2, () %tuple.29, (s32[1]{0:T(128)}, f32[2,2,256,1024]{3,2,1,0:T(8,128)}, f32[2,2,256,128]{3,2,1,0:T(8,128)S(1)}, f32[2,2,256,128]{3,2,1,0:T(8,128)S(1)}) %tuple.32), branch_computations={%region_0.0_spmd, %region_1.0_spmd} | conditional | flops 100000000 | bytes 20485816 | solution.py:634
  26.1 3.3 %branch_1_fun.1 = (f32[2,2,128,1280]{3,2,1,0:T(8,128)}, f32[2,2,128,512]{3,2,1,0:T(8,128)S(1)}) custom-call(s32[1]{0:T(128)} %get-tuple-element.16.tx, f32[2,2,256,1024]{3,2,1,0:T(8,128)} %get-tuple-element.17.tile, f32[2,2,256,128]{3,2,1,0:T(8,128)S(1)} %get-tuple-element.18.left, f32[2,2,256,128]{3,2,1,0:T(8,128)S(1)} %get-tuple-element.19.right), custom_call_target="tpu_custom_call" | custom-call | flops 100000000 | bytes 10000000 | tf_op jit(solution)/shard_map/cond/branch_1_fun/pallas_call | solution.py:443
  29.3 5.7 %collective-permute-start = (f32[2,2,128,1280]{3,2,1,0:T(8,128)}, f32[2,2,128,1280]{3,2,1,0:T(8,128)}, u32[]{:S(2)}, u32[]{:S(2)}) collective-permute-start(f32[2,2,128,1280]{3,2,1,0:T(8,128)} %get-tuple-element.20), channel_id=1, source_target_pairs={{0,4},{4,0},{8,12},{12,8},{16,20},{20,16},{24,28},{28,24},{1,5},{5... | collective-permute-start | bytes 7864328 | tf_op jit(solution)/shard_map/cond/branch_1_fun/ppermute | solution.py:565
  35.0 4.9 %collective-permute-done = f32[2,2,128,1280]{3,2,1,0:T(8,128)} collective-permute-done((f32[2,2,128,1280]{3,2,1,0:T(8,128)}, f32[2,2,128,1280]{3,2,1,0:T(8,128)}, u32[]{:S(2)}, u32[]{:S(2)}) %collective-permute-start) | collective-permute-done | bytes 2621472 | tf_op jit(solution)/shard_map/cond/branch_1_fun/ppermute | solution.py:565
  39.9 1.9 %collective-permute-start.10 = (f32[2,2,128,512]{3,2,1,0:T(8,128)S(1)}, f32[2,2,128,512]{3,2,1,0:T(8,128)}, u32[]{:S(2)}, u32[]{:S(2)}) collective-permute-start(f32[2,2,128,512]{3,2,1,0:T(8,128)S(1)} %get-tuple-element.66), channel_id=1, source_target_pairs={{4,8},{8,4},{12,16},{16,12},{20,24},{24,20},{5,9},{9,5},{13,17},{1... | collective-permute-start | bytes 3145736 | tf_op jit(solution)/shard_map/ppermute | solution.py:565
  41.9 1.0 copy-done.5
  42.9 9.3 %shard_map.97 = (f32[2,2,2,512,256]{4,3,2,1,0:T(8,128)}, f32[2,2,256,256]{3,2,1,0:T(8,128)}, f32[2,2,128,256]{3,2,1,0:T(8,128)}, f32[2,2,128,256]{3,2,1,0:T(8,128)}, f32[2,256,256]{2,1,0:T(8,128)}) custom-call(s32[1]{0:T(128)} %bitcast.tx, s32[1]{0:T(128)} %bitcast.1.ty, s32[8,2]{1,0:T(8,128)} %copy.11.centers, s32[32]{0:T(128)S(1)} %copy-done.7, ...), custom_call_target="tpu_custom_call" | custom-call | flops 20000000000 | bytes 10000000 | tf_op jit(solution)/shard_map/pallas_call | solution.py:388
  52.2 3.6 %collective-permute-start.14 = (f32[2,2,128,256]{3,2,1,0:T(8,128)}, f32[2,2,128,256]{3,2,1,0:T(8,128)S(1)}, u32[]{:S(2)}, u32[]{:S(2)}) collective-permute-start(f32[2,2,128,256]{3,2,1,0:T(8,128)} %get-tuple-element.80), channel_id=1, source_target_pairs={{4,8},{8,4},{12,16},{16,12},{20,24},{24,20},{5,9},{9,5},{13,17},{1... | collective-permute-start | bytes 1572872 | tf_op jit(solution)/shard_map/ppermute | solution.py:565
  55.9 9.7 %collective-permute-done.10.off_ends = f32[2,2,128,512]{3,2,1,0:T(8,128)} collective-permute-done((f32[2,2,128,512]{3,2,1,0:T(8,128)S(1)}, f32[2,2,128,512]{3,2,1,0:T(8,128)}, u32[]{:S(2)}, u32[]{:S(2)}) %collective-permute-start.10) | collective-permute-done | bytes 1048608 | tf_op jit(solution)/shard_map/ppermute | solution.py:565
  65.6 11.0 %shard_map.98 = (f32[2,2,256,256]{3,2,1,0:T(8,128)}, f32[2,2,256,512]{3,2,1,0:T(8,128)}, f32[2,2,128,256]{3,2,1,0:T(8,128)}, f32[2,2,128,512]{3,2,1,0:T(8,128)},...) custom-call(s32[1]{0:T(128)} %bitcast.tx, ...), custom_call_target="tpu_custom_call" | custom-call | flops 20000000000 | bytes 10000000 | tf_op jit(solution)/shard_map/pallas_call | solution.py:388
  76.6 1.9 %collective-permute-start.15 = (f32[2,2,128,512]{3,2,1,0:T(8,128)}, f32[2,2,128,512]{3,2,1,0:T(8,128)S(1)}, u32[]{:S(2)}, u32[]{:S(2)}) collective-permute-start(f32[2,2,128,512]{3,2,1,0:T(8,128)} %get-tuple-element.82), channel_id=1, source_target_pairs={{4,8},{8,4},{12,16},{16,12},{20,24},{24,20},{5,9},{9,5},{13,17},{1... | collective-permute-start | bytes 3145736 | tf_op jit(solution)/shard_map/ppermute | solution.py:565
  78.5 18.6 %collective-permute-start.16 = (f32[2,2,256,128]{3,2,1,0:T(8,128)}, f32[2,2,256,128]{3,2,1,0:T(8,128)S(1)}, u32[]{:S(2)}, u32[]{:S(2)}) collective-permute-start(f32[2,2,256,128]{3,2,1,0:T(8,128)} %get-tuple-element.85), channel_id=1, source_target_pairs={{0,1},{1,2},{2,3},{4,5},{5,6},{6,7},{8,9},{9,10},{10,11},{12,13},{... | collective-permute-start | bytes 1572872 | tf_op jit(solution)/shard_map/ppermute | solution.py:557
  97.1 1.3 collective-permute-start.17
  98.4 20.7 %conditional.3 = (f32[128,256]{1,0:T(8,128)S(1)}) conditional(s32[]{:T(128)} %bitcast.2, f32[512,256]{1,0:T(8,128)S(1)} %bitcast.6, (f32[512,256]{1,0:T(8,128)S(1)}, s32[32]{0:T(128)S(1)}) %tuple.47), branch_computations={%region_2.0_spmd, %region_3.5_spmd} | conditional | flops 196696 | bytes 5374882 | solution.py:669
  98.5 0.1 collective-permute-start.1
  98.6 1.5 collective-permute-done.1
  100.1 3.0 %collective-permute-start.2 = (f32[128,256]{1,0:T(8,128)S(1)}, f32[128,256]{1,0:T(8,128)S(1)}, u32[]{:S(2)}, u32[]{:S(2)}) collective-permute-start(f32[128,256]{1,0:T(8,128)S(1)} %constant_dynamic-slice_fusion), channel_id=1, source_target_pairs={{0,16},{4,20},{8,24},{12,28},{16,0},{20,4},{24,8},{28,12},{1,17},{... | collective-permute-start | bytes 393224 | tf_op jit(solution)/shard_map/cond/branch_1_fun/ppermute | solution.py:588
  103.2 3.6 %collective-permute-done.2 = f32[128,256]{1,0:T(8,128)S(1)} collective-permute-done((f32[128,256]{1,0:T(8,128)S(1)}, f32[128,256]{1,0:T(8,128)S(1)}, u32[]{:S(2)}, u32[]{:S(2)}) %collective-permute-start.2) | collective-permute-done | bytes 131104 | tf_op jit(solution)/shard_map/cond/branch_1_fun/ppermute | solution.py:588
  106.8 3.7 %collective-permute-start.3 = (f32[128,256]{1,0:T(8,128)S(1)}, f32[128,256]{1,0:T(8,128)S(1)}, u32[]{:S(2)}, u32[]{:S(2)}) collective-permute-start(f32[128,256]{1,0:T(8,128)S(1)} %dynamic-slice_add_fusion.1), channel_id=1, source_target_pairs={{0,1},{1,0},{2,3},{3,2},{4,5},{5,4},{6,7},{7,6},{8,9},{9,8},{10,11... | collective-permute-start | bytes 393224 | tf_op jit(solution)/shard_map/cond/branch_1_fun/ppermute | solution.py:666
  110.5 2.4 %collective-permute-done.3 = f32[128,256]{1,0:T(8,128)S(1)} collective-permute-done((f32[128,256]{1,0:T(8,128)S(1)}, f32[128,256]{1,0:T(8,128)S(1)}, u32[]{:S(2)}, u32[]{:S(2)}) %collective-permute-start.3) | collective-permute-done | bytes 131104 | tf_op jit(solution)/shard_map/cond/branch_1_fun/ppermute | solution.py:666
  112.9 0.1 collective-permute-start.4
  112.9 0.6 reduce_sum.8
  114.3 4.8 %collective-permute-done.4 = f32[128,256]{1,0:T(8,128)S(1)} collective-permute-done((f32[128,256]{1,0:T(8,128)S(1)}, f32[128,256]{1,0:T(8,128)S(1)}, u32[]{:S(2)}, u32[]{:S(2)}) %collective-permute-start.4) | collective-permute-done | bytes 131104 | tf_op jit(solution)/shard_map/cond/branch_1_fun/ppermute | solution.py:666
  119.1 0.8 copy-done
  119.9 0.2 copy-done.1
  120.1 3.6 %shard_map.99 = (f32[2,2,128,1024]{3,2,1,0:T(8,128)}, f32[2,2,128,256]{3,2,1,0:T(8,128)}) custom-call(f32[2,2,128,256]{3,2,1,0:T(8,128)} %get-tuple-element.83.on_ends, f32[2,2,128,256]{3,2,1,0:T(8,128)} %get-tuple-element.84.off_ends, f32[2,2,256,128]{3,2,1,0:T(8,128)} %copy-done, f32[2,2,256,128]{3,2,1,0:T(8,128)} %copy-done.1, ...), custom_call_target="tpu_custom_call" | custom-call | flops 1000000 | bytes 100000 | tf_op jit(solution)/shard_map/pallas_call | solution.py:502
  123.8 2.8 %collective-permute-start.18 = (f32[2,2,128,1024]{3,2,1,0:T(8,128)}, f32[2,2,128,1024]{3,2,1,0:T(8,128)S(1)}, u32[]{:S(2)}, u32[]{:S(2)}) collective-permute-start(f32[2,2,128,1024]{3,2,1,0:T(8,128)} %get-tuple-element.89), channel_id=1, source_target_pairs={{0,4},{4,0},{8,12},{12,8},{16,20},{20,16},{24,28},{28,24},{1,5},{5... | collective-permute-start | bytes 6291464 | tf_op jit(solution)/shard_map/ppermute | solution.py:565
  126.5 6.5 %collective-permute-start.20 = (f32[128,256]{1,0:T(8,128)S(1)}, f32[128,256]{1,0:T(8,128)S(1)}, u32[]{:S(2)}, u32[]{:S(2)}) collective-permute-start(f32[128,256]{1,0:T(8,128)S(1)} %get-tuple-element.102), channel_id=1, source_target_pairs={{0,8},{4,12},{8,0},{12,4},{16,24},{20,28},{24,16},{28,20},{1,9},{5... | collective-permute-start | bytes 393224 | tf_op jit(solution)/shard_map/ppermute | solution.py:670
  133.1 2.1 %collective-permute-start.12 = (f32[2,2,256,128]{3,2,1,0:T(8,128)}, f32[2,2,256,128]{3,2,1,0:T(8,128)}, u32[]{:S(2)}, u32[]{:S(2)}) collective-permute-start(f32[2,2,256,128]{3,2,1,0:T(8,128)} %get-tuple-element.73), channel_id=1, source_target_pairs={{0,1},{1,2},{2,3},{4,5},{5,6},{6,7},{8,9},{9,10},{10,11},{12,13},{... | collective-permute-start | bytes 1572872 | tf_op jit(solution)/shard_map/ppermute | solution.py:557
  135.2 1.3 collective-permute-start.13
  136.5 1.9 %collective-permute-start.19 = (f32[2,2,128,256]{3,2,1,0:T(8,128)}, f32[2,2,128,256]{3,2,1,0:T(8,128)}, u32[]{:S(2)}, u32[]{:S(2)}) collective-permute-start(f32[2,2,128,256]{3,2,1,0:T(8,128)} %get-tuple-element.90), channel_id=1, source_target_pairs={{4,8},{8,4},{12,16},{16,12},{20,24},{24,20},{5,9},{9,5},{13,17},{1... | collective-permute-start | bytes 1572872 | tf_op jit(solution)/shard_map/ppermute | solution.py:565
  138.4 0.3 collective-permute-start.21
  138.7 5.9 %collective-permute-done.21 = f32[128,256]{1,0:T(8,128)S(1)} collective-permute-done((f32[128,256]{1,0:T(8,128)S(1)}, f32[128,256]{1,0:T(8,128)S(1)}, u32[]{:S(2)}, u32[]{:S(2)}) %collective-permute-start.21) | collective-permute-done | bytes 131104 | tf_op jit(solution)/shard_map/ppermute | solution.py:593
  144.6 1.3 collective-permute-done.12.left
  145.9 4.6 %collective-permute-done.13.right = f32[2,2,256,128]{3,2,1,0:T(8,128)} collective-permute-done((f32[2,2,256,128]{3,2,1,0:T(8,128)}, f32[2,2,256,128]{3,2,1,0:T(8,128)}, u32[]{:S(2)}, u32[]{:S(2)}) %collective-permute-start.13) | collective-permute-done | bytes 524320 | tf_op jit(solution)/shard_map/ppermute | solution.py:557
  150.5 1.2 collective-permute-start.22
  151.7 1.4 copy-done.3
  153.1 6.1 %shard_map.100 = f32[2,2,256,1024]{3,2,1,0:T(8,128)} custom-call(s32[1]{0:T(128)} %bitcast.tx, f32[2,2,256,256]{3,2,1,0:T(8,128)} %get-tuple-element.70.ends, f32[2,2,256,512]{3,2,1,0:T(8,128)} %get-tuple-element.71.quarters, f32[2,2,256,256]{3,2,1,0:T(8,128)} %get-tuple-element.72.mid, f32[2,2,256,128]{3,2,1,0:T(8,128)} %collective-permute-done.12.left, ...), custom_call_target="tpu_custom_call" | custom-call | flops 99999997952 | bytes 10000000 | tf_op jit(solution)/shard_map/pallas_call | solution.py:544
  159.3 0.8 pad_maximum_fusion
  (36 shorter events, 0.3 us)
Async XLA Ops:
  0.6 18.9 %copy-start.7 = (s32[32]{0:T(128)S(1)}, s32[32]{0:T(128)}, u32[]{:S(2)}) copy-start(s32[32]{0:T(128)} %counts.5) | copy-start | bytes 388
  3.9 14.0 %collective-permute-start.5 = (f32[2,2,128,512]{3,2,1,0:T(8,128)}, f32[2,2,128,512]{3,2,1,0:T(8,128)}, u32[]{:S(2)}, u32[]{:S(2)}) collective-permute-start(f32[2,2,128,512]{3,2,1,0:T(8,128)} %get-tuple-element.62), channel_id=1, source_target_pairs={{12,28},{16,0},{13,29},{17,1},{14,30},{18,2},{15,31},{19,3}} | collective-permute-start | bytes 3145736 | tf_op jit(solution)/shard_map/ppermute | solution.py:570
  5.6 36.3 %collective-permute-start.8 = (f32[2,2,128,512]{3,2,1,0:T(8,128)}, f32[2,2,128,512]{3,2,1,0:T(8,128)S(1)}, u32[]{:S(2)}, u32[]{:S(2)}) collective-permute-start(f32[2,2,128,512]{3,2,1,0:T(8,128)} %get-tuple-element.62), channel_id=1, source_target_pairs={{4,8},{8,4},{20,24},{24,20},{5,9},{9,5},{21,25},{25,21},{6,10},{10... | collective-permute-start | bytes 3145736 | tf_op jit(solution)/shard_map/ppermute | solution.py:565
  10.1 16.0 %collective-permute-start.7 = (f32[2,2,256,128]{3,2,1,0:T(8,128)}, f32[2,2,256,128]{3,2,1,0:T(8,128)S(1)}, u32[]{:S(2)}, u32[]{:S(2)}) collective-permute-start(f32[2,2,256,128]{3,2,1,0:T(8,128)} %get-tuple-element.60), channel_id=1, source_target_pairs={{1,0},{2,1},{3,2},{5,4},{6,5},{7,6},{9,8},{10,9},{11,10},{13,12},{... | collective-permute-start | bytes 1572872 | tf_op jit(solution)/shard_map/ppermute | solution.py:557
  11.4 14.7 %collective-permute-start.6 = (f32[2,2,256,128]{3,2,1,0:T(8,128)}, f32[2,2,256,128]{3,2,1,0:T(8,128)S(1)}, u32[]{:S(2)}, u32[]{:S(2)}) collective-permute-start(f32[2,2,256,128]{3,2,1,0:T(8,128)} %get-tuple-element.64), channel_id=1, source_target_pairs={{0,1},{1,2},{2,3},{4,5},{5,6},{6,7},{8,9},{9,10},{10,11},{12,13},{... | collective-permute-start | bytes 1572872 | tf_op jit(solution)/shard_map/ppermute | solution.py:557
  15.4 26.4 %collective-permute-start.11 = (f32[2,2,128,256]{3,2,1,0:T(8,128)}, f32[2,2,128,256]{3,2,1,0:T(8,128)}, u32[]{:S(2)}, u32[]{:S(2)}) collective-permute-start(f32[2,2,128,256]{3,2,1,0:T(8,128)} %get-tuple-element.67), channel_id=1, source_target_pairs={{4,8},{8,4},{12,16},{16,12},{20,24},{24,20},{5,9},{9,5},{13,17},{1... | collective-permute-start | bytes 1572872 | tf_op jit(solution)/shard_map/ppermute | solution.py:565
  17.9 24.0 %collective-permute-start.9 = (f32[2,2,128,512]{3,2,1,0:T(8,128)}, f32[2,2,128,512]{3,2,1,0:T(8,128)}, u32[]{:S(2)}, u32[]{:S(2)}) collective-permute-start(f32[2,2,128,512]{3,2,1,0:T(8,128)} %collective-permute-done.5), channel_id=1, source_target_pairs={{28,16},{0,12},{29,17},{1,13},{30,18},{2,14},{31,19},{3,15}} | collective-permute-start | bytes 3145736 | tf_op jit(solution)/shard_map/ppermute | solution.py:575
  19.5 5.8 %copy-start.2 = (s32[8,2]{0,1:T(2,128)S(1)}, s32[8,2]{0,1:T(2,128)}, u32[]{:S(2)}) copy-start(s32[8,2]{0,1:T(2,128)} %param.15) | copy-start | bytes 196
  29.3 10.6 %collective-permute-start = (f32[2,2,128,1280]{3,2,1,0:T(8,128)}, f32[2,2,128,1280]{3,2,1,0:T(8,128)}, u32[]{:S(2)}, u32[]{:S(2)}) collective-permute-start(f32[2,2,128,1280]{3,2,1,0:T(8,128)} %get-tuple-element.20), channel_id=1, source_target_pairs={{0,4},{4,0},{8,12},{12,8},{16,20},{20,16},{24,28},{28,24},{1,5},{5... | collective-permute-start | bytes 7864328 | tf_op jit(solution)/shard_map/cond/branch_1_fun/ppermute | solution.py:565
  39.9 25.6 %collective-permute-start.10 = (f32[2,2,128,512]{3,2,1,0:T(8,128)S(1)}, f32[2,2,128,512]{3,2,1,0:T(8,128)}, u32[]{:S(2)}, u32[]{:S(2)}) collective-permute-start(f32[2,2,128,512]{3,2,1,0:T(8,128)S(1)} %get-tuple-element.66), channel_id=1, source_target_pairs={{4,8},{8,4},{12,16},{16,12},{20,24},{24,20},{5,9},{9,5},{13,17},{1... | collective-permute-start | bytes 3145736 | tf_op jit(solution)/shard_map/ppermute | solution.py:565
  41.9 1.0 copy-start.5
  52.2 24.3 %collective-permute-start.14 = (f32[2,2,128,256]{3,2,1,0:T(8,128)}, f32[2,2,128,256]{3,2,1,0:T(8,128)S(1)}, u32[]{:S(2)}, u32[]{:S(2)}) collective-permute-start(f32[2,2,128,256]{3,2,1,0:T(8,128)} %get-tuple-element.80), channel_id=1, source_target_pairs={{4,8},{8,4},{12,16},{16,12},{20,24},{24,20},{5,9},{9,5},{13,17},{1... | collective-permute-start | bytes 1572872 | tf_op jit(solution)/shard_map/ppermute | solution.py:565
  76.6 21.8 %copy-start.6 = (f32[2,2,128,256]{3,2,1,0:T(8,128)}, f32[2,2,128,256]{3,2,1,0:T(8,128)S(1)}, u32[]{:S(2)}) copy-start(f32[2,2,128,256]{3,2,1,0:T(8,128)S(1)} %collective-permute-done.14.off_mid) | copy-start | bytes 1572868
  76.6 42.5 %collective-permute-start.15 = (f32[2,2,128,512]{3,2,1,0:T(8,128)}, f32[2,2,128,512]{3,2,1,0:T(8,128)S(1)}, u32[]{:S(2)}, u32[]{:S(2)}) collective-permute-start(f32[2,2,128,512]{3,2,1,0:T(8,128)} %get-tuple-element.82), channel_id=1, source_target_pairs={{4,8},{8,4},{12,16},{16,12},{20,24},{24,20},{5,9},{9,5},{13,17},{1... | collective-permute-start | bytes 3145736 | tf_op jit(solution)/shard_map/ppermute | solution.py:565
  78.5 40.6 %collective-permute-start.16 = (f32[2,2,256,128]{3,2,1,0:T(8,128)}, f32[2,2,256,128]{3,2,1,0:T(8,128)S(1)}, u32[]{:S(2)}, u32[]{:S(2)}) collective-permute-start(f32[2,2,256,128]{3,2,1,0:T(8,128)} %get-tuple-element.85), channel_id=1, source_target_pairs={{0,1},{1,2},{2,3},{4,5},{5,6},{6,7},{8,9},{9,10},{10,11},{12,13},{... | collective-permute-start | bytes 1572872 | tf_op jit(solution)/shard_map/ppermute | solution.py:557
  97.1 22.0 %collective-permute-start.17 = (f32[2,2,256,128]{3,2,1,0:T(8,128)}, f32[2,2,256,128]{3,2,1,0:T(8,128)S(1)}, u32[]{:S(2)}, u32[]{:S(2)}) collective-permute-start(f32[2,2,256,128]{3,2,1,0:T(8,128)} %get-tuple-element.86), channel_id=1, source_target_pairs={{1,0},{2,1},{3,2},{5,4},{6,5},{7,6},{9,8},{10,9},{11,10},{13,12},{... | collective-permute-start | bytes 1572872 | tf_op jit(solution)/shard_map/ppermute | solution.py:557
  98.5 1.6 collective-permute-start.1
  100.1 6.6 %collective-permute-start.2 = (f32[128,256]{1,0:T(8,128)S(1)}, f32[128,256]{1,0:T(8,128)S(1)}, u32[]{:S(2)}, u32[]{:S(2)}) collective-permute-start(f32[128,256]{1,0:T(8,128)S(1)} %constant_dynamic-slice_fusion), channel_id=1, source_target_pairs={{0,16},{4,20},{8,24},{12,28},{16,0},{20,4},{24,8},{28,12},{1,17},{... | collective-permute-start | bytes 393224 | tf_op jit(solution)/shard_map/cond/branch_1_fun/ppermute | solution.py:588
  106.8 6.1 %collective-permute-start.3 = (f32[128,256]{1,0:T(8,128)S(1)}, f32[128,256]{1,0:T(8,128)S(1)}, u32[]{:S(2)}, u32[]{:S(2)}) collective-permute-start(f32[128,256]{1,0:T(8,128)S(1)} %dynamic-slice_add_fusion.1), channel_id=1, source_target_pairs={{0,1},{1,0},{2,3},{3,2},{4,5},{5,4},{6,7},{7,6},{8,9},{9,8},{10,11... | collective-permute-start | bytes 393224 | tf_op jit(solution)/shard_map/cond/branch_1_fun/ppermute | solution.py:666
  112.9 6.2 %collective-permute-start.4 = (f32[128,256]{1,0:T(8,128)S(1)}, f32[128,256]{1,0:T(8,128)S(1)}, u32[]{:S(2)}, u32[]{:S(2)}) collective-permute-start(f32[128,256]{1,0:T(8,128)S(1)} %add.38), channel_id=1, source_target_pairs={{0,2},{1,3},{2,0},{3,1},{4,6},{5,7},{6,4},{7,5},{8,10},{9,11},{10,... | collective-permute-start | bytes 393224 | tf_op jit(solution)/shard_map/cond/branch_1_fun/ppermute | solution.py:666
  119.1 32.6 %copy-start.4 = (f32[2,2,128,512]{3,2,1,0:T(8,128)}, f32[2,2,128,512]{3,2,1,0:T(8,128)S(1)}, u32[]{:S(2)}) copy-start(f32[2,2,128,512]{3,2,1,0:T(8,128)S(1)} %collective-permute-done.15.off_quarters) | copy-start | bytes 3145732
  119.1 0.8 copy-start
  119.1 1.0 copy-start.1
  123.8 27.9 %collective-permute-start.18 = (f32[2,2,128,1024]{3,2,1,0:T(8,128)}, f32[2,2,128,1024]{3,2,1,0:T(8,128)S(1)}, u32[]{:S(2)}, u32[]{:S(2)}) collective-permute-start(f32[2,2,128,1024]{3,2,1,0:T(8,128)} %get-tuple-element.89), channel_id=1, source_target_pairs={{0,4},{4,0},{8,12},{12,8},{16,20},{20,16},{24,28},{28,24},{1,5},{5... | collective-permute-start | bytes 6291464 | tf_op jit(solution)/shard_map/ppermute | solution.py:565
  126.5 11.9 %collective-permute-start.20 = (f32[128,256]{1,0:T(8,128)S(1)}, f32[128,256]{1,0:T(8,128)S(1)}, u32[]{:S(2)}, u32[]{:S(2)}) collective-permute-start(f32[128,256]{1,0:T(8,128)S(1)} %get-tuple-element.102), channel_id=1, source_target_pairs={{0,8},{4,12},{8,0},{12,4},{16,24},{20,28},{24,16},{28,20},{1,9},{5... | collective-permute-start | bytes 393224 | tf_op jit(solution)/shard_map/ppermute | solution.py:670
  133.1 12.9 %collective-permute-start.12 = (f32[2,2,256,128]{3,2,1,0:T(8,128)}, f32[2,2,256,128]{3,2,1,0:T(8,128)}, u32[]{:S(2)}, u32[]{:S(2)}) collective-permute-start(f32[2,2,256,128]{3,2,1,0:T(8,128)} %get-tuple-element.73), channel_id=1, source_target_pairs={{0,1},{1,2},{2,3},{4,5},{5,6},{6,7},{8,9},{9,10},{10,11},{12,13},{... | collective-permute-start | bytes 1572872 | tf_op jit(solution)/shard_map/ppermute | solution.py:557
  135.2 15.4 %collective-permute-start.13 = (f32[2,2,256,128]{3,2,1,0:T(8,128)}, f32[2,2,256,128]{3,2,1,0:T(8,128)}, u32[]{:S(2)}, u32[]{:S(2)}) collective-permute-start(f32[2,2,256,128]{3,2,1,0:T(8,128)} %get-tuple-element.74), channel_id=1, source_target_pairs={{1,0},{2,1},{3,2},{5,4},{6,5},{7,6},{9,8},{10,9},{11,10},{13,12},{... | collective-permute-start | bytes 1572872 | tf_op jit(solution)/shard_map/ppermute | solution.py:557
  136.5 15.3 %collective-permute-start.19 = (f32[2,2,128,256]{3,2,1,0:T(8,128)}, f32[2,2,128,256]{3,2,1,0:T(8,128)}, u32[]{:S(2)}, u32[]{:S(2)}) collective-permute-start(f32[2,2,128,256]{3,2,1,0:T(8,128)} %get-tuple-element.90), channel_id=1, source_target_pairs={{4,8},{8,4},{12,16},{16,12},{20,24},{24,20},{5,9},{9,5},{13,17},{1... | collective-permute-start | bytes 1572872 | tf_op jit(solution)/shard_map/ppermute | solution.py:565
  138.4 6.2 %collective-permute-start.21 = (f32[128,256]{1,0:T(8,128)S(1)}, f32[128,256]{1,0:T(8,128)S(1)}, u32[]{:S(2)}, u32[]{:S(2)}) collective-permute-start(f32[128,256]{1,0:T(8,128)S(1)} %add.45), channel_id=1, source_target_pairs={{0,16},{4,20},{8,24},{12,28},{16,0},{20,4},{24,8},{28,12},{1,17},{... | collective-permute-start | bytes 393224 | tf_op jit(solution)/shard_map/ppermute | solution.py:593
  150.5 8.7 %collective-permute-start.22 = (f32[256,256]{1,0:T(8,128)S(1)}, f32[256,256]{1,0:T(8,128)S(1)}, u32[]{:S(2)}, u32[]{:S(2)}) collective-permute-start(f32[256,256]{1,0:T(8,128)S(1)} %pad_maximum_fusion.1), channel_id=1, source_target_pairs={{0,4},{4,0},{8,12},{12,8},{16,20},{20,16},{24,28},{28,24},{1,5},{5... | collective-permute-start | bytes 786440 | tf_op jit(solution)/shard_map/ppermute | solution.py:679
  151.7 1.4 copy-start.3

commit v4 on v3

--- a/solution.py
+++ b/solution.py
@@ -234,11 +234,15 @@
     first = listed(0, jnp.zeros((), jnp.int32))
     count = listed(1, first)
 
-    def amplitude_copy(slot):
-        return pltpu.make_async_copy(amplitudes.at[slot], amps.at[slot], amp_sem.at[slot])
+    part = amplitudes[0].shape[0]
+
+    def amplitude_copy(slot, source):
+        return pltpu.make_async_copy(source, amps.at[slot], amp_sem.at[slot])
 
     def fetch(i, _):
-        amplitude_copy(order[i]).start()
+        slot = order[i]
+        pl.when(slot < part)(lambda: amplitude_copy(slot, amplitudes[0].at[slot]).start())
+        pl.when(slot >= part)(lambda: amplitude_copy(slot, amplitudes[1].at[slot - part]).start())
         return 0
 
     lax.fori_loop(0, count, fetch, 0)
@@ -250,7 +254,7 @@
         slot = order[i]
 
         def amplitude():
-            amplitude_copy(slot).wait()
+            amplitude_copy(slot, amplitudes[0].at[0]).wait()
             return amps[slot]
 
         return Slot(here.start(slot), step * (i >= first).astype(jnp.int32), amplitude, obj, acc)
@@ -282,7 +286,7 @@
 
 
 def inner_body(
-    axes, tx, ty, centers, counts, tile, on, off_quarters, relayed, off_mid, amplitudes, probe_in, table_in,
+    axes, tx, ty, centers, counts, tile, on, off_quarters, relayed, off_mid, early, late, probe_in, table_in,
     g_quarters, g_tile_mid, g_on_mid, g_off_mid, g_probe, obj, acc, probe, table, amps, order, sem, out_sem, amp_sem,
 ):
     width = probe.shape[-1]
@@ -313,13 +317,13 @@
             (acc.at[1, :, :, here.off], g_off_mid),
         ],
     )
-    two_groups(here, (1, 2), 1, waits, stores, amplitudes, amps, amp_sem, order, out_sem, probe, table, obj, acc, g_probe)
+    two_groups(here, (1, 2), 1, waits, stores, (early, late), amps, amp_sem, order, out_sem, probe, table, obj, acc, g_probe)
 
 
 def outer_body(
-    axes, tx, ty, centers, counts, tile, on, off_quarters, relayed, off_ends, left, right, carried, carried_probe, amplitudes, probe_in, table_in,
+    axes, tx, ty, centers, counts, tile, on, off_quarters, relayed, off_ends, left, right, carried, carried_probe, early, late, probe_in, table_in,
     g_tile_ends, g_tile_quarters, g_on_ends, g_on_quarters, g_off_ends, g_off_quarters,
-    g_left, g_left_corners, g_right, g_right_corners, g_probe,
+    g_left, g_right, g_probe,
     obj, acc, probe, table, amps, order, sem, out_sem, amp_sem,
 ):
     width = probe.shape[-1]
@@ -329,9 +333,9 @@
     own = slice(rim, rim + tile_rows)
     one, two = slice(0, rim), slice(rim, width)
     waits, stores = [], []
-    for k, (end, quarter, near, far, half, side, g_side, g_corners) in enumerate((
-        (0, 1, two, slice(0, rim), one, left, g_left, g_left_corners),
-        (3, 2, one, slice(tile_cols - rim, tile_cols), two, right, g_right, g_right_corners),
+    for k, (end, quarter, near, far, half, side, g_side) in enumerate((
+        (0, 1, two, slice(0, rim), one, left, g_left),
+        (3, 2, one, slice(tile_cols - rim, tile_cols), two, right, g_right),
     )):
         first = rim if k == 0 else tile_cols - rim - width
         there = slice(first, first + width)
@@ -353,9 +357,9 @@
             (acc.at[end, :, :, own, near], g_tile_ends.at[:, :, :, half]),
             (acc.at[end, :, :, here.on, near], g_on_ends.at[:, :, :, half]),
             (acc.at[end, :, :, here.off, near], g_off_ends.at[:, :, :, half]),
-            (acc.at[end, :, :, own, half], g_side),
-            (acc.at[end, :, :, here.on, half], g_corners.at[:, :, :rim]),
-            (acc.at[end, :, :, here.off, half], g_corners.at[:, :, rim:]),
+            (acc.at[end, :, :, own, half], g_side.at[:, :, :tile_rows]),
+            (acc.at[end, :, :, here.on, half], g_side.at[:, :, tile_rows : tile_rows + rim]),
+            (acc.at[end, :, :, here.off, half], g_side.at[:, :, tile_rows + rim :]),
             (acc.at[quarter, :, :, own], g_tile_quarters.at[:, :, :, lanes]),
             (acc.at[quarter, :, :, here.on], g_on_quarters.at[:, :, :, lanes]),
             (acc.at[quarter, :, :, here.off], g_off_quarters.at[:, :, :, lanes]),
@@ -364,13 +368,13 @@
     for end in (0, 3):
         acc[end] = jnp.zeros_like(acc[end])
     last_block = (tile_cols + 2 * rim) // width - 2
-    two_groups(here, (0, last_block), 2, waits, stores, amplitudes, amps, amp_sem, order, out_sem, probe, table, obj, acc, g_probe)
+    two_groups(here, (0, last_block), 2, waits, stores, (early, late), amps, amp_sem, order, out_sem, probe, table, obj, acc, g_probe)
 
 
 SMEM = pl.BlockSpec(memory_space=pltpu.SMEM)
 VMEM = pl.BlockSpec(memory_space=pltpu.VMEM)
-HBM = pl.BlockSpec(memory_space=pl.ANY)
-ROOM = pltpu.CompilerParams(vmem_limit_bytes=60 * 2**20)
+HBM = pl.BlockSpec(memory_space=pltpu.HBM)
+ROOM = pltpu.CompilerParams(vmem_limit_bytes=63 * 2**20)
 
 
 def shape(*dims):
@@ -385,25 +389,26 @@
     width = probe.shape[-1]
     padded = (blocks, 2, 2, tile_rows + width, width)
     table = tables(width)
+    slots = sum(part.shape[0] for part in amplitudes)
     return pl.pallas_call(
         functools.partial(body, axes),
         out_shape=tuple(outs) + (jax.ShapeDtypeStruct(probe.shape, F32),),
-        in_specs=[SMEM] * len(scalars) + [HBM] * (len(arrays) + 3),
+        in_specs=[SMEM] * len(scalars) + [HBM] * (len(arrays) + 4),
         out_specs=(HBM,) * len(outs) + (VMEM,),
         scratch_shapes=[
             pltpu.VMEM(padded, F32),
             pltpu.VMEM(padded, F32),
             pltpu.VMEM(probe.shape, F32),
             pltpu.VMEM(table.shape, table.dtype),
-            pltpu.VMEM(amplitudes.shape, F32),
-            pltpu.SMEM((amplitudes.shape[0] + 1,), jnp.int32),
+            pltpu.VMEM((slots, width, width), F32),
+            pltpu.SMEM((slots + 1,), jnp.int32),
             pltpu.SemaphoreType.DMA((32,)),
             pltpu.SemaphoreType.DMA((18,)),
-            pltpu.SemaphoreType.DMA((amplitudes.shape[0],)),
+            pltpu.SemaphoreType.DMA((slots,)),
         ],
         compiler_params=ROOM,
         cost_estimate=costs(2 * 10**10),
-    )(*scalars, *arrays, amplitudes, probe, table)
+    )(*scalars, *arrays, *amplitudes, probe, table)
 
 
 def pack_body(tx, tile, left, right, quarters, mid, sem):
@@ -451,7 +456,7 @@
     )(*scalars, *arrays)
 
 
-def amplitude_body(axes, tx, ty, counts, patterns, pick, out):
+def amplitude_body(axes, first, tx, ty, counts, patterns, pick, out):
     width = patterns.shape[-1]
 
     def work():
@@ -459,21 +464,21 @@
         both = jnp.dot(pick[0], pair(hi, lo, 1), preferred_element_type=F32).astype(jnp.bfloat16)
         out[0] = jnp.dot(both, pick[1:].reshape(-1, width), preferred_element_type=F32)
 
-    pl.when(pl.program_id(0) < counts[tx[0] * axes[1] + ty[0]])(work)
-
-
-def amplitudes_of(axes, scalars, patterns):
+    pl.when(first + pl.program_id(0) < counts[tx[0] * axes[1] + ty[0]])(work)
+
+
+def amplitudes_of(axes, scalars, patterns, first, count):
     width = patterns.shape[-1]
     pick = np.zeros((width, width))
     pick[np.arange(width), np.concatenate([np.arange(0, width, 2), np.arange(1, width, 2)])] = 1
     pick = jnp.asarray(np.stack([pick, pick.T, pick.T]).astype(ml_dtypes.bfloat16))
-    block = pl.BlockSpec((1, width, width), lambda i: (i, 0, 0))
+    block = pl.BlockSpec((1, width, width), lambda i: (first + i, 0, 0))
     return pl.pallas_call(
-        functools.partial(amplitude_body, axes),
-        grid=(patterns.shape[0],),
-        out_shape=jax.ShapeDtypeStruct(patterns.shape, F32),
+        functools.partial(amplitude_body, axes, first),
+        grid=(count,),
+        out_shape=shape(count, width, width),
         in_specs=[SMEM, SMEM, SMEM, block, VMEM],
-        out_specs=block,
+        out_specs=pl.BlockSpec((1, width, width), lambda i: (i, 0, 0)),
         compiler_params=ROOM,
         cost_estimate=costs(10**11),
     )(*scalars, patterns, pick)
@@ -482,13 +487,15 @@
 def merge_body(on_ends, off_ends, left, right, quarters, mid, on, off, sides, sem):
     rim = left.shape[-1]
     width = 2 * rim
+    tile_rows = left.shape[2] - width
+    on_rows, off_rows = slice(tile_rows, tile_rows + rim), slice(tile_rows + rim, tile_rows + width)
     wait_all(run_all([
         (on_ends, on.at[:, :, :, :width]),
         (off_ends, off),
-        (left.at[:, :, :rim], sides.at[0, :, :, :, :rim]),
-        (right.at[:, :, :rim], sides.at[0, :, :, :, rim:]),
-        (left.at[:, :, rim:], sides.at[1, :, :, :, :rim]),
-        (right.at[:, :, rim:], sides.at[1, :, :, :, rim:]),
+        (left.at[:, :, on_rows], sides.at[0, :, :, :, :rim]),
+        (right.at[:, :, on_rows], sides.at[0, :, :, :, rim:]),
+        (left.at[:, :, off_rows], sides.at[1, :, :, :, :rim]),
+        (right.at[:, :, off_rows], sides.at[1, :, :, :, rim:]),
         (quarters, on.at[:, :, :, width : 3 * width]),
         (mid, on.at[:, :, :, 3 * width :]),
     ], sem))
@@ -510,46 +517,79 @@
     )(on_ends, off_ends, left, right, quarters, mid)
 
 
-def total_body(tx, ends, quarters, mid, left, right, on, off_quarters, off_ends, off_mid, out):
-    rim = left.shape[-1]
+def inner_total_body(tx, quarters, mid, on, off_quarters, off_mid, out, total, on_part, off_part, sem):
+    rim = on.shape[2]
+    width = 2 * rim
+    rows = quarters.shape[2]
+    cols = out.shape[3]
+    last = cols - 2 * width
+    middle = slice(width, last)
+    odd = tx[0] % 2
+    wait_all(run_all([
+        (quarters.at[:, :, :, :width], total.at[:, :, :, :width]),
+        (mid, total.at[:, :, :, middle]),
+        (quarters.at[:, :, :, width:], total.at[:, :, :, last:]),
+        (on.at[:, :, :, width : 2 * width], on_part.at[:, :, :, :width]),
+        (on.at[:, :, :, 3 * width :], on_part.at[:, :, :, middle]),
+        (on.at[:, :, :, 2 * width : 3 * width], on_part.at[:, :, :, last:]),
+        (off_quarters.at[:, :, :, :width], off_part.at[:, :, :, :width]),
+        (off_mid, off_part.at[:, :, :, middle]),
+        (off_quarters.at[:, :, :, width:], off_part.at[:, :, :, last:]),
+    ], sem))
+    total[:, :, rows_at((1 - odd) * (rows - rim), rim)] += on_part[...]
+    total[:, :, rows_at(odd * (rows - rim), rim)] += off_part[...]
+    wait_all(run_all([(total, out.at[:, :, :, rim : cols - rim])], sem))
+
+
+def inner_total(tx, parts, tile_shape):
+    rim, width = parts[2].shape[2], 2 * parts[2].shape[2]
+    cols = tile_shape[3] - width
+    return pl.pallas_call(
+        inner_total_body,
+        out_shape=jax.ShapeDtypeStruct(tile_shape, F32),
+        in_specs=[SMEM] + [HBM] * len(parts),
+        out_specs=HBM,
+        scratch_shapes=[pltpu.VMEM(tile_shape[:3] + (cols,), F32)]
+        + [pltpu.VMEM(tile_shape[:2] + (rim, cols), F32)] * 2
+        + [pltpu.SemaphoreType.DMA((9,))],
+        compiler_params=ROOM,
+        cost_estimate=costs(10**8),
+    )(tx, *parts)
+
+
+def end_total_body(tx, ends, left, right, on, off, inner, out, total, sides, on_part, off_part, sem):
+    del inner
+    rim = on.shape[2]
     rows, cols = out.shape[2:]
-    width = 2 * rim
-    one, five = slice(0, rim), slice(cols - rim, cols)
-    two, four = slice(rim, rim + width), slice(cols - rim - width, cols - rim)
-    three = slice(rim + width, cols - rim - width)
     odd = tx[0] % 2
-    out[0, 0, :, one] = ends[0, 0, :, :rim] + left[0, 0]
-    out[0, 0, :, five] = ends[0, 0, :, rim:] + right[0, 0]
-    out[0, 0, :, two] = quarters[0, 0, :, :width]
-    out[0, 0, :, four] = quarters[0, 0, :, width:]
-    out[0, 0, :, three] = mid[0, 0]
-    here = rows_at((1 - odd) * (rows - rim), rim)
-    out[0, 0, here, one] += on[0, 0, :, :rim]
-    out[0, 0, here, five] += on[0, 0, :, rim:width]
-    out[0, 0, here, two] += on[0, 0, :, width : 2 * width]
-    out[0, 0, here, four] += on[0, 0, :, 2 * width : 3 * width]
-    out[0, 0, here, three] += on[0, 0, :, 3 * width :]
-    here = rows_at(odd * (rows - rim), rim)
-    out[0, 0, here, one] += off_ends[0, 0, :, :rim]
-    out[0, 0, here, five] += off_ends[0, 0, :, rim:]
-    out[0, 0, here, two] += off_quarters[0, 0, :, :width]
-    out[0, 0, here, four] += off_quarters[0, 0, :, width:]
-    out[0, 0, here, three] += off_mid[0, 0]
-
-
-def total_of(tx, parts, tile_shape):
-    def block(dims):
-        return pl.BlockSpec((1, 1) + tuple(dims[2:]), lambda i, j: (i, j, 0, 0))
-
+    wait_all(run_all([
+        (ends, total),
+        (left.at[:, :, :rows], sides.at[:, :, :, :rim]),
+        (right.at[:, :, :rows], sides.at[:, :, :, rim:]),
+        (on.at[:, :, :, : 2 * rim], on_part),
+        (off, off_part),
+    ], sem))
+    total[...] += sides[...]
+    total[:, :, rows_at((1 - odd) * (rows - rim), rim)] += on_part[...]
+    total[:, :, rows_at(odd * (rows - rim), rim)] += off_part[...]
+    wait_all(run_all([
+        (total.at[:, :, :, :rim], out.at[:, :, :, :rim]),
+        (total.at[:, :, :, rim:], out.at[:, :, :, cols - rim :]),
+    ], sem))
+
+
+def end_total(tx, parts, inner):
+    ends, off = parts[0], parts[-1]
     return pl.pallas_call(
-        total_body,
-        grid=tile_shape[:2],
-        out_shape=jax.ShapeDtypeStruct(tile_shape, F32),
-        in_specs=[SMEM] + [block(x.shape) for x in parts],
-        out_specs=block(tile_shape),
+        end_total_body,
+        out_shape=jax.ShapeDtypeStruct(inner.shape, F32),
+        in_specs=[SMEM] + [HBM] * (len(parts) + 1),
+        out_specs=HBM,
+        scratch_shapes=[pltpu.VMEM(ends.shape, F32)] * 2 + [pltpu.VMEM(off.shape, F32)] * 2 + [pltpu.SemaphoreType.DMA((5,))],
+        input_output_aliases={len(parts) + 1: 0},
         compiler_params=ROOM,
         cost_estimate=costs(10**11),
-    )(tx, *parts)
+    )(tx, *parts, inner)
 
 
 def along(x, step):
@@ -588,9 +628,10 @@
     return mine + lax.ppermute(other, "tx", pairs)
 
 
-def doubled(flat, apart):
+def doubled(flat, apart, meanwhile):
     bit = (lax.axis_index("tx") // apart) % 2
-    return joined(flat, lax.ppermute(flat, "tx", [(i, i ^ apart) for i in range(lax.axis_size("tx"))]), bit)
+    other = lax.ppermute(flat, "tx", [(i, i ^ apart) for i in range(lax.axis_size("tx"))])
+    return joined(flat, after(other, meanwhile), bit)
 
 
 def joined(flat, other, bit):
@@ -621,17 +662,20 @@
     off_quarters = across(quarters, 1, middle - 1)
     off_mid = across(mid, 1)
     on_shape = shape(slices, 2, rim, tile_cols + width)
-    amplitudes = amplitudes_of(axes, (tx, ty, counts), after(patterns, to_left))
-
-    def strips(tile, left, right):
+    part = patterns.shape[0] // 2
+    early = amplitudes_of(axes, (tx, ty, counts), after(patterns, to_left), 0, part)
+
+    def strips(patterns, tile, left, right):
         on, ends = copies_call(strips_body, (tx,), (tile, left, right), (on_shape, quarters_shape), 10**8)
-        return across(on, 0), ends
-
-    def nothing(tile, left, right):
-        return jnp.zeros(on_shape.shape, F32), jnp.zeros(quarters_shape.shape, F32)
+        late = amplitudes_of(axes, (tx, ty, counts), after(patterns, on), part, part)
+        return across(on, 0), ends, late
+
+    def nothing(patterns, tile, left, right):
+        return jnp.zeros(on_shape.shape, F32), jnp.zeros(quarters_shape.shape, F32), patterns[part:]
 
     relayed = relay_in(carried)
-    on, ends = lax.cond(counts[0] >= 0, strips, nothing, after(tile, amplitudes, carried), left, right)
+    on, ends, late = lax.cond(counts[0] >= 0, strips, nothing, patterns, after(tile, early, carried), left, right)
+    amplitudes = (early, late)
     off_ends = across(ends, 1)
 
     scalars = (tx, ty, centers, counts)
@@ -640,24 +684,20 @@
         (shape(2, slices, 2, full, width), shape(slices, 2, tile_rows, mid_cols), mid_shape, mid_shape), tile_rows,
     )
     back_mid = across(g_off_mid, 1)
-    (
-        g_tile_ends, g_tile_quarters, g_on_ends, g_on_quarters, g_off_ends, g_off_quarters,
-        g_left, g_left_corners, g_right, g_right_corners, g_probe,
-    ) = field_call(
+    g_tile_ends, g_tile_quarters, g_on_ends, g_on_quarters, g_off_ends, g_off_quarters, g_left, g_right, g_probe = field_call(
         outer_body, axes, 4, scalars, (tile, on, off_quarters, relayed, off_ends, left, right, g_quarters, g_probe), amplitudes, probe,
         (
             shape(slices, 2, tile_rows, width), shape(slices, 2, tile_rows, 2 * width), ends_shape, quarters_shape,
-            ends_shape, quarters_shape, column_shape, column_shape, column_shape, column_shape,
+            ends_shape, quarters_shape, side_shape, side_shape,
         ),
         tile_rows,
     )
-    g_off_quarters, g_left_corners, g_right_corners, g_probe, _ = lax.optimization_barrier(
-        (g_off_quarters, g_left_corners, g_right_corners, g_probe, back_mid)
-    )
-    corners_left, corners_right = along(g_right_corners, 1), along(g_left_corners, -1)
+    g_off_quarters, g_left, g_right, g_probe, _ = lax.optimization_barrier((g_off_quarters, g_left, g_right, g_probe, back_mid))
+    from_left, from_right = along(g_right, 1), along(g_left, -1)
     back_quarters = across(g_off_quarters, 1)
     apart = [1] + [2**k for k in range(axes[0].bit_length() - 2, 1, -1)]
     shard = g_probe.size // width // 2 ** len(apart)
+    some = counts[0] >= 0
 
     def shared(flat):
         for step in apart:
@@ -668,20 +708,15 @@
 
     flat = lax.cond(counts[0] >= 0, shared, lambda x: x[:shard], g_probe.reshape(-1, width))
     other = lax.ppermute(flat, "tx", [(i, i ^ 2) for i in range(axes[0])])
-    on_all, off_ends = merged(after(g_on_ends, flat, back_quarters), g_off_ends, corners_left, corners_right, g_on_quarters, g_on_mid)
+    on_all, off_ends = merged(after(g_on_ends, flat, back_quarters), g_off_ends, from_left, from_right, g_on_quarters, g_on_mid)
     back_ends = across(off_ends, 1)
     back_on = across(on_all, 0)
-    from_left, from_right = along(g_right, 1), along(g_left, -1)
+    inner = inner_total(tx, (g_tile_quarters, g_tile_mid, back_on, back_quarters, back_mid), tile.shape)
     flat = after(flat + other, on_all)
     for step in reversed(apart[1:]):
-        flat = doubled(flat, step)
-    flat = after(flat, from_left, from_right)
+        flat = doubled(flat, step, inner)
     last = lax.ppermute(flat, "tx", [(i, i ^ 1) for i in range(axes[0])])
-    inner = total_of(
-        tx,
-        (g_tile_ends, g_tile_quarters, g_tile_mid, from_left, from_right, back_on, back_quarters, back_ends, back_mid),
-        tile.shape,
-    )
+    inner = end_total(tx, (g_tile_ends, from_left, from_right, back_on, back_ends), inner)
     probe_sum = joined(flat, after(last, inner), lax.axis_index("tx") % 2).reshape(probe.shape)
     return (inner, probe_sum)
 

time: 161 us -> 158 us (0.981)
  Pallas kernels: 42.4 us -> 59.7 us
  waiting for transfers between devices: 38.6 us -> 25.3 us
  starting transfers between devices: 71.6 us -> 67.2 us
  local copies, waits for them, and re-layouts: 4.11 us -> 0.93 us
    ppermute x6 -> x4, starting transfers between devices: 28.6 us -> 14.4 us  [along(): lax.ppermute(x, 'ty', [(i, i + step) for i in range(count) if 0 <= i + st...]
    pallas_call x2, Pallas kernels: 20.3 us -> 33 us  [field_call(): pl.pallas_call(functools.partial(body, axes), out_shape=tuple(outs) + (ja...]
    ppermute x2, starting transfers between devices: 3.78 us -> 14.6 us  [shared(): lax.ppermute(flat, 'ty', [(i, i ^ step) for i in range(axes[1])])]
    ppermute x2, starting transfers between devices: 3.11 us -> 10.6 us  [halved(): return mine + lax.ppermute(other, 'tx', pairs)]
    ppermute x1, waiting for transfers between devices: 5.9 us -> 0.01 us  [doubled(): lax.ppermute(flat, 'tx', [(i, i ^ apart) for i in range(lax.axis_size('tx...]
    ppermute x8, starting transfers between devices: 24.8 us -> 19.1 us  [across(): return lax.ppermute(x, 'tx', pairs)]
    ppermute x6 -> x4, waiting for transfers between devices: 5.91 us -> 0.59 us  [along(): lax.ppermute(x, 'ty', [(i, i + step) for i in range(count) if 0 <= i + st...]
    pallas_call x2 -> x4, Pallas kernels: 11.9 us -> 15.9 us  [the longest x2 7.93 us: amplitudes_of(): pl.pallas_call(functools.partial(amplitude_body, axes, first), grid=(coun...]
  transfers between devices with their start and end apart: 23 -> 21, of which waited for: 9 -> 9; matrix products, arithmetic and copies ran while one was open for 1% -> 1% of each run, Pallas kernels for 22% -> 34%
where the time goes in v4:
time: 158 us; the launch traced here: 157 us
  starting transfers between devices  67.2 us (43%)
  Pallas kernels  59.7 us (38%)
  waiting for transfers between devices  25.3 us (16%)
  other arithmetic  1.64 us (1%)
    pallas_call x2, Pallas kernels, field_call(): pl.pallas_call(functools.partial(body, axes), out_shape=tuple(outs) + (ja...  33 us
    ppermute x8, starting transfers between devices, across(): return lax.ppermute(x, 'tx', pairs)  19.1 us
    ppermute x2, starting transfers between devices, shared(): lax.ppermute(flat, 'ty', [(i, i ^ step) for i in range(axes[1])])  14.6 us
    ppermute x4, starting transfers between devices, along(): lax.ppermute(x, 'ty', [(i, i + step) for i in range(count) if 0 <= i + st...  14.4 us
    ppermute x8, waiting for transfers between devices, across(): return lax.ppermute(x, 'tx', pairs)  10.9 us
    ppermute x2, starting transfers between devices, halved(): return mine + lax.ppermute(other, 'tx', pairs)  10.6 us
    pallas_call x2, Pallas kernels, amplitudes_of(): pl.pallas_call(functools.partial(amplitude_body, axes, first), grid=(coun...  7.93 us
    pallas_call x2, Pallas kernels, copies_call(): pl.pallas_call(body, out_shape=tuple(outs), in_specs=[SMEM] * len(scalars...  7.06 us
  transfers between devices with their start and end apart: 21, of which 9 were waited for; matrix products, arithmetic and copies ran while one was open for 1% of the time, Pallas kernels for 34%

profile of v4, /device:TPU:1, one launch (start us, length us, event | category | flops | bytes accessed | tf_op | source)
XLA Modules:
  0.0 156.6 jit_solution(7501950866086172949)
XLA Ops:
  0.6 3.3 %shard_map.107 = (f32[2,2,256,128]{3,2,1,0:T(8,128)}, f32[2,2,256,128]{3,2,1,0:T(8,128)}, f32[2,2,128,512]{3,2,1,0:T(8,128)}, f32[2,2,128,256]{3,2,1,0:T(8,128)}) custom-call(s32[1]{0:T(128)} %bitcast.tx, f32[2,2,256,1024]{3,2,1,0:T(8,128)} %tile.5), custom_call_target="tpu_custom_call" | custom-call | flops 100000000 | bytes 10000000 | tf_op jit(solution)/shard_map/pallas_call | solution.py:448
  4.0 1.6 %collective-permute-start.5 = (f32[2,2,128,512]{3,2,1,0:T(8,128)}, f32[2,2,128,512]{3,2,1,0:T(8,128)}, u32[]{:S(2)}, u32[]{:S(2)}) collective-permute-start(f32[2,2,128,512]{3,2,1,0:T(8,128)} %get-tuple-element.75), channel_id=1, source_target_pairs={{12,28},{16,0},{13,29},{17,1},{14,30},{18,2},{15,31},{19,3}} | collective-permute-start | bytes 3145736 | tf_op jit(solution)/shard_map/ppermute | solution.py:610
  5.6 4.5 %collective-permute-start.8 = (f32[2,2,128,512]{3,2,1,0:T(8,128)}, f32[2,2,128,512]{3,2,1,0:T(8,128)}, u32[]{:S(2)}, u32[]{:S(2)}) collective-permute-start(f32[2,2,128,512]{3,2,1,0:T(8,128)} %get-tuple-element.75), channel_id=1, source_target_pairs={{4,8},{8,4},{20,24},{24,20},{5,9},{9,5},{21,25},{25,21},{6,10},{10... | collective-permute-start | bytes 3145736 | tf_op jit(solution)/shard_map/ppermute | solution.py:605
  10.1 1.3 collective-permute-start.7
  11.4 4.8 %collective-permute-start.6 = (f32[2,2,256,128]{3,2,1,0:T(8,128)}, f32[2,2,256,128]{3,2,1,0:T(8,128)}, u32[]{:S(2)}, u32[]{:S(2)}) collective-permute-start(f32[2,2,256,128]{3,2,1,0:T(8,128)} %get-tuple-element.77), channel_id=1, source_target_pairs={{0,1},{1,2},{2,3},{4,5},{5,6},{6,7},{8,9},{9,10},{10,11},{12,13},{... | collective-permute-start | bytes 1572872 | tf_op jit(solution)/shard_map/ppermute | solution.py:597
  16.2 2.5 %collective-permute-start.11 = (f32[2,2,128,256]{3,2,1,0:T(8,128)}, f32[2,2,128,256]{3,2,1,0:T(8,128)}, u32[]{:S(2)}, u32[]{:S(2)}) collective-permute-start(f32[2,2,128,256]{3,2,1,0:T(8,128)} %get-tuple-element.80), channel_id=1, source_target_pairs={{4,8},{8,4},{12,16},{16,12},{20,24},{24,20},{5,9},{9,5},{13,17},{1... | collective-permute-start | bytes 1572872 | tf_op jit(solution)/shard_map/ppermute | solution.py:605
  18.7 0.0 collective-permute-done.5
  18.7 1.7 %collective-permute-start.9 = (f32[2,2,128,512]{3,2,1,0:T(8,128)}, f32[2,2,128,512]{3,2,1,0:T(8,128)}, u32[]{:S(2)}, u32[]{:S(2)}) collective-permute-start(f32[2,2,128,512]{3,2,1,0:T(8,128)} %collective-permute-done.5), channel_id=1, source_target_pairs={{28,16},{0,12},{29,17},{1,13},{30,18},{2,14},{31,19},{3,15}} | collective-permute-start | bytes 3145736 | tf_op jit(solution)/shard_map/ppermute | solution.py:615
  20.4 4.4 %shard_map.108.early = f32[4,256,256]{2,1,0:T(8,128)} custom-call(s32[1]{0:T(128)} %bitcast.tx, s32[1]{0:T(128)} %bitcast.1.ty, s32[32]{0:T(128)S(1)} %copy-done.2, f32[8,256,256]{2,1,0:T(8,128)} %patterns, bf16[3,256,256]{2,1,0:T(8,128)(2,1)} %constant.97.clone.pick), custom_call_target="tpu_custom_call" | custom-call | flops 99999997952 | bytes 10000000 | tf_op jit(solution)/shard_map/pallas_call | solution.py:476
  24.8 0.7 copy.13.centers
  25.5 0.0 collective-permute-done.7.right
  25.5 0.6 collective-permute-done.6.left
  26.1 0.2 copy-done
  26.3 12.8 %conditional.2 = (f32[2,2,128,1280]{3,2,1,0:T(8,128)}, f32[2,2,128,512]{3,2,1,0:T(8,128)}, f32[4,256,256]{2,1,0:T(8,128)}) conditional(s32[]{:T(128)} %bitcast.2, f32[8,256,256]{2,1,0:T(8,128)} %patterns, (s32[1]{0:T(128)}, f32[2,2,256,1024]{3,2,1,0:T(8,128)}, f32[2,2,256,128]{3,2,1,0:T(8,128)}, f32[2,2,256,128]{3,2,1,0:T(8,128)S(1)}, ...), branch_computations={%region_0.0_spmd, %region_1.0_spmd} | conditional | flops 100099997696 | bytes 30485824 | solution.py:677
  26.3 3.7 %branch_1_fun.2 = (f32[2,2,128,1280]{3,2,1,0:T(8,128)}, f32[2,2,128,512]{3,2,1,0:T(8,128)}) custom-call(s32[1]{0:T(128)} %get-tuple-element.25.tx, f32[2,2,256,1024]{3,2,1,0:T(8,128)} %get-tuple-element.26.tile, f32[2,2,256,128]{3,2,1,0:T(8,128)} %get-tuple-element.27.left, f32[2,2,256,128]{3,2,1,0:T(8,128)S(1)} %get-tuple-element.28.right), custom_call_target="tpu_custom_call" | custom-call | flops 100000000 | bytes 10000000 | tf_op jit(solution)/shard_map/cond/branch_1_fun/pallas_call | solution.py:448
  30.0 4.2 %collective-permute-start = (f32[2,2,128,1280]{3,2,1,0:T(8,128)}, f32[2,2,128,1280]{3,2,1,0:T(8,128)}, u32[]{:S(2)}, u32[]{:S(2)}) collective-permute-start(f32[2,2,128,1280]{3,2,1,0:T(8,128)} %get-tuple-element.29), channel_id=1, source_target_pairs={{0,4},{4,0},{8,12},{12,8},{16,20},{20,16},{24,28},{28,24},{1,5},{5... | collective-permute-start | bytes 7864328 | tf_op jit(solution)/shard_map/cond/branch_1_fun/ppermute | solution.py:605
  34.2 3.5 %branch_1_fun.3 = f32[4,256,256]{2,1,0:T(8,128)} custom-call(s32[1]{0:T(128)} %get-tuple-element.25.tx, s32[1]{0:T(128)} %get-tuple-element.31.ty, s32[32]{0:T(128)S(1)} %get-tuple-element.32.counts, f32[8,256,256]{2,1,0:T(8,128)} %get-tuple-element.34.patterns, bf16[3,256,256]{2,1,0:T(8,128)(2,1)} %get-tuple-element.35.pick), custom_call_target="tpu_custom_call" | custom-call | flops 99999997952 | bytes 10000000 | tf_op jit(solution)/shard_map/cond/branch_1_fun/pallas_call | solution.py:476
  37.8 1.4 collective-permute-done
  39.1 1.9 %collective-permute-start.10 = (f32[2,2,128,512]{3,2,1,0:T(8,128)}, f32[2,2,128,512]{3,2,1,0:T(8,128)}, u32[]{:S(2)}, u32[]{:S(2)}) collective-permute-start(f32[2,2,128,512]{3,2,1,0:T(8,128)} %get-tuple-element.79), channel_id=1, source_target_pairs={{4,8},{8,4},{12,16},{16,12},{20,24},{24,20},{5,9},{9,5},{13,17},{1... | collective-permute-start | bytes 3145736 | tf_op jit(solution)/shard_map/ppermute | solution.py:605
  41.0 0.0 collective-permute-done.11.off_mid
  41.1 17.4 %shard_map.109 = (f32[2,2,2,512,256]{4,3,2,1,0:T(8,128)}, f32[2,2,256,256]{3,2,1,0:T(8,128)}, f32[2,2,128,256]{3,2,1,0:T(8,128)}, f32[2,2,128,256]{3,2,1,0:T(8,128)}, f32[2,256,256]{2,1,0:T(8,128)}) custom-call(s32[1]{0:T(128)} %bitcast.tx, s32[1]{0:T(128)} %bitcast.1.ty, s32[8,2]{1,0:T(8,128)} %copy.13.centers, s32[32]{0:T(128)S(1)} %copy-done.2, ...), custom_call_target="tpu_custom_call" | custom-call | flops 20000000000 | bytes 10000000 | tf_op jit(solution)/shard_map/pallas_call | solution.py:393
  58.5 2.1 %collective-permute-start.12 = (f32[2,2,128,256]{3,2,1,0:T(8,128)}, f32[2,2,128,256]{3,2,1,0:T(8,128)}, u32[]{:S(2)}, u32[]{:S(2)}) collective-permute-start(f32[2,2,128,256]{3,2,1,0:T(8,128)} %get-tuple-element.89), channel_id=1, source_target_pairs={{4,8},{8,4},{12,16},{16,12},{20,24},{24,20},{5,9},{9,5},{13,17},{1... | collective-permute-start | bytes 1572872 | tf_op jit(solution)/shard_map/ppermute | solution.py:605
  60.6 4.9 %collective-permute-done.10.off_ends = f32[2,2,128,512]{3,2,1,0:T(8,128)} collective-permute-done((f32[2,2,128,512]{3,2,1,0:T(8,128)}, f32[2,2,128,512]{3,2,1,0:T(8,128)}, u32[]{:S(2)}, u32[]{:S(2)}) %collective-permute-start.10) | collective-permute-done | bytes 1048608 | tf_op jit(solution)/shard_map/ppermute | solution.py:605
  65.5 15.6 %shard_map.110 = (f32[2,2,256,256]{3,2,1,0:T(8,128)}, f32[2,2,256,512]{3,2,1,0:T(8,128)}, f32[2,2,128,256]{3,2,1,0:T(8,128)}, f32[2,2,128,512]{3,2,1,0:T(8,128)}...) custom-call(s32[1]{0:T(128)} %bitcast.tx, ...), custom_call_target="tpu_custom_call" | custom-call | flops 20000000000 | bytes 10000000 | tf_op jit(solution)/shard_map/pallas_call | solution.py:393
  81.2 1.9 %collective-permute-start.15 = (f32[2,2,128,512]{3,2,1,0:T(8,128)}, f32[2,2,128,512]{3,2,1,0:T(8,128)}, u32[]{:S(2)}, u32[]{:S(2)}) collective-permute-start(f32[2,2,128,512]{3,2,1,0:T(8,128)} %get-tuple-element.94), channel_id=1, source_target_pairs={{4,8},{8,4},{12,16},{16,12},{20,24},{24,20},{5,9},{9,5},{13,17},{1... | collective-permute-start | bytes 3145736 | tf_op jit(solution)/shard_map/ppermute | solution.py:605
  83.1 7.0 %collective-permute-start.13 = (f32[2,2,512,128]{3,2,1,0:T(8,128)}, f32[2,2,512,128]{3,2,1,0:T(8,128)}, u32[]{:S(2)}, u32[]{:S(2)}) collective-permute-start(f32[2,2,512,128]{3,2,1,0:T(8,128)} %get-tuple-element.90), channel_id=1, source_target_pairs={{0,1},{1,2},{2,3},{4,5},{5,6},{6,7},{8,9},{9,10},{10,11},{12,13},{... | collective-permute-start | bytes 3145736 | tf_op jit(solution)/shard_map/ppermute | solution.py:597
  90.1 1.3 collective-permute-start.14
  91.4 38.7 %conditional.3 = (f32[128,256]{1,0:T(8,128)S(1)}) conditional(s32[]{:T(128)} %bitcast.2, f32[512,256]{1,0:T(8,128)S(1)} %bitcast.6, (f32[512,256]{1,0:T(8,128)S(1)}, s32[32]{0:T(128)S(1)}) %tuple.48), branch_computations={%region_2.0_spmd, %region_3.5_spmd} | conditional | flops 196696 | bytes 5374882 | solution.py:709
  91.4 0.1 collective-permute-start.1
  91.6 1.5 collective-permute-done.1
  93.1 10.5 %collective-permute-start.2 = (f32[128,256]{1,0:T(8,128)S(1)}, f32[128,256]{1,0:T(8,128)S(1)}, u32[]{:S(2)}, u32[]{:S(2)}) collective-permute-start(f32[128,256]{1,0:T(8,128)S(1)} %constant_dynamic-slice_fusion), channel_id=1, source_target_pairs={{0,16},{4,20},{8,24},{12,28},{16,0},{20,4},{24,8},{28,12},{1,17},{... | collective-permute-start | bytes 393224 | tf_op jit(solution)/shard_map/cond/branch_1_fun/ppermute | solution.py:628
  103.6 4.5 %collective-permute-done.2 = f32[128,256]{1,0:T(8,128)S(1)} collective-permute-done((f32[128,256]{1,0:T(8,128)S(1)}, f32[128,256]{1,0:T(8,128)S(1)}, u32[]{:S(2)}, u32[]{:S(2)}) %collective-permute-start.2) | collective-permute-done | bytes 131104 | tf_op jit(solution)/shard_map/cond/branch_1_fun/ppermute | solution.py:628
  108.1 6.8 %collective-permute-start.3 = (f32[128,256]{1,0:T(8,128)S(1)}, f32[128,256]{1,0:T(8,128)S(1)}, u32[]{:S(2)}, u32[]{:S(2)}) collective-permute-start(f32[128,256]{1,0:T(8,128)S(1)} %dynamic-slice_add_fusion.1), channel_id=1, source_target_pairs={{0,1},{1,0},{2,3},{3,2},{4,5},{5,4},{6,7},{7,6},{8,9},{9,8},{10,11... | collective-permute-start | bytes 393224 | tf_op jit(solution)/shard_map/cond/branch_1_fun/ppermute | solution.py:706
  114.9 4.1 %collective-permute-done.3 = f32[128,256]{1,0:T(8,128)S(1)} collective-permute-done((f32[128,256]{1,0:T(8,128)S(1)}, f32[128,256]{1,0:T(8,128)S(1)}, u32[]{:S(2)}, u32[]{:S(2)}) %collective-permute-start.3) | collective-permute-done | bytes 131104 | tf_op jit(solution)/shard_map/cond/branch_1_fun/ppermute | solution.py:706
  119.1 7.9 %collective-permute-start.4 = (f32[128,256]{1,0:T(8,128)S(1)}, f32[128,256]{1,0:T(8,128)S(1)}, u32[]{:S(2)}, u32[]{:S(2)}) collective-permute-start(f32[128,256]{1,0:T(8,128)S(1)} %add.38), channel_id=1, source_target_pairs={{0,2},{1,3},{2,0},{3,1},{4,6},{5,7},{6,4},{7,5},{8,10},{9,11},{10,... | collective-permute-start | bytes 393224 | tf_op jit(solution)/shard_map/cond/branch_1_fun/ppermute | solution.py:706
  126.9 0.6 reduce_sum.8
  128.2 1.8 %collective-permute-done.4 = f32[128,256]{1,0:T(8,128)S(1)} collective-permute-done((f32[128,256]{1,0:T(8,128)S(1)}, f32[128,256]{1,0:T(8,128)S(1)}, u32[]{:S(2)}, u32[]{:S(2)}) %collective-permute-start.4) | collective-permute-done | bytes 131104 | tf_op jit(solution)/shard_map/cond/branch_1_fun/ppermute | solution.py:706
  130.1 3.6 %shard_map.111 = (f32[2,2,128,1024]{3,2,1,0:T(8,128)}, f32[2,2,128,256]{3,2,1,0:T(8,128)}) custom-call(f32[2,2,128,256]{3,2,1,0:T(8,128)} %get-tuple-element.95.on_ends, f32[2,2,128,256]{3,2,1,0:T(8,128)} %get-tuple-element.96.off_ends, f32[2,2,512,128]{3,2,1,0:T(8,128)} %collective-permute-done.13.left, f32[2,2,512,128]{3,2,1,0:T(8,128)} %collective-permute-done.14.right, ...), custom_call_target="tpu_custom_call" | custom-call | flops 1000000 | bytes 100000 | tf_op jit(solution)/shard_map/pallas_call | solution.py:509
  133.7 0.1 collective-permute-start.16
  133.8 3.7 %collective-permute-start.18 = (f32[128,256]{1,0:T(8,128)S(1)}, f32[128,256]{1,0:T(8,128)S(1)}, u32[]{:S(2)}, u32[]{:S(2)}) collective-permute-start(f32[128,256]{1,0:T(8,128)S(1)} %get-tuple-element.116), channel_id=1, source_target_pairs={{0,8},{4,12},{8,0},{12,4},{16,24},{20,28},{24,16},{28,20},{1,9},{5... | collective-permute-start | bytes 393224 | tf_op jit(solution)/shard_map/ppermute | solution.py:710
  137.5 1.9 %collective-permute-start.17 = (f32[2,2,128,256]{3,2,1,0:T(8,128)}, f32[2,2,128,256]{3,2,1,0:T(8,128)}, u32[]{:S(2)}, u32[]{:S(2)}) collective-permute-start(f32[2,2,128,256]{3,2,1,0:T(8,128)} %get-tuple-element.100), channel_id=1, source_target_pairs={{4,8},{8,4},{12,16},{16,12},{20,24},{24,20},{5,9},{9,5},{13,17},{1... | collective-permute-start | bytes 1572872 | tf_op jit(solution)/shard_map/ppermute | solution.py:605
  139.4 1.9 %collective-permute-done.18 = f32[128,256]{1,0:T(8,128)S(1)} collective-permute-done((f32[128,256]{1,0:T(8,128)S(1)}, f32[128,256]{1,0:T(8,128)S(1)}, u32[]{:S(2)}, u32[]{:S(2)}) %collective-permute-start.18) | collective-permute-done | bytes 131104 | tf_op jit(solution)/shard_map/ppermute | solution.py:710
  141.3 0.1 collective-permute-start.19
  141.4 5.0 %shard_map.112.inner = f32[2,2,256,1024]{3,2,1,0:T(8,128)} custom-call(s32[1]{0:T(128)} %bitcast.tx, f32[2,2,256,512]{3,2,1,0:T(8,128)} %get-tuple-element.101.quarters, f32[2,2,256,256]{3,2,1,0:T(8,128)} %get-tuple-element.102.mid, f32[2,2,128,1024]{3,2,1,0:T(8,128)} %collective-permute-done.16.on, f32[2,2,128,512]{3,2,1,0:T(8,128)} %collective-permute-done.15.off_quarters, ...), custom_call_target="tpu_custom_call" | custom-call | flops 100000000 | bytes 10000000 | tf_op jit(solution)/shard_map/pallas_call | solution.py:547
  146.5 1.4 collective-permute-start.20
  147.9 4.7 %collective-permute-done.17.off = f32[2,2,128,256]{3,2,1,0:T(8,128)} collective-permute-done((f32[2,2,128,256]{3,2,1,0:T(8,128)}, f32[2,2,128,256]{3,2,1,0:T(8,128)}, u32[]{:S(2)}, u32[]{:S(2)}) %collective-permute-start.17) | collective-permute-done | bytes 524320 | tf_op jit(solution)/shard_map/ppermute | solution.py:605
  152.6 3.1 %shard_map.113 = f32[2,2,256,1024]{3,2,1,0:T(8,128)} custom-call(s32[1]{0:T(128)} %bitcast.tx, f32[2,2,256,256]{3,2,1,0:T(8,128)} %get-tuple-element.84.ends, f32[2,2,512,128]{3,2,1,0:T(8,128)} %collective-permute-done.13.left, f32[2,2,512,128]{3,2,1,0:T(8,128)} %collective-permute-done.14.right, ...), custom_call_target="tpu_custom_call", output_to_operand_aliasing={{}: (6, {})} | custom-call | flops 99999997952 | bytes 10000000 | tf_op jit(solution)/shard_map/pallas_call | solution.py:583
  155.7 0.8 pad_maximum_fusion
  (24 shorter events, 0.3 us)
Async XLA Ops:
  0.6 19.7 %copy-start.2 = (s32[32]{0:T(128)S(1)}, s32[32]{0:T(128)}, u32[]{:S(2)}) copy-start(s32[32]{0:T(128)} %counts.5) | copy-start | bytes 388
  4.0 14.7 %collective-permute-start.5 = (f32[2,2,128,512]{3,2,1,0:T(8,128)}, f32[2,2,128,512]{3,2,1,0:T(8,128)}, u32[]{:S(2)}, u32[]{:S(2)}) collective-permute-start(f32[2,2,128,512]{3,2,1,0:T(8,128)} %get-tuple-element.75), channel_id=1, source_target_pairs={{12,28},{16,0},{13,29},{17,1},{14,30},{18,2},{15,31},{19,3}} | collective-permute-start | bytes 3145736 | tf_op jit(solution)/shard_map/ppermute | solution.py:610
  5.6 35.5 %collective-permute-start.8 = (f32[2,2,128,512]{3,2,1,0:T(8,128)}, f32[2,2,128,512]{3,2,1,0:T(8,128)}, u32[]{:S(2)}, u32[]{:S(2)}) collective-permute-start(f32[2,2,128,512]{3,2,1,0:T(8,128)} %get-tuple-element.75), channel_id=1, source_target_pairs={{4,8},{8,4},{20,24},{24,20},{5,9},{9,5},{21,25},{25,21},{6,10},{10... | collective-permute-start | bytes 3145736 | tf_op jit(solution)/shard_map/ppermute | solution.py:605
  10.1 15.4 %collective-permute-start.7 = (f32[2,2,256,128]{3,2,1,0:T(8,128)}, f32[2,2,256,128]{3,2,1,0:T(8,128)S(1)}, u32[]{:S(2)}, u32[]{:S(2)}) collective-permute-start(f32[2,2,256,128]{3,2,1,0:T(8,128)} %get-tuple-element.73), channel_id=1, source_target_pairs={{1,0},{2,1},{3,2},{5,4},{6,5},{7,6},{9,8},{10,9},{11,10},{13,12},{... | collective-permute-start | bytes 1572872 | tf_op jit(solution)/shard_map/ppermute | solution.py:597
  11.4 14.7 %collective-permute-start.6 = (f32[2,2,256,128]{3,2,1,0:T(8,128)}, f32[2,2,256,128]{3,2,1,0:T(8,128)}, u32[]{:S(2)}, u32[]{:S(2)}) collective-permute-start(f32[2,2,256,128]{3,2,1,0:T(8,128)} %get-tuple-element.77), channel_id=1, source_target_pairs={{0,1},{1,2},{2,3},{4,5},{5,6},{6,7},{8,9},{9,10},{10,11},{12,13},{... | collective-permute-start | bytes 1572872 | tf_op jit(solution)/shard_map/ppermute | solution.py:597
  16.2 24.9 %collective-permute-start.11 = (f32[2,2,128,256]{3,2,1,0:T(8,128)}, f32[2,2,128,256]{3,2,1,0:T(8,128)}, u32[]{:S(2)}, u32[]{:S(2)}) collective-permute-start(f32[2,2,128,256]{3,2,1,0:T(8,128)} %get-tuple-element.80), channel_id=1, source_target_pairs={{4,8},{8,4},{12,16},{16,12},{20,24},{24,20},{5,9},{9,5},{13,17},{1... | collective-permute-start | bytes 1572872 | tf_op jit(solution)/shard_map/ppermute | solution.py:605
  18.7 22.4 %collective-permute-start.9 = (f32[2,2,128,512]{3,2,1,0:T(8,128)}, f32[2,2,128,512]{3,2,1,0:T(8,128)}, u32[]{:S(2)}, u32[]{:S(2)}) collective-permute-start(f32[2,2,128,512]{3,2,1,0:T(8,128)} %collective-permute-done.5), channel_id=1, source_target_pairs={{28,16},{0,12},{29,17},{1,13},{30,18},{2,14},{31,19},{3,15}} | collective-permute-start | bytes 3145736 | tf_op jit(solution)/shard_map/ppermute | solution.py:615
  20.4 4.5 %copy-start.1 = (s32[8,2]{0,1:T(2,128)S(1)}, s32[8,2]{0,1:T(2,128)}, u32[]{:S(2)}) copy-start(s32[8,2]{0,1:T(2,128)} %param.16) | copy-start | bytes 196
  25.5 0.8 copy-start
  30.0 9.1 %collective-permute-start = (f32[2,2,128,1280]{3,2,1,0:T(8,128)}, f32[2,2,128,1280]{3,2,1,0:T(8,128)}, u32[]{:S(2)}, u32[]{:S(2)}) collective-permute-start(f32[2,2,128,1280]{3,2,1,0:T(8,128)} %get-tuple-element.29), channel_id=1, source_target_pairs={{0,4},{4,0},{8,12},{12,8},{16,20},{20,16},{24,28},{28,24},{1,5},{5... | collective-permute-start | bytes 7864328 | tf_op jit(solution)/shard_map/cond/branch_1_fun/ppermute | solution.py:605
  39.1 26.4 %collective-permute-start.10 = (f32[2,2,128,512]{3,2,1,0:T(8,128)}, f32[2,2,128,512]{3,2,1,0:T(8,128)}, u32[]{:S(2)}, u32[]{:S(2)}) collective-permute-start(f32[2,2,128,512]{3,2,1,0:T(8,128)} %get-tuple-element.79), channel_id=1, source_target_pairs={{4,8},{8,4},{12,16},{16,12},{20,24},{24,20},{5,9},{9,5},{13,17},{1... | collective-permute-start | bytes 3145736 | tf_op jit(solution)/shard_map/ppermute | solution.py:605
  58.5 22.6 %collective-permute-start.12 = (f32[2,2,128,256]{3,2,1,0:T(8,128)}, f32[2,2,128,256]{3,2,1,0:T(8,128)}, u32[]{:S(2)}, u32[]{:S(2)}) collective-permute-start(f32[2,2,128,256]{3,2,1,0:T(8,128)} %get-tuple-element.89), channel_id=1, source_target_pairs={{4,8},{8,4},{12,16},{16,12},{20,24},{24,20},{5,9},{9,5},{13,17},{1... | collective-permute-start | bytes 1572872 | tf_op jit(solution)/shard_map/ppermute | solution.py:605
  81.2 48.9 %collective-permute-start.15 = (f32[2,2,128,512]{3,2,1,0:T(8,128)}, f32[2,2,128,512]{3,2,1,0:T(8,128)}, u32[]{:S(2)}, u32[]{:S(2)}) collective-permute-start(f32[2,2,128,512]{3,2,1,0:T(8,128)} %get-tuple-element.94), channel_id=1, source_target_pairs={{4,8},{8,4},{12,16},{16,12},{20,24},{24,20},{5,9},{9,5},{13,17},{1... | collective-permute-start | bytes 3145736 | tf_op jit(solution)/shard_map/ppermute | solution.py:605
  83.1 47.0 %collective-permute-start.13 = (f32[2,2,512,128]{3,2,1,0:T(8,128)}, f32[2,2,512,128]{3,2,1,0:T(8,128)}, u32[]{:S(2)}, u32[]{:S(2)}) collective-permute-start(f32[2,2,512,128]{3,2,1,0:T(8,128)} %get-tuple-element.90), channel_id=1, source_target_pairs={{0,1},{1,2},{2,3},{4,5},{5,6},{6,7},{8,9},{9,10},{10,11},{12,13},{... | collective-permute-start | bytes 3145736 | tf_op jit(solution)/shard_map/ppermute | solution.py:597
  90.1 40.0 %collective-permute-start.14 = (f32[2,2,512,128]{3,2,1,0:T(8,128)}, f32[2,2,512,128]{3,2,1,0:T(8,128)}, u32[]{:S(2)}, u32[]{:S(2)}) collective-permute-start(f32[2,2,512,128]{3,2,1,0:T(8,128)} %get-tuple-element.91), channel_id=1, source_target_pairs={{1,0},{2,1},{3,2},{5,4},{6,5},{7,6},{9,8},{10,9},{11,10},{13,12},{... | collective-permute-start | bytes 3145736 | tf_op jit(solution)/shard_map/ppermute | solution.py:597
  91.4 1.6 %collective-permute-start.1 = (f32[256,256]{1,0:T(8,128)S(1)}, f32[256,256]{1,0:T(8,128)S(1)}, u32[]{:S(2)}, u32[]{:S(2)}) collective-permute-start(f32[256,256]{1,0:T(8,128)S(1)} %constant_dynamic-slice_fusion.1), channel_id=1, source_target_pairs={{0,4},{4,0},{8,12},{12,8},{16,20},{20,16},{24,28},{28,24},{1,5},{5... | collective-permute-start | bytes 786440 | tf_op jit(solution)/shard_map/cond/branch_1_fun/ppermute | solution.py:628
  93.1 15.0 %collective-permute-start.2 = (f32[128,256]{1,0:T(8,128)S(1)}, f32[128,256]{1,0:T(8,128)S(1)}, u32[]{:S(2)}, u32[]{:S(2)}) collective-permute-start(f32[128,256]{1,0:T(8,128)S(1)} %constant_dynamic-slice_fusion), channel_id=1, source_target_pairs={{0,16},{4,20},{8,24},{12,28},{16,0},{20,4},{24,8},{28,12},{1,17},{... | collective-permute-start | bytes 393224 | tf_op jit(solution)/shard_map/cond/branch_1_fun/ppermute | solution.py:628
  108.1 10.9 %collective-permute-start.3 = (f32[128,256]{1,0:T(8,128)S(1)}, f32[128,256]{1,0:T(8,128)S(1)}, u32[]{:S(2)}, u32[]{:S(2)}) collective-permute-start(f32[128,256]{1,0:T(8,128)S(1)} %dynamic-slice_add_fusion.1), channel_id=1, source_target_pairs={{0,1},{1,0},{2,3},{3,2},{4,5},{5,4},{6,7},{7,6},{8,9},{9,8},{10,11... | collective-permute-start | bytes 393224 | tf_op jit(solution)/shard_map/cond/branch_1_fun/ppermute | solution.py:706
  119.1 11.0 %collective-permute-start.4 = (f32[128,256]{1,0:T(8,128)S(1)}, f32[128,256]{1,0:T(8,128)S(1)}, u32[]{:S(2)}, u32[]{:S(2)}) collective-permute-start(f32[128,256]{1,0:T(8,128)S(1)} %add.38), channel_id=1, source_target_pairs={{0,2},{1,3},{2,0},{3,1},{4,6},{5,7},{6,4},{7,5},{8,10},{9,11},{10,... | collective-permute-start | bytes 393224 | tf_op jit(solution)/shard_map/cond/branch_1_fun/ppermute | solution.py:706
  133.7 7.7 %collective-permute-start.16 = (f32[2,2,128,1024]{3,2,1,0:T(8,128)}, f32[2,2,128,1024]{3,2,1,0:T(8,128)}, u32[]{:S(2)}, u32[]{:S(2)}) collective-permute-start(f32[2,2,128,1024]{3,2,1,0:T(8,128)} %get-tuple-element.99), channel_id=1, source_target_pairs={{0,4},{4,0},{8,12},{12,8},{16,20},{20,16},{24,28},{28,24},{1,5},{5... | collective-permute-start | bytes 6291464 | tf_op jit(solution)/shard_map/ppermute | solution.py:605
  133.8 7.5 %collective-permute-start.18 = (f32[128,256]{1,0:T(8,128)S(1)}, f32[128,256]{1,0:T(8,128)S(1)}, u32[]{:S(2)}, u32[]{:S(2)}) collective-permute-start(f32[128,256]{1,0:T(8,128)S(1)} %get-tuple-element.116), channel_id=1, source_target_pairs={{0,8},{4,12},{8,0},{12,4},{16,24},{20,28},{24,16},{28,20},{1,9},{5... | collective-permute-start | bytes 393224 | tf_op jit(solution)/shard_map/ppermute | solution.py:710
  137.5 15.1 %collective-permute-start.17 = (f32[2,2,128,256]{3,2,1,0:T(8,128)}, f32[2,2,128,256]{3,2,1,0:T(8,128)}, u32[]{:S(2)}, u32[]{:S(2)}) collective-permute-start(f32[2,2,128,256]{3,2,1,0:T(8,128)} %get-tuple-element.100), channel_id=1, source_target_pairs={{4,8},{8,4},{12,16},{16,12},{20,24},{24,20},{5,9},{9,5},{13,17},{1... | collective-permute-start | bytes 1572872 | tf_op jit(solution)/shard_map/ppermute | solution.py:605
  141.3 5.1 %collective-permute-start.19 = (f32[128,256]{1,0:T(8,128)S(1)}, f32[128,256]{1,0:T(8,128)S(1)}, u32[]{:S(2)}, u32[]{:S(2)}) collective-permute-start(f32[128,256]{1,0:T(8,128)S(1)} %add.45), channel_id=1, source_target_pairs={{0,16},{4,20},{8,24},{12,28},{16,0},{20,4},{24,8},{28,12},{1,17},{... | collective-permute-start | bytes 393224 | tf_op jit(solution)/shard_map/ppermute | solution.py:633
  146.5 9.2 %collective-permute-start.20 = (f32[256,256]{1,0:T(8,128)S(1)}, f32[256,256]{1,0:T(8,128)S(1)}, u32[]{:S(2)}, u32[]{:S(2)}) collective-permute-start(f32[256,256]{1,0:T(8,128)S(1)} %pad_maximum_fusion.1), channel_id=1, source_target_pairs={{0,4},{4,0},{8,12},{12,8},{16,20},{20,16},{24,28},{28,24},{1,5},{5... | collective-permute-start | bytes 786440 | tf_op jit(solution)/shard_map/ppermute | solution.py:718

commit v5 on v4

--- a/solution.py
+++ b/solution.py
@@ -517,7 +517,7 @@
     )(on_ends, off_ends, left, right, quarters, mid)
 
 
-def inner_total_body(tx, quarters, mid, on, off_quarters, off_mid, out, total, on_part, off_part, sem):
+def inner_total_body(axes, tx, quarters, mid, on, off_quarters, far_quarters, off_mid, out, total, on_part, off_part, sem):
     rim = on.shape[2]
     width = 2 * rim
     rows = quarters.shape[2]
@@ -532,20 +532,22 @@
         (on.at[:, :, :, width : 2 * width], on_part.at[:, :, :, :width]),
         (on.at[:, :, :, 3 * width :], on_part.at[:, :, :, middle]),
         (on.at[:, :, :, 2 * width : 3 * width], on_part.at[:, :, :, last:]),
-        (off_quarters.at[:, :, :, :width], off_part.at[:, :, :, :width]),
         (off_mid, off_part.at[:, :, :, middle]),
-        (off_quarters.at[:, :, :, width:], off_part.at[:, :, :, last:]),
     ], sem))
+    is_far = (tx[0] == axes[0] // 2) | (tx[0] == axes[0] // 2 - 1)
+    for here, source in ((is_far, far_quarters), (jnp.logical_not(is_far), off_quarters)):
+        pairs = [(source.at[:, :, :, :width], off_part.at[:, :, :, :width]), (source.at[:, :, :, width:], off_part.at[:, :, :, last:])]
+        pl.when(here)(lambda pairs=pairs: wait_all(run_all(pairs, sem)))
     total[:, :, rows_at((1 - odd) * (rows - rim), rim)] += on_part[...]
     total[:, :, rows_at(odd * (rows - rim), rim)] += off_part[...]
     wait_all(run_all([(total, out.at[:, :, :, rim : cols - rim])], sem))
 
 
-def inner_total(tx, parts, tile_shape):
+def inner_total(axes, tx, parts, tile_shape):
     rim, width = parts[2].shape[2], 2 * parts[2].shape[2]
     cols = tile_shape[3] - width
     return pl.pallas_call(
-        inner_total_body,
+        functools.partial(inner_total_body, axes),
         out_shape=jax.ShapeDtypeStruct(tile_shape, F32),
         in_specs=[SMEM] + [HBM] * len(parts),
         out_specs=HBM,
@@ -694,24 +696,27 @@
     )
     g_off_quarters, g_left, g_right, g_probe, _ = lax.optimization_barrier((g_off_quarters, g_left, g_right, g_probe, back_mid))
     from_left, from_right = along(g_right, 1), along(g_left, -1)
-    back_quarters = across(g_off_quarters, 1)
+    back_quarters = across(g_off_quarters, 1, middle - 1)
     apart = [1] + [2**k for k in range(axes[0].bit_length() - 2, 1, -1)]
     shard = g_probe.size // width // 2 ** len(apart)
     some = counts[0] >= 0
 
-    def shared(flat):
+    def shared(flat, quarters):
         for step in apart:
             flat = halved(flat, step)
+        far = lax.ppermute(after(quarters, flat), "tx", [(middle - 1, middle), (middle, middle - 1)])
         for step in (2**k for k in range(axes[1].bit_length() - 1)):
             flat = flat + lax.ppermute(flat, "ty", [(i, i ^ step) for i in range(axes[1])])
-        return flat / jnp.sqrt(jnp.maximum(jnp.sum(counts), 1).astype(F32))
-
-    flat = lax.cond(counts[0] >= 0, shared, lambda x: x[:shard], g_probe.reshape(-1, width))
+        return flat / jnp.sqrt(jnp.maximum(jnp.sum(counts), 1).astype(F32)), far
+
+    flat, far_quarters = lax.cond(
+        counts[0] >= 0, shared, lambda x, quarters: (x[:shard], quarters), g_probe.reshape(-1, width), g_off_quarters
+    )
     other = lax.ppermute(flat, "tx", [(i, i ^ 2) for i in range(axes[0])])
     on_all, off_ends = merged(after(g_on_ends, flat, back_quarters), g_off_ends, from_left, from_right, g_on_quarters, g_on_mid)
     back_ends = across(off_ends, 1)
     back_on = across(on_all, 0)
-    inner = inner_total(tx, (g_tile_quarters, g_tile_mid, back_on, back_quarters, back_mid), tile.shape)
+    inner = inner_total(axes, tx, (g_tile_quarters, g_tile_mid, back_on, back_quarters, far_quarters, back_mid), tile.shape)
     flat = after(flat + other, on_all)
     for step in reversed(apart[1:]):
         flat = doubled(flat, step, inner)

time: 158 us -> 153 us (0.968); the launches traced: 157 us -> 154 us
  Pallas kernels: 59.7 us -> 47.3 us
  starting transfers between devices: 67.2 us -> 72.1 us
  waiting for transfers between devices: 25.3 us -> 30.1 us
    pallas_call x2, Pallas kernels: 33 us -> 20.6 us  [field_call(): pl.pallas_call(functools.partial(body, axes), out_shape=tuple(outs) + (ja...]
    ppermute x2, starting transfers between devices: 14.6 us -> 6.56 us  [shared(): lax.ppermute(flat, 'ty', [(i, i ^ step) for i in range(axes[1])])]
    ppermute x1, starting transfers between devices: 0.07 us -> 6.82 us  [doubled(): lax.ppermute(flat, 'tx', [(i, i ^ apart) for i in range(lax.axis_size('tx...]
    ppermute x4, starting transfers between devices: 14.4 us -> 19.4 us  [along(): lax.ppermute(x, 'ty', [(i, i + step) for i in range(count) if 0 <= i + st...]
    ppermute x2, starting transfers between devices: 10.6 us -> 7.46 us  [halved(): return mine + lax.ppermute(other, 'tx', pairs)]
    ppermute x8, starting transfers between devices: 19.1 us -> 22 us  [across(): return lax.ppermute(x, 'tx', pairs)]
    ppermute x1, waiting for transfers between devices: 0.01 us -> 1.84 us  [doubled(): lax.ppermute(flat, 'tx', [(i, i ^ apart) for i in range(lax.axis_size('tx...]
    ppermute x0 -> x1, starting transfers between devices: none -> 1.67 us  [shared(): lax.ppermute(after(quarters, flat), 'tx', [(middle - 1, middle), (middle,...]
  transfers between devices with their start and end apart: 21 -> 22, of which waited for: 9 -> 9; matrix products, arithmetic and copies ran while one was open for 1% -> 1% of each run, Pallas kernels for 34% -> 26%
where the time goes in v5:
time: 153 us; the launch traced here: 154 us
  starting transfers between devices  72.1 us (47%)
  Pallas kernels  47.3 us (31%)
  waiting for transfers between devices  30.1 us (20%)
  other arithmetic  1.64 us (1%)
    ppermute x8, starting transfers between devices, across(): return lax.ppermute(x, 'tx', pairs)  22 us
    pallas_call x2, Pallas kernels, field_call(): pl.pallas_call(functools.partial(body, axes), out_shape=tuple(outs) + (ja...  20.6 us
    ppermute x4, starting transfers between devices, along(): lax.ppermute(x, 'ty', [(i, i + step) for i in range(count) if 0 <= i + st...  19.4 us
    ppermute x8, waiting for transfers between devices, across(): return lax.ppermute(x, 'tx', pairs)  12.4 us
    ppermute x2, waiting for transfers between devices, shared(): lax.ppermute(flat, 'ty', [(i, i ^ step) for i in range(axes[1])])  7.5 us
    ppermute x2, starting transfers between devices, halved(): return mine + lax.ppermute(other, 'tx', pairs)  7.46 us
    pallas_call x2, Pallas kernels, amplitudes_of(): pl.pallas_call(functools.partial(amplitude_body, axes, first), grid=(coun...  7.06 us
    pallas_call x2, Pallas kernels, copies_call(): pl.pallas_call(body, out_shape=tuple(outs), in_specs=[SMEM] * len(scalars...  7.05 us
  transfers between devices with their start and end apart: 22, of which 9 were waited for; matrix products, arithmetic and copies ran while one was open for 1% of the time, Pallas kernels for 26%

profile of v5, /device:TPU:1, one launch (start us, length us, event | category | flops | bytes accessed | tf_op | source)
XLA Modules:
  0.0 153.6 jit_solution(9531210709476122204)
XLA Ops:
  0.6 3.3 %shard_map.107 = (f32[2,2,256,128]{3,2,1,0:T(8,128)}, f32[2,2,256,128]{3,2,1,0:T(8,128)}, f32[2,2,128,512]{3,2,1,0:T(8,128)}, f32[2,2,128,256]{3,2,1,0:T(8,128)}) custom-call(s32[1]{0:T(128)} %bitcast.tx, f32[2,2,256,1024]{3,2,1,0:T(8,128)} %tile.5), custom_call_target="tpu_custom_call" | custom-call | flops 100000000 | bytes 10000000 | tf_op jit(solution)/shard_map/pallas_call | solution.py:448
  4.0 1.6 %collective-permute-start.6 = (f32[2,2,128,512]{3,2,1,0:T(8,128)}, f32[2,2,128,512]{3,2,1,0:T(8,128)}, u32[]{:S(2)}, u32[]{:S(2)}) collective-permute-start(f32[2,2,128,512]{3,2,1,0:T(8,128)} %get-tuple-element.83), channel_id=1, source_target_pairs={{12,28},{16,0},{13,29},{17,1},{14,30},{18,2},{15,31},{19,3}} | collective-permute-start | bytes 3145736 | tf_op jit(solution)/shard_map/ppermute | solution.py:612
  5.6 4.5 %collective-permute-start.9 = (f32[2,2,128,512]{3,2,1,0:T(8,128)}, f32[2,2,128,512]{3,2,1,0:T(8,128)}, u32[]{:S(2)}, u32[]{:S(2)}) collective-permute-start(f32[2,2,128,512]{3,2,1,0:T(8,128)} %get-tuple-element.83), channel_id=1, source_target_pairs={{4,8},{8,4},{20,24},{24,20},{5,9},{9,5},{21,25},{25,21},{6,10},{10... | collective-permute-start | bytes 3145736 | tf_op jit(solution)/shard_map/ppermute | solution.py:607
  10.1 1.3 collective-permute-start.8
  11.4 4.8 %collective-permute-start.7 = (f32[2,2,256,128]{3,2,1,0:T(8,128)}, f32[2,2,256,128]{3,2,1,0:T(8,128)}, u32[]{:S(2)}, u32[]{:S(2)}) collective-permute-start(f32[2,2,256,128]{3,2,1,0:T(8,128)} %get-tuple-element.85), channel_id=1, source_target_pairs={{0,1},{1,2},{2,3},{4,5},{5,6},{6,7},{8,9},{9,10},{10,11},{12,13},{... | collective-permute-start | bytes 1572872 | tf_op jit(solution)/shard_map/ppermute | solution.py:599
  16.2 2.5 %collective-permute-start.12 = (f32[2,2,128,256]{3,2,1,0:T(8,128)}, f32[2,2,128,256]{3,2,1,0:T(8,128)}, u32[]{:S(2)}, u32[]{:S(2)}) collective-permute-start(f32[2,2,128,256]{3,2,1,0:T(8,128)} %get-tuple-element.88), channel_id=1, source_target_pairs={{4,8},{8,4},{12,16},{16,12},{20,24},{24,20},{5,9},{9,5},{13,17},{1... | collective-permute-start | bytes 1572872 | tf_op jit(solution)/shard_map/ppermute | solution.py:607
  18.7 1.7 %collective-permute-start.10 = (f32[2,2,128,512]{3,2,1,0:T(8,128)}, f32[2,2,128,512]{3,2,1,0:T(8,128)}, u32[]{:S(2)}, u32[]{:S(2)}) collective-permute-start(f32[2,2,128,512]{3,2,1,0:T(8,128)} %collective-permute-done.6), channel_id=1, source_target_pairs={{28,16},{0,12},{29,17},{1,13},{30,18},{2,14},{31,19},{3,15}} | collective-permute-start | bytes 3145736 | tf_op jit(solution)/shard_map/ppermute | solution.py:617
  20.4 3.5 %shard_map.108.early = f32[4,256,256]{2,1,0:T(8,128)} custom-call(s32[1]{0:T(128)} %bitcast.tx, s32[1]{0:T(128)} %bitcast.1.ty, s32[32]{0:T(128)S(1)} %copy-done.2, f32[8,256,256]{2,1,0:T(8,128)} %patterns, bf16[3,256,256]{2,1,0:T(8,128)(2,1)} %constant.97.clone.pick), custom_call_target="tpu_custom_call" | custom-call | flops 99999997952 | bytes 10000000 | tf_op jit(solution)/shard_map/pallas_call | solution.py:476
  24.0 0.7 copy.13.centers
  24.7 0.0 collective-permute-done.8.right
  24.7 1.4 collective-permute-done.7.left
  26.1 12.6 %conditional.2 = (f32[2,2,128,1280]{3,2,1,0:T(8,128)}, f32[2,2,128,512]{3,2,1,0:T(8,128)}, f32[4,256,256]{2,1,0:T(8,128)}) conditional(s32[]{:T(128)} %bitcast.2, f32[8,256,256]{2,1,0:T(8,128)} %patterns, (s32[1]{0:T(128)}, f32[2,2,256,1024]{3,2,1,0:T(8,128)}, f32[2,2,256,128]{3,2,1,0:T(8,128)}, f32[2,2,256,128]{3,2,1,0:T(8,128)S(1)}, ...), branch_computations={%region_0.0_spmd, %region_1.0_spmd} | conditional | flops 100099997696 | bytes 30485824 | solution.py:679
  26.1 3.7 %branch_1_fun.2 = (f32[2,2,128,1280]{3,2,1,0:T(8,128)}, f32[2,2,128,512]{3,2,1,0:T(8,128)}) custom-call(s32[1]{0:T(128)} %get-tuple-element.27.tx, f32[2,2,256,1024]{3,2,1,0:T(8,128)} %get-tuple-element.28.tile, f32[2,2,256,128]{3,2,1,0:T(8,128)} %get-tuple-element.29.left, f32[2,2,256,128]{3,2,1,0:T(8,128)S(1)} %get-tuple-element.30.right), custom_call_target="tpu_custom_call" | custom-call | flops 100000000 | bytes 10000000 | tf_op jit(solution)/shard_map/cond/branch_1_fun/pallas_call | solution.py:448
  29.8 4.0 %collective-permute-start = (f32[2,2,128,1280]{3,2,1,0:T(8,128)}, f32[2,2,128,1280]{3,2,1,0:T(8,128)}, u32[]{:S(2)}, u32[]{:S(2)}) collective-permute-start(f32[2,2,128,1280]{3,2,1,0:T(8,128)} %get-tuple-element.31), channel_id=1, source_target_pairs={{0,4},{4,0},{8,12},{12,8},{16,20},{20,16},{24,28},{28,24},{1,5},{5... | collective-permute-start | bytes 7864328 | tf_op jit(solution)/shard_map/cond/branch_1_fun/ppermute | solution.py:607
  33.8 3.5 %branch_1_fun.3 = f32[4,256,256]{2,1,0:T(8,128)} custom-call(s32[1]{0:T(128)} %get-tuple-element.27.tx, s32[1]{0:T(128)} %get-tuple-element.33.ty, s32[32]{0:T(128)S(1)} %get-tuple-element.34.counts, f32[8,256,256]{2,1,0:T(8,128)} %get-tuple-element.36.patterns, bf16[3,256,256]{2,1,0:T(8,128)(2,1)} %get-tuple-element.37.pick), custom_call_target="tpu_custom_call" | custom-call | flops 99999997952 | bytes 10000000 | tf_op jit(solution)/shard_map/cond/branch_1_fun/pallas_call | solution.py:476
  37.3 1.4 collective-permute-done
  38.7 1.9 %collective-permute-start.11 = (f32[2,2,128,512]{3,2,1,0:T(8,128)}, f32[2,2,128,512]{3,2,1,0:T(8,128)}, u32[]{:S(2)}, u32[]{:S(2)}) collective-permute-start(f32[2,2,128,512]{3,2,1,0:T(8,128)} %get-tuple-element.87), channel_id=1, source_target_pairs={{4,8},{8,4},{12,16},{16,12},{20,24},{24,20},{5,9},{9,5},{13,17},{1... | collective-permute-start | bytes 3145736 | tf_op jit(solution)/shard_map/ppermute | solution.py:607
  40.6 0.0 collective-permute-done.12.off_mid
  40.6 0.0 collective-permute-done.9.off_quarters
  40.6 9.3 %shard_map.109 = (f32[2,2,2,512,256]{4,3,2,1,0:T(8,128)}, f32[2,2,256,256]{3,2,1,0:T(8,128)}, f32[2,2,128,256]{3,2,1,0:T(8,128)}, f32[2,2,128,256]{3,2,1,0:T(8,128)}, f32[2,256,256]{2,1,0:T(8,128)}) custom-call(s32[1]{0:T(128)} %bitcast.tx, s32[1]{0:T(128)} %bitcast.1.ty, s32[8,2]{1,0:T(8,128)} %copy.13.centers, s32[32]{0:T(128)S(1)} %copy-done.2, ...), custom_call_target="tpu_custom_call" | custom-call | flops 20000000000 | bytes 10000000 | tf_op jit(solution)/shard_map/pallas_call | solution.py:393
  50.0 3.8 %collective-permute-start.13 = (f32[2,2,128,256]{3,2,1,0:T(8,128)}, f32[2,2,128,256]{3,2,1,0:T(8,128)}, u32[]{:S(2)}, u32[]{:S(2)}) collective-permute-start(f32[2,2,128,256]{3,2,1,0:T(8,128)} %get-tuple-element.97), channel_id=1, source_target_pairs={{4,8},{8,4},{12,16},{16,12},{20,24},{24,20},{5,9},{9,5},{13,17},{1... | collective-permute-start | bytes 1572872 | tf_op jit(solution)/shard_map/ppermute | solution.py:607
  53.8 11.0 %collective-permute-done.11.off_ends = f32[2,2,128,512]{3,2,1,0:T(8,128)} collective-permute-done((f32[2,2,128,512]{3,2,1,0:T(8,128)}, f32[2,2,128,512]{3,2,1,0:T(8,128)}, u32[]{:S(2)}, u32[]{:S(2)}) %collective-permute-start.11) | collective-permute-done | bytes 1048608 | tf_op jit(solution)/shard_map/ppermute | solution.py:607
  64.8 11.3 %shard_map.110 = (f32[2,2,256,256]{3,2,1,0:T(8,128)}, f32[2,2,256,512]{3,2,1,0:T(8,128)}, f32[2,2,128,256]{3,2,1,0:T(8,128)}, f32[2,2,128,512]{3,2,1,0:T(8,128)}...) custom-call(s32[1]{0:T(128)} %bitcast.tx, ...), custom_call_target="tpu_custom_call" | custom-call | flops 20000000000 | bytes 10000000 | tf_op jit(solution)/shard_map/pallas_call | solution.py:393
  76.2 1.9 %collective-permute-start.16 = (f32[2,2,128,512]{3,2,1,0:T(8,128)}, f32[2,2,128,512]{3,2,1,0:T(8,128)}, u32[]{:S(2)}, u32[]{:S(2)}) collective-permute-start(f32[2,2,128,512]{3,2,1,0:T(8,128)} %get-tuple-element.102), channel_id=1, source_target_pairs={{4,8},{8,4},{20,24},{24,20},{5,9},{9,5},{21,25},{25,21},{6,10},{10... | collective-permute-start | bytes 3145736 | tf_op jit(solution)/shard_map/ppermute | solution.py:607
  78.1 12.0 %collective-permute-start.14 = (f32[2,2,512,128]{3,2,1,0:T(8,128)}, f32[2,2,512,128]{3,2,1,0:T(8,128)}, u32[]{:S(2)}, u32[]{:S(2)}) collective-permute-start(f32[2,2,512,128]{3,2,1,0:T(8,128)} %get-tuple-element.98), channel_id=1, source_target_pairs={{0,1},{1,2},{2,3},{4,5},{5,6},{6,7},{8,9},{9,10},{10,11},{12,13},{... | collective-permute-start | bytes 3145736 | tf_op jit(solution)/shard_map/ppermute | solution.py:599
  90.1 1.3 collective-permute-start.15
  91.4 29.8 %conditional.3 = (f32[128,256]{1,0:T(8,128)S(1)}, f32[2,2,128,512]{3,2,1,0:T(8,128)}) conditional(s32[]{:T(128)} %bitcast.2, (f32[512,256]{1,0:T(8,128)S(1)}, f32[2,2,128,512]{3,2,1,0:T(8,128)}) %tuple.50, (f32[512,256]{1,0:T(8,128)S(1)}, s32[32]{0:T(128)S(1)}, f32[2,2,128,512]{3,2,1,0:T(8,128)}) %tuple.53), branch_computations={%region_2.0_spmd, %region_3.5_spmd} | conditional | flops 196696 | bytes 9569234 | solution.py:712
  91.5 0.1 collective-permute-start.1
  91.6 1.5 collective-permute-done.1
  93.2 7.4 %collective-permute-start.2 = (f32[128,256]{1,0:T(8,128)S(1)}, f32[128,256]{1,0:T(8,128)S(1)}, u32[]{:S(2)}, u32[]{:S(2)}) collective-permute-start(f32[128,256]{1,0:T(8,128)S(1)} %constant_dynamic-slice_fusion), channel_id=1, source_target_pairs={{0,16},{4,20},{8,24},{12,28},{16,0},{20,4},{24,8},{28,12},{1,17},{... | collective-permute-start | bytes 393224 | tf_op jit(solution)/shard_map/cond/branch_1_fun/ppermute | solution.py:630
  100.5 3.6 %collective-permute-done.2 = f32[128,256]{1,0:T(8,128)S(1)} collective-permute-done((f32[128,256]{1,0:T(8,128)S(1)}, f32[128,256]{1,0:T(8,128)S(1)}, u32[]{:S(2)}, u32[]{:S(2)}) %collective-permute-start.2) | collective-permute-done | bytes 131104 | tf_op jit(solution)/shard_map/cond/branch_1_fun/ppermute | solution.py:630
  104.1 1.7 %collective-permute-start.5 = (f32[2,2,128,512]{3,2,1,0:T(8,128)}, f32[2,2,128,512]{3,2,1,0:T(8,128)}, u32[]{:S(2)}, u32[]{:S(2)}) collective-permute-start(f32[2,2,128,512]{3,2,1,0:T(8,128)} %get-tuple-element.43), channel_id=1, source_target_pairs={{12,16},{16,12},{13,17},{17,13},{14,18},{18,14},{15,19},{19,15}} | collective-permute-start | bytes 3145736 | tf_op jit(solution)/shard_map/cond/branch_1_fun/ppermute | solution.py:707
  105.8 2.4 %collective-permute-start.3 = (f32[128,256]{1,0:T(8,128)S(1)}, f32[128,256]{1,0:T(8,128)S(1)}, u32[]{:S(2)}, u32[]{:S(2)}) collective-permute-start(f32[128,256]{1,0:T(8,128)S(1)} %dynamic-slice_add_fusion.1), channel_id=1, source_target_pairs={{0,1},{1,0},{2,3},{3,2},{4,5},{5,4},{6,7},{7,6},{8,9},{9,8},{10,11... | collective-permute-start | bytes 393224 | tf_op jit(solution)/shard_map/cond/branch_1_fun/ppermute | solution.py:709
  108.2 3.0 %collective-permute-done.3 = f32[128,256]{1,0:T(8,128)S(1)} collective-permute-done((f32[128,256]{1,0:T(8,128)S(1)}, f32[128,256]{1,0:T(8,128)S(1)}, u32[]{:S(2)}, u32[]{:S(2)}) %collective-permute-start.3) | collective-permute-done | bytes 131104 | tf_op jit(solution)/shard_map/cond/branch_1_fun/ppermute | solution.py:709
  111.2 4.2 %collective-permute-start.4 = (f32[128,256]{1,0:T(8,128)S(1)}, f32[128,256]{1,0:T(8,128)S(1)}, u32[]{:S(2)}, u32[]{:S(2)}) collective-permute-start(f32[128,256]{1,0:T(8,128)S(1)} %add.38), channel_id=1, source_target_pairs={{0,2},{1,3},{2,0},{3,1},{4,6},{5,7},{6,4},{7,5},{8,10},{9,11},{10,... | collective-permute-start | bytes 393224 | tf_op jit(solution)/shard_map/cond/branch_1_fun/ppermute | solution.py:709
  115.4 0.6 reduce_sum.8
  116.7 4.5 %collective-permute-done.4 = f32[128,256]{1,0:T(8,128)S(1)} collective-permute-done((f32[128,256]{1,0:T(8,128)S(1)}, f32[128,256]{1,0:T(8,128)S(1)}, u32[]{:S(2)}, u32[]{:S(2)}) %collective-permute-start.4) | collective-permute-done | bytes 131104 | tf_op jit(solution)/shard_map/cond/branch_1_fun/ppermute | solution.py:709
  121.3 3.6 %shard_map.111 = (f32[2,2,128,1024]{3,2,1,0:T(8,128)}, f32[2,2,128,256]{3,2,1,0:T(8,128)}) custom-call(f32[2,2,128,256]{3,2,1,0:T(8,128)} %get-tuple-element.104.on_ends, f32[2,2,128,256]{3,2,1,0:T(8,128)} %get-tuple-element.105.off_ends, f32[2,2,512,128]{3,2,1,0:T(8,128)} %collective-permute-done.14.left, f32[2,2,512,128]{3,2,1,0:T(8,128)} %collective-permute-done.15.right, ...), custom_call_target="tpu_custom_call" | custom-call | flops 1000000 | bytes 100000 | tf_op jit(solution)/shard_map/pallas_call | solution.py:509
  124.9 1.5 collective-permute-start.17
  126.4 4.3 %collective-permute-start.19 = (f32[128,256]{1,0:T(8,128)S(1)}, f32[128,256]{1,0:T(8,128)S(1)}, u32[]{:S(2)}, u32[]{:S(2)}) collective-permute-start(f32[128,256]{1,0:T(8,128)S(1)} %get-tuple-element.103), channel_id=1, source_target_pairs={{0,8},{4,12},{8,0},{12,4},{16,24},{20,28},{24,16},{28,20},{1,9},{5... | collective-permute-start | bytes 393224 | tf_op jit(solution)/shard_map/ppermute | solution.py:715
  130.7 1.9 %collective-permute-start.18 = (f32[2,2,128,256]{3,2,1,0:T(8,128)}, f32[2,2,128,256]{3,2,1,0:T(8,128)}, u32[]{:S(2)}, u32[]{:S(2)}) collective-permute-start(f32[2,2,128,256]{3,2,1,0:T(8,128)} %get-tuple-element.109), channel_id=1, source_target_pairs={{4,8},{8,4},{12,16},{16,12},{20,24},{24,20},{5,9},{9,5},{13,17},{1... | collective-permute-start | bytes 1572872 | tf_op jit(solution)/shard_map/ppermute | solution.py:607
  132.6 1.9 %collective-permute-done.19 = f32[128,256]{1,0:T(8,128)S(1)} collective-permute-done((f32[128,256]{1,0:T(8,128)S(1)}, f32[128,256]{1,0:T(8,128)S(1)}, u32[]{:S(2)}, u32[]{:S(2)}) %collective-permute-start.19) | collective-permute-done | bytes 131104 | tf_op jit(solution)/shard_map/ppermute | solution.py:715
  134.5 6.8 %collective-permute-start.20 = (f32[128,256]{1,0:T(8,128)S(1)}, f32[128,256]{1,0:T(8,128)S(1)}, u32[]{:S(2)}, u32[]{:S(2)}) collective-permute-start(f32[128,256]{1,0:T(8,128)S(1)} %add.45), channel_id=1, source_target_pairs={{0,16},{4,20},{8,24},{12,28},{16,0},{20,4},{24,8},{28,12},{1,17},{... | collective-permute-start | bytes 393224 | tf_op jit(solution)/shard_map/ppermute | solution.py:635
  141.3 5.8 %shard_map.112.inner = f32[2,2,256,1024]{3,2,1,0:T(8,128)} custom-call(s32[1]{0:T(128)} %bitcast.tx, f32[2,2,256,512]{3,2,1,0:T(8,128)} %get-tuple-element.110.quarters, f32[2,2,256,256]{3,2,1,0:T(8,128)} %get-tuple-element.111.mid, f32[2,2,128,1024]{3,2,1,0:T(8,128)} %collective-permute-done.17.on, f32[2,2,128,512]{3,2,1,0:T(8,128)} %collective-permute-done.16.off_quarters, ...), custom_call_target="tpu_custom_call" | custom-call | flops 100000000 | bytes 10000000 | tf_op jit(solution)/shard_map/pallas_call | solution.py:549
  147.2 1.8 %collective-permute-done.20 = f32[128,256]{1,0:T(8,128)S(1)} collective-permute-done((f32[128,256]{1,0:T(8,128)S(1)}, f32[128,256]{1,0:T(8,128)S(1)}, u32[]{:S(2)}, u32[]{:S(2)}) %collective-permute-start.20) | collective-permute-done | bytes 131104 | tf_op jit(solution)/shard_map/ppermute | solution.py:635
  149.1 0.6 collective-permute-start.21
  149.6 3.1 %shard_map.113 = f32[2,2,256,1024]{3,2,1,0:T(8,128)} custom-call(s32[1]{0:T(128)} %bitcast.tx, f32[2,2,256,256]{3,2,1,0:T(8,128)} %get-tuple-element.92.ends, f32[2,2,512,128]{3,2,1,0:T(8,128)} %collective-permute-done.14.left, f32[2,2,512,128]{3,2,1,0:T(8,128)} %collective-permute-done.15.right, ...), custom_call_target="tpu_custom_call", output_to_operand_aliasing={{}: (6, {})} | custom-call | flops 99999997952 | bytes 10000000 | tf_op jit(solution)/shard_map/pallas_call | solution.py:585
  152.8 0.8 pad_maximum_fusion
  (26 shorter events, 0.3 us)
Async XLA Ops:
  0.6 19.8 %copy-start.2 = (s32[32]{0:T(128)S(1)}, s32[32]{0:T(128)}, u32[]{:S(2)}) copy-start(s32[32]{0:T(128)} %counts.5) | copy-start | bytes 388
  4.0 14.7 %collective-permute-start.6 = (f32[2,2,128,512]{3,2,1,0:T(8,128)}, f32[2,2,128,512]{3,2,1,0:T(8,128)}, u32[]{:S(2)}, u32[]{:S(2)}) collective-permute-start(f32[2,2,128,512]{3,2,1,0:T(8,128)} %get-tuple-element.83), channel_id=1, source_target_pairs={{12,28},{16,0},{13,29},{17,1},{14,30},{18,2},{15,31},{19,3}} | collective-permute-start | bytes 3145736 | tf_op jit(solution)/shard_map/ppermute | solution.py:612
  5.6 35.0 %collective-permute-start.9 = (f32[2,2,128,512]{3,2,1,0:T(8,128)}, f32[2,2,128,512]{3,2,1,0:T(8,128)}, u32[]{:S(2)}, u32[]{:S(2)}) collective-permute-start(f32[2,2,128,512]{3,2,1,0:T(8,128)} %get-tuple-element.83), channel_id=1, source_target_pairs={{4,8},{8,4},{20,24},{24,20},{5,9},{9,5},{21,25},{25,21},{6,10},{10... | collective-permute-start | bytes 3145736 | tf_op jit(solution)/shard_map/ppermute | solution.py:607
  10.1 14.5 %collective-permute-start.8 = (f32[2,2,256,128]{3,2,1,0:T(8,128)}, f32[2,2,256,128]{3,2,1,0:T(8,128)S(1)}, u32[]{:S(2)}, u32[]{:S(2)}) collective-permute-start(f32[2,2,256,128]{3,2,1,0:T(8,128)} %get-tuple-element.81), channel_id=1, source_target_pairs={{1,0},{2,1},{3,2},{5,4},{6,5},{7,6},{9,8},{10,9},{11,10},{13,12},{... | collective-permute-start | bytes 1572872 | tf_op jit(solution)/shard_map/ppermute | solution.py:599
  11.4 14.7 %collective-permute-start.7 = (f32[2,2,256,128]{3,2,1,0:T(8,128)}, f32[2,2,256,128]{3,2,1,0:T(8,128)}, u32[]{:S(2)}, u32[]{:S(2)}) collective-permute-start(f32[2,2,256,128]{3,2,1,0:T(8,128)} %get-tuple-element.85), channel_id=1, source_target_pairs={{0,1},{1,2},{2,3},{4,5},{5,6},{6,7},{8,9},{9,10},{10,11},{12,13},{... | collective-permute-start | bytes 1572872 | tf_op jit(solution)/shard_map/ppermute | solution.py:599
  16.2 24.4 %collective-permute-start.12 = (f32[2,2,128,256]{3,2,1,0:T(8,128)}, f32[2,2,128,256]{3,2,1,0:T(8,128)}, u32[]{:S(2)}, u32[]{:S(2)}) collective-permute-start(f32[2,2,128,256]{3,2,1,0:T(8,128)} %get-tuple-element.88), channel_id=1, source_target_pairs={{4,8},{8,4},{12,16},{16,12},{20,24},{24,20},{5,9},{9,5},{13,17},{1... | collective-permute-start | bytes 1572872 | tf_op jit(solution)/shard_map/ppermute | solution.py:607
  18.7 21.9 %collective-permute-start.10 = (f32[2,2,128,512]{3,2,1,0:T(8,128)}, f32[2,2,128,512]{3,2,1,0:T(8,128)}, u32[]{:S(2)}, u32[]{:S(2)}) collective-permute-start(f32[2,2,128,512]{3,2,1,0:T(8,128)} %collective-permute-done.6), channel_id=1, source_target_pairs={{28,16},{0,12},{29,17},{1,13},{30,18},{2,14},{31,19},{3,15}} | collective-permute-start | bytes 3145736 | tf_op jit(solution)/shard_map/ppermute | solution.py:617
  20.4 3.6 %copy-start.1 = (s32[8,2]{0,1:T(2,128)S(1)}, s32[8,2]{0,1:T(2,128)}, u32[]{:S(2)}) copy-start(s32[8,2]{0,1:T(2,128)} %param.16) | copy-start | bytes 196
  24.7 1.4 copy-start
  29.8 8.9 %collective-permute-start = (f32[2,2,128,1280]{3,2,1,0:T(8,128)}, f32[2,2,128,1280]{3,2,1,0:T(8,128)}, u32[]{:S(2)}, u32[]{:S(2)}) collective-permute-start(f32[2,2,128,1280]{3,2,1,0:T(8,128)} %get-tuple-element.31), channel_id=1, source_target_pairs={{0,4},{4,0},{8,12},{12,8},{16,20},{20,16},{24,28},{28,24},{1,5},{5... | collective-permute-start | bytes 7864328 | tf_op jit(solution)/shard_map/cond/branch_1_fun/ppermute | solution.py:607
  38.7 26.1 %collective-permute-start.11 = (f32[2,2,128,512]{3,2,1,0:T(8,128)}, f32[2,2,128,512]{3,2,1,0:T(8,128)}, u32[]{:S(2)}, u32[]{:S(2)}) collective-permute-start(f32[2,2,128,512]{3,2,1,0:T(8,128)} %get-tuple-element.87), channel_id=1, source_target_pairs={{4,8},{8,4},{12,16},{16,12},{20,24},{24,20},{5,9},{9,5},{13,17},{1... | collective-permute-start | bytes 3145736 | tf_op jit(solution)/shard_map/ppermute | solution.py:607
  50.0 26.2 %collective-permute-start.13 = (f32[2,2,128,256]{3,2,1,0:T(8,128)}, f32[2,2,128,256]{3,2,1,0:T(8,128)}, u32[]{:S(2)}, u32[]{:S(2)}) collective-permute-start(f32[2,2,128,256]{3,2,1,0:T(8,128)} %get-tuple-element.97), channel_id=1, source_target_pairs={{4,8},{8,4},{12,16},{16,12},{20,24},{24,20},{5,9},{9,5},{13,17},{1... | collective-permute-start | bytes 1572872 | tf_op jit(solution)/shard_map/ppermute | solution.py:607
  76.2 45.1 %collective-permute-start.16 = (f32[2,2,128,512]{3,2,1,0:T(8,128)}, f32[2,2,128,512]{3,2,1,0:T(8,128)}, u32[]{:S(2)}, u32[]{:S(2)}) collective-permute-start(f32[2,2,128,512]{3,2,1,0:T(8,128)} %get-tuple-element.102), channel_id=1, source_target_pairs={{4,8},{8,4},{20,24},{24,20},{5,9},{9,5},{21,25},{25,21},{6,10},{10... | collective-permute-start | bytes 3145736 | tf_op jit(solution)/shard_map/ppermute | solution.py:607
  78.1 43.2 %collective-permute-start.14 = (f32[2,2,512,128]{3,2,1,0:T(8,128)}, f32[2,2,512,128]{3,2,1,0:T(8,128)}, u32[]{:S(2)}, u32[]{:S(2)}) collective-permute-start(f32[2,2,512,128]{3,2,1,0:T(8,128)} %get-tuple-element.98), channel_id=1, source_target_pairs={{0,1},{1,2},{2,3},{4,5},{5,6},{6,7},{8,9},{9,10},{10,11},{12,13},{... | collective-permute-start | bytes 3145736 | tf_op jit(solution)/shard_map/ppermute | solution.py:599
  90.1 31.1 %collective-permute-start.15 = (f32[2,2,512,128]{3,2,1,0:T(8,128)}, f32[2,2,512,128]{3,2,1,0:T(8,128)}, u32[]{:S(2)}, u32[]{:S(2)}) collective-permute-start(f32[2,2,512,128]{3,2,1,0:T(8,128)} %get-tuple-element.99), channel_id=1, source_target_pairs={{1,0},{2,1},{3,2},{5,4},{6,5},{7,6},{9,8},{10,9},{11,10},{13,12},{... | collective-permute-start | bytes 3145736 | tf_op jit(solution)/shard_map/ppermute | solution.py:599
  91.5 1.6 %collective-permute-start.1 = (f32[256,256]{1,0:T(8,128)S(1)}, f32[256,256]{1,0:T(8,128)S(1)}, u32[]{:S(2)}, u32[]{:S(2)}) collective-permute-start(f32[256,256]{1,0:T(8,128)S(1)} %constant_dynamic-slice_fusion.1), channel_id=1, source_target_pairs={{0,4},{4,0},{8,12},{12,8},{16,20},{20,16},{24,28},{28,24},{1,5},{5... | collective-permute-start | bytes 786440 | tf_op jit(solution)/shard_map/cond/branch_1_fun/ppermute | solution.py:630
  93.2 11.0 %collective-permute-start.2 = (f32[128,256]{1,0:T(8,128)S(1)}, f32[128,256]{1,0:T(8,128)S(1)}, u32[]{:S(2)}, u32[]{:S(2)}) collective-permute-start(f32[128,256]{1,0:T(8,128)S(1)} %constant_dynamic-slice_fusion), channel_id=1, source_target_pairs={{0,16},{4,20},{8,24},{12,28},{16,0},{20,4},{24,8},{28,12},{1,17},{... | collective-permute-start | bytes 393224 | tf_op jit(solution)/shard_map/cond/branch_1_fun/ppermute | solution.py:630
  104.1 17.1 %collective-permute-start.5 = (f32[2,2,128,512]{3,2,1,0:T(8,128)}, f32[2,2,128,512]{3,2,1,0:T(8,128)}, u32[]{:S(2)}, u32[]{:S(2)}) collective-permute-start(f32[2,2,128,512]{3,2,1,0:T(8,128)} %get-tuple-element.43), channel_id=1, source_target_pairs={{12,16},{16,12},{13,17},{17,13},{14,18},{18,14},{15,19},{19,15}} | collective-permute-start | bytes 3145736 | tf_op jit(solution)/shard_map/cond/branch_1_fun/ppermute | solution.py:707
  105.8 5.3 %collective-permute-start.3 = (f32[128,256]{1,0:T(8,128)S(1)}, f32[128,256]{1,0:T(8,128)S(1)}, u32[]{:S(2)}, u32[]{:S(2)}) collective-permute-start(f32[128,256]{1,0:T(8,128)S(1)} %dynamic-slice_add_fusion.1), channel_id=1, source_target_pairs={{0,1},{1,0},{2,3},{3,2},{4,5},{5,4},{6,7},{7,6},{8,9},{9,8},{10,11... | collective-permute-start | bytes 393224 | tf_op jit(solution)/shard_map/cond/branch_1_fun/ppermute | solution.py:709
  111.2 10.0 %collective-permute-start.4 = (f32[128,256]{1,0:T(8,128)S(1)}, f32[128,256]{1,0:T(8,128)S(1)}, u32[]{:S(2)}, u32[]{:S(2)}) collective-permute-start(f32[128,256]{1,0:T(8,128)S(1)} %add.38), channel_id=1, source_target_pairs={{0,2},{1,3},{2,0},{3,1},{4,6},{5,7},{6,4},{7,5},{8,10},{9,11},{10,... | collective-permute-start | bytes 393224 | tf_op jit(solution)/shard_map/cond/branch_1_fun/ppermute | solution.py:709
  124.9 16.4 %collective-permute-start.17 = (f32[2,2,128,1024]{3,2,1,0:T(8,128)}, f32[2,2,128,1024]{3,2,1,0:T(8,128)}, u32[]{:S(2)}, u32[]{:S(2)}) collective-permute-start(f32[2,2,128,1024]{3,2,1,0:T(8,128)} %get-tuple-element.108), channel_id=1, source_target_pairs={{0,4},{4,0},{8,12},{12,8},{16,20},{20,16},{24,28},{28,24},{1,5},{5... | collective-permute-start | bytes 6291464 | tf_op jit(solution)/shard_map/ppermute | solution.py:607
  126.4 8.1 %collective-permute-start.19 = (f32[128,256]{1,0:T(8,128)S(1)}, f32[128,256]{1,0:T(8,128)S(1)}, u32[]{:S(2)}, u32[]{:S(2)}) collective-permute-start(f32[128,256]{1,0:T(8,128)S(1)} %get-tuple-element.103), channel_id=1, source_target_pairs={{0,8},{4,12},{8,0},{12,4},{16,24},{20,28},{24,16},{28,20},{1,9},{5... | collective-permute-start | bytes 393224 | tf_op jit(solution)/shard_map/ppermute | solution.py:715
  130.7 18.9 %collective-permute-start.18 = (f32[2,2,128,256]{3,2,1,0:T(8,128)}, f32[2,2,128,256]{3,2,1,0:T(8,128)}, u32[]{:S(2)}, u32[]{:S(2)}) collective-permute-start(f32[2,2,128,256]{3,2,1,0:T(8,128)} %get-tuple-element.109), channel_id=1, source_target_pairs={{4,8},{8,4},{12,16},{16,12},{20,24},{24,20},{5,9},{9,5},{13,17},{1... | collective-permute-start | bytes 1572872 | tf_op jit(solution)/shard_map/ppermute | solution.py:607
  134.5 14.5 %collective-permute-start.20 = (f32[128,256]{1,0:T(8,128)S(1)}, f32[128,256]{1,0:T(8,128)S(1)}, u32[]{:S(2)}, u32[]{:S(2)}) collective-permute-start(f32[128,256]{1,0:T(8,128)S(1)} %add.45), channel_id=1, source_target_pairs={{0,16},{4,20},{8,24},{12,28},{16,0},{20,4},{24,8},{28,12},{1,17},{... | collective-permute-start | bytes 393224 | tf_op jit(solution)/shard_map/ppermute | solution.py:635
  149.1 3.6 %collective-permute-start.21 = (f32[256,256]{1,0:T(8,128)S(1)}, f32[256,256]{1,0:T(8,128)S(1)}, u32[]{:S(2)}, u32[]{:S(2)}) collective-permute-start(f32[256,256]{1,0:T(8,128)S(1)} %pad_maximum_fusion.1), channel_id=1, source_target_pairs={{0,4},{4,0},{8,12},{12,8},{16,20},{20,16},{24,28},{28,24},{1,5},{5... | collective-permute-start | bytes 786440 | tf_op jit(solution)/shard_map/ppermute | solution.py:723

commit v6 on v5

--- a/solution.py
+++ b/solution.py
@@ -265,6 +265,7 @@
     def two(p, _):
         i = 2 * p
         pl.when((i + 1 >= first) & (i - 1 < first))(loads[1].wait)
+        pl.when((first == 0) & (p == 0))(lambda: store(0))
         visit([slot_at(i), slot_at(i + 1)], probe, table, g_probe)
         after_first(i)
         return 0
@@ -273,12 +274,14 @@
         visit([slot_at(count - 1)], probe, table, g_probe)
         after_first(count - 1)
 
+    soon = first < 2
+    pl.when(soon)(loads[1].start)
     loads[0].wait()
-    loads[1].start()
-    pl.when(first == 0)(lambda: store(0))
+    pl.when(jnp.logical_not(soon))(loads[1].start)
     pairs = count // 2
     lax.fori_loop(0, pairs, two, 0)
     pl.when(2 * pairs - 1 < first)(loads[1].wait)
+    pl.when((first == 0) & (pairs == 0))(lambda: store(0))
     pl.when(count % 2 == 1)(one)
     store(1)
     for g in (0, 1):
@@ -369,6 +372,8 @@
         acc[end] = jnp.zeros_like(acc[end])
     last_block = (tile_cols + 2 * rim) // width - 2
     two_groups(here, (0, last_block), 2, waits, stores, (early, late), amps, amp_sem, order, out_sem, probe, table, obj, acc, g_probe)
+    positions = lax.fori_loop(0, counts.shape[0], lambda i, n: n + counts[i], jnp.zeros((), jnp.int32))
+    g_probe[...] = g_probe[...] / jnp.sqrt(jnp.full(g_probe.shape, jnp.maximum(positions, 1).astype(F32)))
 
 
 SMEM = pl.BlockSpec(memory_space=pltpu.SMEM)
@@ -707,7 +712,7 @@
         far = lax.ppermute(after(quarters, flat), "tx", [(middle - 1, middle), (middle, middle - 1)])
         for step in (2**k for k in range(axes[1].bit_length() - 1)):
             flat = flat + lax.ppermute(flat, "ty", [(i, i ^ step) for i in range(axes[1])])
-        return flat / jnp.sqrt(jnp.maximum(jnp.sum(counts), 1).astype(F32)), far
+        return flat, far
 
     flat, far_quarters = lax.cond(
         counts[0] >= 0, shared, lambda x, quarters: (x[:shard], quarters), g_probe.reshape(-1, width), g_off_quarters

time: 153 us -> 154 us (level); the launches traced: 154 us -> 152 us
  Pallas kernels: 47.3 us -> 53.6 us
  starting transfers between devices: 72.1 us -> 67.7 us
  waiting for transfers between devices: 30.1 us -> 27.9 us
    ppermute x4, starting transfers between devices: 19.4 us -> 10.1 us  [along(): lax.ppermute(x, 'ty', [(i, i + step) for i in range(count) if 0 <= i + st...]
    pallas_call x2, Pallas kernels: 20.6 us -> 26.5 us  [field_call(): pl.pallas_call(functools.partial(body, axes), out_shape=tuple(outs) + (ja...]
    ppermute x8, waiting for transfers between devices: 12.4 us -> 8.78 us  [across(): return lax.ppermute(x, 'tx', pairs)]
    ppermute x2, waiting for transfers between devices: 7.5 us -> 10.7 us  [shared(): lax.ppermute(flat, 'ty', [(i, i ^ step) for i in range(axes[1])])]
    ppermute x1, starting transfers between devices: 4.32 us -> 1.42 us  [per_device(): other = lax.ppermute(flat, 'tx', [(i, i ^ 2) for i in range(axes[0])])]
    ppermute x2, starting transfers between devices: 7.46 us -> 10.2 us  [halved(): return mine + lax.ppermute(other, 'tx', pairs)]
    ppermute x1, starting transfers between devices: 6.82 us -> 8.76 us  [doubled(): lax.ppermute(flat, 'tx', [(i, i ^ apart) for i in range(lax.axis_size('tx...]
    ppermute x8, starting transfers between devices: 22 us -> 23.9 us  [across(): return lax.ppermute(x, 'tx', pairs)]
  transfers between devices with their start and end apart: 22 -> 22, of which waited for: 9 -> 9; matrix products, arithmetic and copies ran while one was open for 1% -> 1% of each run, Pallas kernels for 26% -> 31%
where the time goes in v6:
time: 154 us; the launch traced here: 152 us
  starting transfers between devices  67.7 us (44%)
  Pallas kernels  53.6 us (35%)
  waiting for transfers between devices  27.9 us (18%)
    pallas_call x2, Pallas kernels, field_call(): pl.pallas_call(functools.partial(body, axes), out_shape=tuple(outs) + (ja...  26.5 us
    ppermute x8, starting transfers between devices, across(): return lax.ppermute(x, 'tx', pairs)  23.9 us
    ppermute x2, waiting for transfers between devices, shared(): lax.ppermute(flat, 'ty', [(i, i ^ step) for i in range(axes[1])])  10.7 us
    ppermute x2, starting transfers between devices, halved(): return mine + lax.ppermute(other, 'tx', pairs)  10.2 us
    ppermute x4, starting transfers between devices, along(): lax.ppermute(x, 'ty', [(i, i + step) for i in range(count) if 0 <= i + st...  10.1 us
    ppermute x8, waiting for transfers between devices, across(): return lax.ppermute(x, 'tx', pairs)  8.78 us
    ppermute x1, starting transfers between devices, doubled(): lax.ppermute(flat, 'tx', [(i, i ^ apart) for i in range(lax.axis_size('tx...  8.76 us
    ppermute x2, starting transfers between devices, shared(): lax.ppermute(flat, 'ty', [(i, i ^ step) for i in range(axes[1])])  7.79 us
  transfers between devices with their start and end apart: 22, of which 9 were waited for; matrix products, arithmetic and copies ran while one was open for 1% of the time, Pallas kernels for 31%

profile of v6, /device:TPU:1, one launch (start us, length us, event | category | flops | bytes accessed | tf_op | source)
XLA Modules:
  0.0 152.0 jit_solution(17925312633383954041)
XLA Ops:
  0.6 3.3 %shard_map.107 = (f32[2,2,256,128]{3,2,1,0:T(8,128)}, f32[2,2,256,128]{3,2,1,0:T(8,128)}, f32[2,2,128,512]{3,2,1,0:T(8,128)}, f32[2,2,128,256]{3,2,1,0:T(8,128)}) custom-call(s32[1]{0:T(128)} %bitcast.tx, f32[2,2,256,1024]{3,2,1,0:T(8,128)} %tile.5), custom_call_target="tpu_custom_call" | custom-call | flops 100000000 | bytes 10000000 | tf_op jit(solution)/shard_map/pallas_call | solution.py:453
  4.0 1.7 %collective-permute-start.6 = (f32[2,2,128,512]{3,2,1,0:T(8,128)}, f32[2,2,128,512]{3,2,1,0:T(8,128)}, u32[]{:S(2)}, u32[]{:S(2)}) collective-permute-start(f32[2,2,128,512]{3,2,1,0:T(8,128)} %get-tuple-element.80), channel_id=1, source_target_pairs={{12,28},{16,0},{13,29},{17,1},{14,30},{18,2},{15,31},{19,3}} | collective-permute-start | bytes 3145736 | tf_op jit(solution)/shard_map/ppermute | solution.py:617
  5.6 4.5 %collective-permute-start.9 = (f32[2,2,128,512]{3,2,1,0:T(8,128)}, f32[2,2,128,512]{3,2,1,0:T(8,128)}, u32[]{:S(2)}, u32[]{:S(2)}) collective-permute-start(f32[2,2,128,512]{3,2,1,0:T(8,128)} %get-tuple-element.80), channel_id=1, source_target_pairs={{4,8},{8,4},{20,24},{24,20},{5,9},{9,5},{21,25},{25,21},{6,10},{10... | collective-permute-start | bytes 3145736 | tf_op jit(solution)/shard_map/ppermute | solution.py:612
  10.1 1.3 collective-permute-start.8
  11.4 4.8 %collective-permute-start.7 = (f32[2,2,256,128]{3,2,1,0:T(8,128)}, f32[2,2,256,128]{3,2,1,0:T(8,128)}, u32[]{:S(2)}, u32[]{:S(2)}) collective-permute-start(f32[2,2,256,128]{3,2,1,0:T(8,128)} %get-tuple-element.82), channel_id=1, source_target_pairs={{0,1},{1,2},{2,3},{4,5},{5,6},{6,7},{8,9},{9,10},{10,11},{12,13},{... | collective-permute-start | bytes 1572872 | tf_op jit(solution)/shard_map/ppermute | solution.py:604
  16.2 2.5 %collective-permute-start.12 = (f32[2,2,128,256]{3,2,1,0:T(8,128)}, f32[2,2,128,256]{3,2,1,0:T(8,128)}, u32[]{:S(2)}, u32[]{:S(2)}) collective-permute-start(f32[2,2,128,256]{3,2,1,0:T(8,128)} %get-tuple-element.85), channel_id=1, source_target_pairs={{4,8},{8,4},{12,16},{16,12},{20,24},{24,20},{5,9},{9,5},{13,17},{1... | collective-permute-start | bytes 1572872 | tf_op jit(solution)/shard_map/ppermute | solution.py:612
  18.7 0.0 collective-permute-done.6
  18.7 1.7 %collective-permute-start.10 = (f32[2,2,128,512]{3,2,1,0:T(8,128)}, f32[2,2,128,512]{3,2,1,0:T(8,128)}, u32[]{:S(2)}, u32[]{:S(2)}) collective-permute-start(f32[2,2,128,512]{3,2,1,0:T(8,128)} %collective-permute-done.6), channel_id=1, source_target_pairs={{28,16},{0,12},{29,17},{1,13},{30,18},{2,14},{31,19},{3,15}} | collective-permute-start | bytes 3145736 | tf_op jit(solution)/shard_map/ppermute | solution.py:622
  20.4 4.0 %shard_map.108.early = f32[4,256,256]{2,1,0:T(8,128)} custom-call(s32[1]{0:T(128)} %bitcast.tx, s32[1]{0:T(128)} %bitcast.1.ty, s32[32]{0:T(128)S(1)} %copy-done.2, f32[8,256,256]{2,1,0:T(8,128)} %patterns, bf16[3,256,256]{2,1,0:T(8,128)(2,1)} %constant.97.clone.pick), custom_call_target="tpu_custom_call" | custom-call | flops 99999997952 | bytes 10000000 | tf_op jit(solution)/shard_map/pallas_call | solution.py:481
  24.4 0.7 copy.13.centers
  25.1 0.0 collective-permute-done.8.right
  25.1 1.0 collective-permute-done.7.left
  26.1 12.6 %conditional.2 = (f32[2,2,128,1280]{3,2,1,0:T(8,128)}, f32[2,2,128,512]{3,2,1,0:T(8,128)}, f32[4,256,256]{2,1,0:T(8,128)}) conditional(s32[]{:T(128)} %bitcast.2, f32[8,256,256]{2,1,0:T(8,128)} %patterns, (s32[1]{0:T(128)}, f32[2,2,256,1024]{3,2,1,0:T(8,128)}, f32[2,2,256,128]{3,2,1,0:T(8,128)}, f32[2,2,256,128]{3,2,1,0:T(8,128)S(1)}, ...), branch_computations={%region_0.0_spmd, %region_1.0_spmd} | conditional | flops 100099997696 | bytes 30485824 | solution.py:684
  26.1 3.7 %branch_1_fun.2 = (f32[2,2,128,1280]{3,2,1,0:T(8,128)}, f32[2,2,128,512]{3,2,1,0:T(8,128)}) custom-call(s32[1]{0:T(128)} %get-tuple-element.25.tx, f32[2,2,256,1024]{3,2,1,0:T(8,128)} %get-tuple-element.26.tile, f32[2,2,256,128]{3,2,1,0:T(8,128)} %get-tuple-element.27.left, f32[2,2,256,128]{3,2,1,0:T(8,128)S(1)} %get-tuple-element.28.right), custom_call_target="tpu_custom_call" | custom-call | flops 100000000 | bytes 10000000 | tf_op jit(solution)/shard_map/cond/branch_1_fun/pallas_call | solution.py:453
  29.8 4.0 %collective-permute-start = (f32[2,2,128,1280]{3,2,1,0:T(8,128)}, f32[2,2,128,1280]{3,2,1,0:T(8,128)}, u32[]{:S(2)}, u32[]{:S(2)}) collective-permute-start(f32[2,2,128,1280]{3,2,1,0:T(8,128)} %get-tuple-element.29), channel_id=1, source_target_pairs={{0,4},{4,0},{8,12},{12,8},{16,20},{20,16},{24,28},{28,24},{1,5},{5... | collective-permute-start | bytes 7864328 | tf_op jit(solution)/shard_map/cond/branch_1_fun/ppermute | solution.py:612
  33.8 3.5 %branch_1_fun.3 = f32[4,256,256]{2,1,0:T(8,128)} custom-call(s32[1]{0:T(128)} %get-tuple-element.25.tx, s32[1]{0:T(128)} %get-tuple-element.31.ty, s32[32]{0:T(128)S(1)} %get-tuple-element.32.counts, f32[8,256,256]{2,1,0:T(8,128)} %get-tuple-element.34.patterns, bf16[3,256,256]{2,1,0:T(8,128)(2,1)} %get-tuple-element.35.pick), custom_call_target="tpu_custom_call" | custom-call | flops 99999997952 | bytes 10000000 | tf_op jit(solution)/shard_map/cond/branch_1_fun/pallas_call | solution.py:481
  37.3 1.4 collective-permute-done
  38.7 1.9 %collective-permute-start.11 = (f32[2,2,128,512]{3,2,1,0:T(8,128)}, f32[2,2,128,512]{3,2,1,0:T(8,128)}, u32[]{:S(2)}, u32[]{:S(2)}) collective-permute-start(f32[2,2,128,512]{3,2,1,0:T(8,128)} %get-tuple-element.84), channel_id=1, source_target_pairs={{4,8},{8,4},{12,16},{16,12},{20,24},{24,20},{5,9},{9,5},{13,17},{1... | collective-permute-start | bytes 3145736 | tf_op jit(solution)/shard_map/ppermute | solution.py:612
  40.6 0.0 collective-permute-done.12.off_mid
  40.6 12.0 %shard_map.109 = (f32[2,2,2,512,256]{4,3,2,1,0:T(8,128)}, f32[2,2,256,256]{3,2,1,0:T(8,128)}, f32[2,2,128,256]{3,2,1,0:T(8,128)}, f32[2,2,128,256]{3,2,1,0:T(8,128)}, f32[2,256,256]{2,1,0:T(8,128)}) custom-call(s32[1]{0:T(128)} %bitcast.tx, s32[1]{0:T(128)} %bitcast.1.ty, s32[8,2]{1,0:T(8,128)} %copy.13.centers, s32[32]{0:T(128)S(1)} %copy-done.2, ...), custom_call_target="tpu_custom_call" | custom-call | flops 20000000000 | bytes 10000000 | tf_op jit(solution)/shard_map/pallas_call | solution.py:398
  52.6 6.4 %collective-permute-start.13 = (f32[2,2,128,256]{3,2,1,0:T(8,128)}, f32[2,2,128,256]{3,2,1,0:T(8,128)}, u32[]{:S(2)}, u32[]{:S(2)}) collective-permute-start(f32[2,2,128,256]{3,2,1,0:T(8,128)} %get-tuple-element.94), channel_id=1, source_target_pairs={{4,8},{8,4},{12,16},{16,12},{20,24},{24,20},{5,9},{9,5},{13,17},{1... | collective-permute-start | bytes 1572872 | tf_op jit(solution)/shard_map/ppermute | solution.py:612
  59.0 7.4 %collective-permute-done.11.off_ends = f32[2,2,128,512]{3,2,1,0:T(8,128)} collective-permute-done((f32[2,2,128,512]{3,2,1,0:T(8,128)}, f32[2,2,128,512]{3,2,1,0:T(8,128)}, u32[]{:S(2)}, u32[]{:S(2)}) %collective-permute-start.11) | collective-permute-done | bytes 1048608 | tf_op jit(solution)/shard_map/ppermute | solution.py:612
  66.4 14.6 %shard_map.110 = (f32[2,2,256,256]{3,2,1,0:T(8,128)}, f32[2,2,256,512]{3,2,1,0:T(8,128)}, f32[2,2,128,256]{3,2,1,0:T(8,128)}, f32[2,2,128,512]{3,2,1,0:T(8,128)}...) custom-call(s32[1]{0:T(128)} %bitcast.tx, ...), custom_call_target="tpu_custom_call" | custom-call | flops 20000000000 | bytes 10000000 | tf_op jit(solution)/shard_map/pallas_call | solution.py:398
  81.0 0.0 collective-permute-done.13.off_mid
  81.0 1.9 %collective-permute-start.16 = (f32[2,2,128,512]{3,2,1,0:T(8,128)}, f32[2,2,128,512]{3,2,1,0:T(8,128)}, u32[]{:S(2)}, u32[]{:S(2)}) collective-permute-start(f32[2,2,128,512]{3,2,1,0:T(8,128)} %get-tuple-element.99), channel_id=1, source_target_pairs={{4,8},{8,4},{20,24},{24,20},{5,9},{9,5},{21,25},{25,21},{6,10},{10... | collective-permute-start | bytes 3145736 | tf_op jit(solution)/shard_map/ppermute | solution.py:612
  82.9 2.7 %collective-permute-start.14 = (f32[2,2,512,128]{3,2,1,0:T(8,128)}, f32[2,2,512,128]{3,2,1,0:T(8,128)}, u32[]{:S(2)}, u32[]{:S(2)}) collective-permute-start(f32[2,2,512,128]{3,2,1,0:T(8,128)} %get-tuple-element.95), channel_id=1, source_target_pairs={{0,1},{1,2},{2,3},{4,5},{5,6},{6,7},{8,9},{9,10},{10,11},{12,13},{... | collective-permute-start | bytes 3145736 | tf_op jit(solution)/shard_map/ppermute | solution.py:604
  85.6 1.3 collective-permute-start.15
  86.9 35.8 %conditional.3 = (f32[128,256]{1,0:T(8,128)S(1)}, f32[2,2,128,512]{3,2,1,0:T(8,128)}) conditional(s32[]{:T(128)} %bitcast.2, (f32[512,256]{1,0:T(8,128)S(1)}, f32[2,2,128,512]{3,2,1,0:T(8,128)}) %tuple.49, (f32[512,256]{1,0:T(8,128)S(1)}, f32[2,2,128,512]{3,2,1,0:T(8,128)}) %tuple.50), branch_computations={%region_2.0_spmd, %region_3.4_spmd} | conditional | flops 163895 | bytes 9569066 | solution.py:717
  87.0 0.1 collective-permute-start.1
  87.1 1.5 collective-permute-done.1
  88.7 10.1 %collective-permute-start.2 = (f32[128,256]{1,0:T(8,128)S(1)}, f32[128,256]{1,0:T(8,128)S(1)}, u32[]{:S(2)}, u32[]{:S(2)}) collective-permute-start(f32[128,256]{1,0:T(8,128)S(1)} %constant_dynamic-slice_fusion), channel_id=1, source_target_pairs={{0,16},{4,20},{8,24},{12,28},{16,0},{20,4},{24,8},{28,12},{1,17},{... | collective-permute-start | bytes 393224 | tf_op jit(solution)/shard_map/cond/branch_1_fun/ppermute | solution.py:635
  98.8 3.7 %collective-permute-done.2 = f32[128,256]{1,0:T(8,128)S(1)} collective-permute-done((f32[128,256]{1,0:T(8,128)S(1)}, f32[128,256]{1,0:T(8,128)S(1)}, u32[]{:S(2)}, u32[]{:S(2)}) %collective-permute-start.2) | collective-permute-done | bytes 131104 | tf_op jit(solution)/shard_map/cond/branch_1_fun/ppermute | solution.py:635
  102.5 1.7 %collective-permute-start.5 = (f32[2,2,128,512]{3,2,1,0:T(8,128)}, f32[2,2,128,512]{3,2,1,0:T(8,128)}, u32[]{:S(2)}, u32[]{:S(2)}) collective-permute-start(f32[2,2,128,512]{3,2,1,0:T(8,128)} %get-tuple-element.40), channel_id=1, source_target_pairs={{12,16},{16,12},{13,17},{17,13},{14,18},{18,14},{15,19},{19,15}} | collective-permute-start | bytes 3145736 | tf_op jit(solution)/shard_map/cond/branch_1_fun/ppermute | solution.py:712
  104.2 2.1 %collective-permute-start.3 = (f32[128,256]{1,0:T(8,128)S(1)}, f32[128,256]{1,0:T(8,128)S(1)}, u32[]{:S(2)}, u32[]{:S(2)}) collective-permute-start(f32[128,256]{1,0:T(8,128)S(1)} %dynamic-slice_add_fusion.1), channel_id=1, source_target_pairs={{0,1},{1,0},{2,3},{3,2},{4,5},{5,4},{6,7},{7,6},{8,9},{9,8},{10,11... | collective-permute-start | bytes 393224 | tf_op jit(solution)/shard_map/cond/branch_1_fun/ppermute | solution.py:714
  106.3 4.5 %collective-permute-done.3 = f32[128,256]{1,0:T(8,128)S(1)} collective-permute-done((f32[128,256]{1,0:T(8,128)S(1)}, f32[128,256]{1,0:T(8,128)S(1)}, u32[]{:S(2)}, u32[]{:S(2)}) %collective-permute-start.3) | collective-permute-done | bytes 131104 | tf_op jit(solution)/shard_map/cond/branch_1_fun/ppermute | solution.py:714
  110.9 5.7 %collective-permute-start.4 = (f32[128,256]{1,0:T(8,128)S(1)}, f32[128,256]{1,0:T(8,128)S(1)}, u32[]{:S(2)}, u32[]{:S(2)}) collective-permute-start(f32[128,256]{1,0:T(8,128)S(1)} %add.38), channel_id=1, source_target_pairs={{0,2},{1,3},{2,0},{3,1},{4,6},{5,7},{6,4},{7,5},{8,10},{9,11},{10,... | collective-permute-start | bytes 393224 | tf_op jit(solution)/shard_map/cond/branch_1_fun/ppermute | solution.py:714
  116.6 6.1 %collective-permute-done.4 = f32[128,256]{1,0:T(8,128)S(1)} collective-permute-done((f32[128,256]{1,0:T(8,128)S(1)}, f32[128,256]{1,0:T(8,128)S(1)}, u32[]{:S(2)}, u32[]{:S(2)}) %collective-permute-start.4) | collective-permute-done | bytes 131104 | tf_op jit(solution)/shard_map/cond/branch_1_fun/ppermute | solution.py:714
  122.8 3.6 %shard_map.111 = (f32[2,2,128,1024]{3,2,1,0:T(8,128)}, f32[2,2,128,256]{3,2,1,0:T(8,128)}) custom-call(f32[2,2,128,256]{3,2,1,0:T(8,128)} %get-tuple-element.101.on_ends, f32[2,2,128,256]{3,2,1,0:T(8,128)} %get-tuple-element.102.off_ends, f32[2,2,512,128]{3,2,1,0:T(8,128)} %collective-permute-done.14.left, f32[2,2,512,128]{3,2,1,0:T(8,128)} %collective-permute-done.15.right, ...), custom_call_target="tpu_custom_call" | custom-call | flops 1000000 | bytes 100000 | tf_op jit(solution)/shard_map/pallas_call | solution.py:514
  126.4 0.5 collective-permute-start.17
  126.9 1.4 collective-permute-start.19
  128.3 2.3 %collective-permute-start.18 = (f32[2,2,128,256]{3,2,1,0:T(8,128)}, f32[2,2,128,256]{3,2,1,0:T(8,128)}, u32[]{:S(2)}, u32[]{:S(2)}) collective-permute-start(f32[2,2,128,256]{3,2,1,0:T(8,128)} %get-tuple-element.106), channel_id=1, source_target_pairs={{4,8},{8,4},{12,16},{16,12},{20,24},{24,20},{5,9},{9,5},{13,17},{1... | collective-permute-start | bytes 1572872 | tf_op jit(solution)/shard_map/ppermute | solution.py:612
  130.5 1.3 collective-permute-done.19
  131.8 8.8 %collective-permute-start.20 = (f32[128,256]{1,0:T(8,128)S(1)}, f32[128,256]{1,0:T(8,128)S(1)}, u32[]{:S(2)}, u32[]{:S(2)}) collective-permute-start(f32[128,256]{1,0:T(8,128)S(1)} %add.45), channel_id=1, source_target_pairs={{0,16},{4,20},{8,24},{12,28},{16,0},{20,4},{24,8},{28,12},{1,17},{... | collective-permute-start | bytes 393224 | tf_op jit(solution)/shard_map/ppermute | solution.py:640
  140.6 5.8 %shard_map.112.inner = f32[2,2,256,1024]{3,2,1,0:T(8,128)} custom-call(s32[1]{0:T(128)} %bitcast.tx, f32[2,2,256,512]{3,2,1,0:T(8,128)} %get-tuple-element.107.quarters, f32[2,2,256,256]{3,2,1,0:T(8,128)} %get-tuple-element.108.mid, f32[2,2,128,1024]{3,2,1,0:T(8,128)} %collective-permute-done.17.on, f32[2,2,128,512]{3,2,1,0:T(8,128)} %collective-permute-done.16.off_quarters, ...), custom_call_target="tpu_custom_call" | custom-call | flops 100000000 | bytes 10000000 | tf_op jit(solution)/shard_map/pallas_call | solution.py:554
  146.4 0.9 collective-permute-done.20
  147.4 0.6 collective-permute-start.21
  148.0 3.1 %shard_map.113 = f32[2,2,256,1024]{3,2,1,0:T(8,128)} custom-call(s32[1]{0:T(128)} %bitcast.tx, f32[2,2,256,256]{3,2,1,0:T(8,128)} %get-tuple-element.89.ends, f32[2,2,512,128]{3,2,1,0:T(8,128)} %collective-permute-done.14.left, f32[2,2,512,128]{3,2,1,0:T(8,128)} %collective-permute-done.15.right, ...), custom_call_target="tpu_custom_call", output_to_operand_aliasing={{}: (6, {})} | custom-call | flops 99999997952 | bytes 10000000 | tf_op jit(solution)/shard_map/pallas_call | solution.py:590
  151.1 0.8 pad_maximum_fusion
  (25 shorter events, 0.3 us)
Async XLA Ops:
  0.6 19.8 %copy-start.2 = (s32[32]{0:T(128)S(1)}, s32[32]{0:T(128)}, u32[]{:S(2)}) copy-start(s32[32]{0:T(128)} %counts.5) | copy-start | bytes 388
  4.0 14.7 %collective-permute-start.6 = (f32[2,2,128,512]{3,2,1,0:T(8,128)}, f32[2,2,128,512]{3,2,1,0:T(8,128)}, u32[]{:S(2)}, u32[]{:S(2)}) collective-permute-start(f32[2,2,128,512]{3,2,1,0:T(8,128)} %get-tuple-element.80), channel_id=1, source_target_pairs={{12,28},{16,0},{13,29},{17,1},{14,30},{18,2},{15,31},{19,3}} | collective-permute-start | bytes 3145736 | tf_op jit(solution)/shard_map/ppermute | solution.py:617
  5.6 35.0 %collective-permute-start.9 = (f32[2,2,128,512]{3,2,1,0:T(8,128)}, f32[2,2,128,512]{3,2,1,0:T(8,128)}, u32[]{:S(2)}, u32[]{:S(2)}) collective-permute-start(f32[2,2,128,512]{3,2,1,0:T(8,128)} %get-tuple-element.80), channel_id=1, source_target_pairs={{4,8},{8,4},{20,24},{24,20},{5,9},{9,5},{21,25},{25,21},{6,10},{10... | collective-permute-start | bytes 3145736 | tf_op jit(solution)/shard_map/ppermute | solution.py:612
  10.1 15.0 %collective-permute-start.8 = (f32[2,2,256,128]{3,2,1,0:T(8,128)}, f32[2,2,256,128]{3,2,1,0:T(8,128)S(1)}, u32[]{:S(2)}, u32[]{:S(2)}) collective-permute-start(f32[2,2,256,128]{3,2,1,0:T(8,128)} %get-tuple-element.78), channel_id=1, source_target_pairs={{1,0},{2,1},{3,2},{5,4},{6,5},{7,6},{9,8},{10,9},{11,10},{13,12},{... | collective-permute-start | bytes 1572872 | tf_op jit(solution)/shard_map/ppermute | solution.py:604
  11.4 14.7 %collective-permute-start.7 = (f32[2,2,256,128]{3,2,1,0:T(8,128)}, f32[2,2,256,128]{3,2,1,0:T(8,128)}, u32[]{:S(2)}, u32[]{:S(2)}) collective-permute-start(f32[2,2,256,128]{3,2,1,0:T(8,128)} %get-tuple-element.82), channel_id=1, source_target_pairs={{0,1},{1,2},{2,3},{4,5},{5,6},{6,7},{8,9},{9,10},{10,11},{12,13},{... | collective-permute-start | bytes 1572872 | tf_op jit(solution)/shard_map/ppermute | solution.py:604
  16.2 24.4 %collective-permute-start.12 = (f32[2,2,128,256]{3,2,1,0:T(8,128)}, f32[2,2,128,256]{3,2,1,0:T(8,128)}, u32[]{:S(2)}, u32[]{:S(2)}) collective-permute-start(f32[2,2,128,256]{3,2,1,0:T(8,128)} %get-tuple-element.85), channel_id=1, source_target_pairs={{4,8},{8,4},{12,16},{16,12},{20,24},{24,20},{5,9},{9,5},{13,17},{1... | collective-permute-start | bytes 1572872 | tf_op jit(solution)/shard_map/ppermute | solution.py:612
  18.7 21.9 %collective-permute-start.10 = (f32[2,2,128,512]{3,2,1,0:T(8,128)}, f32[2,2,128,512]{3,2,1,0:T(8,128)}, u32[]{:S(2)}, u32[]{:S(2)}) collective-permute-start(f32[2,2,128,512]{3,2,1,0:T(8,128)} %collective-permute-done.6), channel_id=1, source_target_pairs={{28,16},{0,12},{29,17},{1,13},{30,18},{2,14},{31,19},{3,15}} | collective-permute-start | bytes 3145736 | tf_op jit(solution)/shard_map/ppermute | solution.py:622
  20.4 4.0 %copy-start.1 = (s32[8,2]{0,1:T(2,128)S(1)}, s32[8,2]{0,1:T(2,128)}, u32[]{:S(2)}) copy-start(s32[8,2]{0,1:T(2,128)} %param.16) | copy-start | bytes 196
  25.1 1.0 copy-start
  29.8 8.9 %collective-permute-start = (f32[2,2,128,1280]{3,2,1,0:T(8,128)}, f32[2,2,128,1280]{3,2,1,0:T(8,128)}, u32[]{:S(2)}, u32[]{:S(2)}) collective-permute-start(f32[2,2,128,1280]{3,2,1,0:T(8,128)} %get-tuple-element.29), channel_id=1, source_target_pairs={{0,4},{4,0},{8,12},{12,8},{16,20},{20,16},{24,28},{28,24},{1,5},{5... | collective-permute-start | bytes 7864328 | tf_op jit(solution)/shard_map/cond/branch_1_fun/ppermute | solution.py:612
  38.7 27.7 %collective-permute-start.11 = (f32[2,2,128,512]{3,2,1,0:T(8,128)}, f32[2,2,128,512]{3,2,1,0:T(8,128)}, u32[]{:S(2)}, u32[]{:S(2)}) collective-permute-start(f32[2,2,128,512]{3,2,1,0:T(8,128)} %get-tuple-element.84), channel_id=1, source_target_pairs={{4,8},{8,4},{12,16},{16,12},{20,24},{24,20},{5,9},{9,5},{13,17},{1... | collective-permute-start | bytes 3145736 | tf_op jit(solution)/shard_map/ppermute | solution.py:612
  52.6 28.4 %collective-permute-start.13 = (f32[2,2,128,256]{3,2,1,0:T(8,128)}, f32[2,2,128,256]{3,2,1,0:T(8,128)}, u32[]{:S(2)}, u32[]{:S(2)}) collective-permute-start(f32[2,2,128,256]{3,2,1,0:T(8,128)} %get-tuple-element.94), channel_id=1, source_target_pairs={{4,8},{8,4},{12,16},{16,12},{20,24},{24,20},{5,9},{9,5},{13,17},{1... | collective-permute-start | bytes 1572872 | tf_op jit(solution)/shard_map/ppermute | solution.py:612
  81.0 41.7 %collective-permute-start.16 = (f32[2,2,128,512]{3,2,1,0:T(8,128)}, f32[2,2,128,512]{3,2,1,0:T(8,128)}, u32[]{:S(2)}, u32[]{:S(2)}) collective-permute-start(f32[2,2,128,512]{3,2,1,0:T(8,128)} %get-tuple-element.99), channel_id=1, source_target_pairs={{4,8},{8,4},{20,24},{24,20},{5,9},{9,5},{21,25},{25,21},{6,10},{10... | collective-permute-start | bytes 3145736 | tf_op jit(solution)/shard_map/ppermute | solution.py:612
  82.9 39.8 %collective-permute-start.14 = (f32[2,2,512,128]{3,2,1,0:T(8,128)}, f32[2,2,512,128]{3,2,1,0:T(8,128)}, u32[]{:S(2)}, u32[]{:S(2)}) collective-permute-start(f32[2,2,512,128]{3,2,1,0:T(8,128)} %get-tuple-element.95), channel_id=1, source_target_pairs={{0,1},{1,2},{2,3},{4,5},{5,6},{6,7},{8,9},{9,10},{10,11},{12,13},{... | collective-permute-start | bytes 3145736 | tf_op jit(solution)/shard_map/ppermute | solution.py:604
  85.6 37.1 %collective-permute-start.15 = (f32[2,2,512,128]{3,2,1,0:T(8,128)}, f32[2,2,512,128]{3,2,1,0:T(8,128)}, u32[]{:S(2)}, u32[]{:S(2)}) collective-permute-start(f32[2,2,512,128]{3,2,1,0:T(8,128)} %get-tuple-element.96), channel_id=1, source_target_pairs={{1,0},{2,1},{3,2},{5,4},{6,5},{7,6},{9,8},{10,9},{11,10},{13,12},{... | collective-permute-start | bytes 3145736 | tf_op jit(solution)/shard_map/ppermute | solution.py:604
  87.0 1.6 %collective-permute-start.1 = (f32[256,256]{1,0:T(8,128)S(1)}, f32[256,256]{1,0:T(8,128)S(1)}, u32[]{:S(2)}, u32[]{:S(2)}) collective-permute-start(f32[256,256]{1,0:T(8,128)S(1)} %constant_dynamic-slice_fusion.1), channel_id=1, source_target_pairs={{0,4},{4,0},{8,12},{12,8},{16,20},{20,16},{24,28},{28,24},{1,5},{5... | collective-permute-start | bytes 786440 | tf_op jit(solution)/shard_map/cond/branch_1_fun/ppermute | solution.py:635
  88.7 13.9 %collective-permute-start.2 = (f32[128,256]{1,0:T(8,128)S(1)}, f32[128,256]{1,0:T(8,128)S(1)}, u32[]{:S(2)}, u32[]{:S(2)}) collective-permute-start(f32[128,256]{1,0:T(8,128)S(1)} %constant_dynamic-slice_fusion), channel_id=1, source_target_pairs={{0,16},{4,20},{8,24},{12,28},{16,0},{20,4},{24,8},{28,12},{1,17},{... | collective-permute-start | bytes 393224 | tf_op jit(solution)/shard_map/cond/branch_1_fun/ppermute | solution.py:635
  102.5 20.2 %collective-permute-start.5 = (f32[2,2,128,512]{3,2,1,0:T(8,128)}, f32[2,2,128,512]{3,2,1,0:T(8,128)}, u32[]{:S(2)}, u32[]{:S(2)}) collective-permute-start(f32[2,2,128,512]{3,2,1,0:T(8,128)} %get-tuple-element.40), channel_id=1, source_target_pairs={{12,16},{16,12},{13,17},{17,13},{14,18},{18,14},{15,19},{19,15}} | collective-permute-start | bytes 3145736 | tf_op jit(solution)/shard_map/cond/branch_1_fun/ppermute | solution.py:712
  104.2 6.6 %collective-permute-start.3 = (f32[128,256]{1,0:T(8,128)S(1)}, f32[128,256]{1,0:T(8,128)S(1)}, u32[]{:S(2)}, u32[]{:S(2)}) collective-permute-start(f32[128,256]{1,0:T(8,128)S(1)} %dynamic-slice_add_fusion.1), channel_id=1, source_target_pairs={{0,1},{1,0},{2,3},{3,2},{4,5},{5,4},{6,7},{7,6},{8,9},{9,8},{10,11... | collective-permute-start | bytes 393224 | tf_op jit(solution)/shard_map/cond/branch_1_fun/ppermute | solution.py:714
  110.9 11.8 %collective-permute-start.4 = (f32[128,256]{1,0:T(8,128)S(1)}, f32[128,256]{1,0:T(8,128)S(1)}, u32[]{:S(2)}, u32[]{:S(2)}) collective-permute-start(f32[128,256]{1,0:T(8,128)S(1)} %add.38), channel_id=1, source_target_pairs={{0,2},{1,3},{2,0},{3,1},{4,6},{5,7},{6,4},{7,5},{8,10},{9,11},{10,... | collective-permute-start | bytes 393224 | tf_op jit(solution)/shard_map/cond/branch_1_fun/ppermute | solution.py:714
  126.4 14.2 %collective-permute-start.17 = (f32[2,2,128,1024]{3,2,1,0:T(8,128)}, f32[2,2,128,1024]{3,2,1,0:T(8,128)}, u32[]{:S(2)}, u32[]{:S(2)}) collective-permute-start(f32[2,2,128,1024]{3,2,1,0:T(8,128)} %get-tuple-element.105), channel_id=1, source_target_pairs={{0,4},{4,0},{8,12},{12,8},{16,20},{20,16},{24,28},{28,24},{1,5},{5... | collective-permute-start | bytes 6291464 | tf_op jit(solution)/shard_map/ppermute | solution.py:612
  126.9 5.0 %collective-permute-start.19 = (f32[128,256]{1,0:T(8,128)S(1)}, f32[128,256]{1,0:T(8,128)S(1)}, u32[]{:S(2)}, u32[]{:S(2)}) collective-permute-start(f32[128,256]{1,0:T(8,128)S(1)} %get-tuple-element.100), channel_id=1, source_target_pairs={{0,8},{4,12},{8,0},{12,4},{16,24},{20,28},{24,16},{28,20},{1,9},{5... | collective-permute-start | bytes 393224 | tf_op jit(solution)/shard_map/ppermute | solution.py:720
  128.3 19.7 %collective-permute-start.18 = (f32[2,2,128,256]{3,2,1,0:T(8,128)}, f32[2,2,128,256]{3,2,1,0:T(8,128)}, u32[]{:S(2)}, u32[]{:S(2)}) collective-permute-start(f32[2,2,128,256]{3,2,1,0:T(8,128)} %get-tuple-element.106), channel_id=1, source_target_pairs={{4,8},{8,4},{12,16},{16,12},{20,24},{24,20},{5,9},{9,5},{13,17},{1... | collective-permute-start | bytes 1572872 | tf_op jit(solution)/shard_map/ppermute | solution.py:612
  131.8 15.5 %collective-permute-start.20 = (f32[128,256]{1,0:T(8,128)S(1)}, f32[128,256]{1,0:T(8,128)S(1)}, u32[]{:S(2)}, u32[]{:S(2)}) collective-permute-start(f32[128,256]{1,0:T(8,128)S(1)} %add.45), channel_id=1, source_target_pairs={{0,16},{4,20},{8,24},{12,28},{16,0},{20,4},{24,8},{28,12},{1,17},{... | collective-permute-start | bytes 393224 | tf_op jit(solution)/shard_map/ppermute | solution.py:640
  147.4 3.6 %collective-permute-start.21 = (f32[256,256]{1,0:T(8,128)S(1)}, f32[256,256]{1,0:T(8,128)S(1)}, u32[]{:S(2)}, u32[]{:S(2)}) collective-permute-start(f32[256,256]{1,0:T(8,128)S(1)} %pad_maximum_fusion.1), channel_id=1, source_target_pairs={{0,4},{4,0},{8,12},{12,8},{16,20},{20,16},{24,28},{28,24},{1,5},{5... | collective-permute-start | bytes 786440 | tf_op jit(solution)/shard_map/ppermute | solution.py:728
